TPU v7x, 256 devices: a whole 4x4x8 slice. The times are simulated.
256 devices in a mesh: tab: 64 (over y, z_hi, x, core), row: 4 (over z_lo).
Axes of the slice: x: 4, y: 4, z: 8 (z_hi: 2, z_lo: 4; z = z_hi * 4 + z_lo), core: 2. Of those that a mesh axis runs over, the one named last changes fastest.
Arguments:
- inputs: bfloat16 [32768, 1152], P(('tab', 'row')), may hold values from -6 to 6
- cotangent: bfloat16 [32768, 1152], P(('tab', 'row')), may hold values from -3 to 3
- cross_down: bfloat16 [1152, 512], replicated, may hold values from -0.1875 to 0.1875
- cross_up: bfloat16 [512, 1152], replicated, may hold values from -0.25 to 0.25
- cross_bias: float32 [1152], replicated, may hold values from -4 to 4
- indices: int32 [32768, 8, 8], P(('tab', 'row')), may hold values from 0 to 32767, as said below
- emb_table: float32 [262144, 128], P(('tab', 'row')), may hold values from -6 to 6
- row_accum: float32 [262144], P(('tab', 'row')), may hold values from 0.01 to 1
Outputs:
- table_new: float32 [262144, 128], P(('tab', 'row'))
- accum_new: float32 [262144], P(('tab', 'row'))
- dense_grad: bfloat16 [32768, 128], P(('tab', 'row'))
- weight_grads: float32 [1024, 1152], P(('tab', 'row'))
Inputs may be any that keep to these rules, and one draw needn't show every extreme that they name: `indices`: row numbers within each table. In every aligned block of 128 samples, the 1024 lookups of each table fall exactly 32 times into each range of 1024 consecutive row numbers starting at a multiple of 1024.
All inputs are finite; a program needn't handle non-finite values.
Results may differ from a plain program's by a relative error of at most 0.0049.
Values may be sent and summed in bfloat16 or wider, within the bound.
No kernel may reach another device: no remote copies, remote signals or barrier semaphores. Data moves between devices by JAX's collectives and lax.ppermute only.
A program may use at most 64 MiB of HBM per device.

v0:
```python
import jax
import jax.numpy as jnp
from jax import lax
from jax.sharding import PartitionSpec as P

EMB = 128
TABLES = 8
HOT = 8


RATE = 0.1
EPSILON = 1e-08


def contract_rows(left_side, right_side):
    return lax.dot_general(
        left_side, right_side, (((0,), (0,)), ((), ())), preferred_element_type=jnp.float32
    )


def contract_cols(left_side, right_side):
    return lax.dot_general(
        left_side, right_side, (((1,), (1,)), ((), ())), preferred_element_type=jnp.float32
    )


def per_device(inputs, cotangent, cross_down, cross_up, cross_bias, indices, emb_table, row_accum):
    batch_rows = inputs.shape[0]
    hidden = jnp.dot(inputs, cross_down, preferred_element_type=jnp.float32).astype(jnp.bfloat16)
    cross_scale = jnp.dot(hidden, cross_up, preferred_element_type=jnp.float32) + cross_bias
    upward = cotangent.astype(jnp.float32)
    grad_scale = (upward * inputs.astype(jnp.float32)).astype(jnp.bfloat16)
    grad_hidden = contract_cols(grad_scale, cross_up).astype(jnp.bfloat16)
    grad_input = upward * (cross_scale + 1.0) + contract_cols(grad_hidden, cross_down)
    dense_part = grad_input[:, :EMB].astype(jnp.bfloat16)
    pooled = grad_input[:, EMB:].astype(jnp.bfloat16).reshape(batch_rows * TABLES, EMB)
    tab_size = lax.axis_size("tab")
    row_size = lax.axis_size("row")
    weight_terms = jnp.concatenate(
        [contract_rows(grad_hidden, inputs), contract_rows(hidden, grad_scale)], axis=0
    )
    weight_total = lax.psum_scatter(weight_terms, ("tab", "row"), scatter_dimension=0, tiled=True)
    owner_rows = emb_table.shape[0]
    ranges = tab_size * row_size // TABLES
    lookups = batch_rows * HOT
    per_owner = lookups // ranges
    owners = jnp.transpose(indices // owner_rows, (1, 0, 2)).reshape(TABLES, lookups)
    within = jnp.transpose(indices % owner_rows, (1, 0, 2)).reshape(TABLES, lookups)
    ranking = jnp.argsort(owners, axis=1, stable=True)
    source = ranking // HOT * TABLES + jnp.arange(TABLES, dtype=jnp.int32)[:, None]
    row_grads = jnp.take(pooled, source.reshape(-1), axis=0).reshape(
        tab_size, row_size, per_owner, EMB
    )
    local_rows = jnp.take_along_axis(within, ranking, axis=1).reshape(tab_size, row_size, per_owner)
    row_grads, local_rows = (
        lax.all_to_all(row_grads, "tab", split_axis=0, concat_axis=0, tiled=True),
        lax.all_to_all(local_rows, "tab", split_axis=0, concat_axis=0, tiled=True),
    )
    row_grads, local_rows = (
        lax.all_to_all(row_grads, "row", split_axis=1, concat_axis=1, tiled=True),
        lax.all_to_all(local_rows, "row", split_axis=1, concat_axis=1, tiled=True),
    )
    summed = jax.ops.segment_sum(
        row_grads.reshape(-1, EMB).astype(jnp.float32),
        local_rows.reshape(-1),
        num_segments=owner_rows,
    )
    accum_new = row_accum + jnp.mean(summed * summed, axis=1)
    table_new = emb_table - RATE * summed / (jnp.sqrt(accum_new) + EPSILON)[:, None]
    return (table_new, accum_new, dense_part, weight_total)


def solution(mesh):
    in_specs = (
        P(("tab", "row"), None),
        P(("tab", "row"), None),
        P(),
        P(),
        P(),
        P(("tab", "row"), None, None),
        P(("tab", "row"), None),
        P(("tab", "row")),
    )
    out_specs = (
        P(("tab", "row"), None),
        P(("tab", "row")),
        P(("tab", "row"), None),
        P(("tab", "row"), None),
    )
    return jax.shard_map(
        per_device, mesh=mesh, in_specs=in_specs, out_specs=out_specs, check_vma=False
    )
```

profile of v0, /device:TPU:1, one launch (start us, length us, event | category | flops | bytes accessed | tf_op | source)
XLA Modules:
  0.0 540.5 jit_solution(9527633416389562580)
XLA Ops:
  8.1 0.9 fusion.10
  9.0 0.2 copy.27
  9.2 0.9 reshape.82
  10.1 0.6 iota.11
  10.7 1.7 convolution_convert_fusion.1
  12.5 0.5 convolution_convert_fusion
  13.0 0.3 fusion.3
  13.4 0.4 copy-done.3
  13.8 0.5 fusion.4
  14.4 0.2 copy.28
  14.6 0.3 reshape.83
  14.9 0.1 reshape.86
  15.0 0.1 sort.19.cloned.1.call-done
  15.1 0.8 fusion.15
  15.9 50.4 %gather_fusion.1 = s32[8192]{0:T(1024)S(1)} fusion(s32[8,1024]{1,0:T(8,128)S(1)} %reshape.83, s32[8192]{0:T(1024)S(1)} %bitcast.34), kind=kCustom, calls=%fused_computation.1 | custom fusion | bytes 131072 | tf_op jit(solution)/shard_map/jit(take_along_axis)/gather | solution.py:54
  66.4 0.1 reshape.85
  66.6 0.6 broadcast_clamp_fusion
  67.2 0.7 compare_and_fusion
  67.9 0.1 select_n.55
  68.0 0.8 reshape.119
  68.8 15.8 %all-to-all-start = ((s32[64,1,128]{2,1,0:T(1,128)}), s32[64,1,128]{2,1,0:T(1,128)}, u32[]{:S(2)}, u32[]{:S(2)}) async-start(s32[64,1,128]{2,1,0:T(1,128)} %reshape.119), calls=%async_computation | async-start | bytes 65536 | tf_op jit(solution)/shard_map/all_to_all | solution.py:57
  84.6 27.9 %gather_fusion = bf16[8192,128]{1,0:T(8,128)(2,1)S(1)} fusion(bf16[1024,128]{1,0:T(8,128)(2,1)S(1)} %reshape.86, s32[8192]{0:T(1024)} %broadcast_clamp_fusion), kind=kCustom, calls=%fused_computation | custom fusion | bytes 4227072 | tf_op jit(solution)/shard_map/jit(_take)/gather | solution.py:51
  112.5 3.7 broadcast_select_fusion
  116.2 12.8 %all-to-all-start.2 = ((bf16[64,4,32,128]{3,2,1,0:T(8,128)(2,1)}), bf16[64,4,32,128]{3,2,1,0:T(8,128)(2,1)S(1)}, u32[]{:S(2)}, u32[]{:S(2)}) async-start(bf16[64,4,32,128]{3,2,1,0:T(8,128)(2,1)} %broadcast_select_fusion), calls=%async_computation.2 | async-start | bytes 4194304 | tf_op jit(solution)/shard_map/all_to_all | solution.py:56
  129.0 0.5 broadcast.85
  129.5 1.5 reduce
  130.9 0.1 reshape.120
  131.2 0.7 reshape.121
  131.9 36.6 %all-to-all-done.2 = bf16[64,4,32,128]{3,2,1,0:T(8,128)(2,1)S(1)} async-done(((bf16[64,4,32,128]{3,2,1,0:T(8,128)(2,1)}), bf16[64,4,32,128]{3,2,1,0:T(8,128)(2,1)S(1)}, u32[]{:S(2)}, u32[]{:S(2)}) %all-to-all-start.2) | async-done | bytes 2097184 | tf_op jit(solution)/shard_map/all_to_all | solution.py:56
  168.5 1.3 copy-done.1
  169.9 18.2 %all-to-all-start.1 = ((s32[4,1,2048]{2,1,0:T(1,128)}), s32[4,1,2048]{2,1,0:T(1,128)}, u32[]{:S(2)}, u32[]{:S(2)}) async-start(s32[4,1,2048]{2,1,0:T(1,128)} %reshape.121), calls=%async_computation.1 | async-start | bytes 65536 | tf_op jit(solution)/shard_map/all_to_all | solution.py:61
  188.0 1.7 fusion.7
  189.9 1.8 copy.31
  191.7 0.9 all-to-all-done.1
  192.6 4.5 all-to-all-start.3
  197.2 1.5 fusion.19
  198.7 2.5 pad_maximum_fusion
  201.2 1.4 slice.15
  202.6 1.5 reduce.1
  204.2 0.1 copy.30
  204.3 0.1 reshape.105
  204.4 275.9 %all-reduce.3.cloned.1.call-done = f32[1024,1152]{1,0:T(8,128)} async-done(((f32[1024,1152]{1,0:T(8,128)}), f32[1024,1152]{1,0:T(8,128)}) %all-reduce.3.cloned.1.call-update) | async-done | bytes 4718608
  480.3 1.4 constant_dynamic-slice_fusion
  481.7 2.2 copy.32
  484.0 45.0 %scatter_custom_fusion = f32[1024,128]{1,0:T(8,128)} fusion(s32[8192]{0:T(1024)S(1)} %reshape.105, bf16[8192,128]{1,0:T(8,128)(2,1)S(1)} %bitcast.36, f32[]{:T(128)} %constant.65.clone.1), kind=kCustom, calls=%fused_computation.4 | custom fusion | flops 2097152 | bytes 2621444 | tf_op jit(solution)/shard_map/scatter-add | solution.py:63
  528.9 1.2 multiply_reduce_fusion
  530.2 0.6 sqrt_add_fusion
  530.8 2.2 divide_subtract_fusion
  (36 shorter events, 0.6 us)
Async XLA Ops:
  8.0 4.4 copy-start
  8.0 4.4 copy-start.4
  8.0 4.4 copy-start.5
  8.0 7.1 %sort.19.cloned.1.call-start = ((), (), s32[]{:S(2)}) async-start(), calls=%async_computation.5 | async-start | bytes 196640 | tf_op jit(solution)/shard_map/jit(argsort)/sort | solution.py:49
  9.0 4.0 copy-start.10
  12.5 1.9 copy-start.7
  12.5 1.3 copy-start.3
  13.0 1.3 copy-start.8
  14.3 52.0 %copy-start.6 = (bf16[128,1152]{1,0:T(8,128)(2,1)}, bf16[128,1152]{1,0:T(8,128)(2,1)S(1)}, u32[]{:S(2)}) copy-start(bf16[128,1152]{1,0:T(8,128)(2,1)S(1)} %fusion.4) | copy-start | bytes 884740
  15.9 50.5 %copy-start.9 = (s32[8,1024]{1,0:T(8,128)S(1)}, s32[8,1024]{1,0:T(8,128)}, u32[]{:S(2)}) copy-start(s32[8,1024]{1,0:T(8,128)} %get-tuple-element.5) | copy-start | bytes 98308
  68.8 47.4 %all-to-all-start = ((s32[64,1,128]{2,1,0:T(1,128)}), s32[64,1,128]{2,1,0:T(1,128)}, u32[]{:S(2)}, u32[]{:S(2)}) async-start(s32[64,1,128]{2,1,0:T(1,128)} %reshape.119), calls=%async_computation | async-start | bytes 65536 | tf_op jit(solution)/shard_map/all_to_all | solution.py:57
  116.2 52.3 %all-to-all-start.2 = ((bf16[64,4,32,128]{3,2,1,0:T(8,128)(2,1)}), bf16[64,4,32,128]{3,2,1,0:T(8,128)(2,1)S(1)}, u32[]{:S(2)}, u32[]{:S(2)}) async-start(bf16[64,4,32,128]{3,2,1,0:T(8,128)(2,1)} %broadcast_select_fusion), calls=%async_computation.2 | async-start | bytes 4194304 | tf_op jit(solution)/shard_map/all_to_all | solution.py:56
  168.5 1.3 copy-start.1
  169.9 22.8 %all-to-all-start.1 = ((s32[4,1,2048]{2,1,0:T(1,128)}), s32[4,1,2048]{2,1,0:T(1,128)}, u32[]{:S(2)}, u32[]{:S(2)}) async-start(s32[4,1,2048]{2,1,0:T(1,128)} %reshape.121), calls=%async_computation.1 | async-start | bytes 65536 | tf_op jit(solution)/shard_map/all_to_all | solution.py:61
  188.0 1.8 copy-start.2
  192.6 289.1 %all-to-all-start.3 = ((bf16[64,4,32,128]{3,2,0,1:T(8,128)(2,1)}), bf16[64,4,32,128]{3,2,0,1:T(8,128)(2,1)}, u32[]{:S(2)}, u32[]{:S(2)}) async-start(bf16[64,4,32,128]{3,2,0,1:T(8,128)(2,1)} %copy.31), calls=%async_computation.3 | async-start | bytes 4194304 | tf_op jit(solution)/shard_map/all_to_all | solution.py:60
  197.1 283.2 %all-reduce.3.cloned.1.call-start = ((), (), s32[]{:S(2)}) async-start(), calls=%async_computation.4 | async-start | bytes 9437184
  484.0 46.2 %copy-start.11 = (f32[1024]{0:T(1024)S(1)}, f32[1024]{0:T(1024)}, u32[]{:S(2)}) copy-start(f32[1024]{0:T(1024)} %param.15) | copy-start | bytes 12292
Sparse Core Ops, SparseCore 0:
  11.9 2.8 sort.21.cloned.1.call-done
  (1 shorter events, 0.0 us)
Sparse Core Ops, SparseCore 1:
  203.9 276.4 all-reduce.2
where the time goes:
time: 543 us; the launch traced here: 540 us
  waiting for transfers between devices  314 us (58%)
  local copies, waits for them, and re-layouts  92.3 us (17%)
  other arithmetic  61.2 us (11%)
  starting transfers between devices  51.2 us (9%)
  between operations  15.8 us (3%)
  matrix products  6.36 us (1%)
    unnamed x2, waiting for transfers between devices  276 us
    gather x2, local copies, waits for them, and re-layouts, per_device(): jnp.take_along_axis(within, ranking, axis=1)  50.4 us
    scatter-add x1, other arithmetic, per_device(): jax.ops.segment_sum(row_grads.reshape(-1, EMB).astype(jnp.float32), local...  45 us
    all_to_all x1, waiting for transfers between devices, per_device(): lax.all_to_all(row_grads, 'tab', split_axis=0, concat_axis=0, tiled=True)  36.6 us
    gather x1, local copies, waits for them, and re-layouts, per_device(): jnp.take(pooled, source.reshape(-1), axis=0)  27.9 us
    all_to_all x1, starting transfers between devices, per_device(): lax.all_to_all(local_rows, 'row', split_axis=1, concat_axis=1, tiled=True)  18.2 us
    all_to_all x1, starting transfers between devices, per_device(): lax.all_to_all(local_rows, 'tab', split_axis=0, concat_axis=0, tiled=True)  15.8 us
    all_to_all x1, starting transfers between devices, per_device(): lax.all_to_all(row_grads, 'tab', split_axis=0, concat_axis=0, tiled=True)  12.8 us
  transfers between devices with their start and end apart: 5, of which 3 were waited for; matrix products, arithmetic and copies ran while one was open for 9% of the time, Pallas kernels for 0%

commit v1 on v0

v1 whole, which is shorter than its diff:
```python
import jax
import jax.numpy as jnp
from jax import lax
from jax.experimental import pallas as pl
from jax.experimental.pallas import tpu as pltpu
from jax.sharding import Mesh, PartitionSpec as P

EMB = 128
TABLES = 8
HOT = 8
RATE = 0.1
EPSILON = 1e-08
BLOCK = 128
ROWS = 1024
SLOTS = 32
META = 16
AXES = ("y", "zh", "x", "c", "zl")
NY, NZH, NX, NC, NZL = 4, 2, 4, 2, 4


def dot(a, b, dims):
    return lax.dot_general(a, b, ((dims[0], dims[1]), ((), ())), preferred_element_type=jnp.float32)


def expand_kernel(core_ref, own_ref, other_ref, out_ref, look_ref, row_ref):
    core = core_ref[0]
    lane_group = lax.broadcasted_iota(jnp.int32, (8, 128), 1) // SLOTS
    sample_iota = lax.broadcasted_iota(jnp.int32, (BLOCK, 128), 0).astype(jnp.float32)

    def gather(ref, first):
        def step(j, _):
            looks, rows = [], []
            for m in range(NX):
                b = j * NX + m
                meta = ref[b, BLOCK:BLOCK + META, :].astype(jnp.float32)
                mine = jnp.where(core == 0, meta[0:8], meta[8:16])
                pick = (sample_iota == mine[0:1]).astype(jnp.bfloat16)
                looks.append(dot(pick, ref[b, 0:BLOCK, :], ((0,), (0,))).astype(jnp.bfloat16))
                rows.append(jnp.broadcast_to(mine[1:2] * 32.0 + mine[2:3], (8, 128)))
            for d in range(NX):
                row = rows[d]
                for g in range(NX):
                    m = (d - g) % NX
                    look_ref[d, first + j, g * SLOTS:(g + 1) * SLOTS, :] = looks[m][g * SLOTS:(g + 1) * SLOTS]
                    if g:
                        row = jnp.where(lane_group == g, rows[m], row)
                row_ref[d, first + j] = row
            return 0

        lax.fori_loop(0, 8, step, 0)

    gather(own_ref, 0)
    gather(other_ref, 8)

    base = lax.broadcasted_iota(jnp.int32, (256, 128), 0).astype(jnp.float32)
    for d in range(NX):
        def rows_step(i, _, d=d):
            here = base + (i * 256).astype(jnp.float32)
            hot = jnp.concatenate(
                [(here == row_ref[d, j, 0:1, :]).astype(jnp.bfloat16) for j in range(16)], axis=1
            )
            total = dot(hot, look_ref[d].reshape(16 * 128, EMB), ((1,), (0,)))
            out_ref[d, pl.ds(pl.multiple_of(i * 256, 256), 256), :] = total.astype(jnp.bfloat16)
            return 0

        lax.fori_loop(0, ROWS // 256, rows_step, 0)


def update_kernel(a_ref, b_ref, c_ref, d_ref, table_ref, accum_ref, table_out, accum_out):
    eye = lax.broadcasted_iota(jnp.int32, (128, 128), 0) == lax.broadcasted_iota(jnp.int32, (128, 128), 1)
    for i in range(ROWS // 128):
        s = slice(i * 128, (i + 1) * 128)
        grad = a_ref[s].astype(jnp.float32) + b_ref[s].astype(jnp.float32)
        grad = grad + (c_ref[s].astype(jnp.float32) + d_ref[s].astype(jnp.float32))
        mean = jnp.sum(grad * grad, axis=1, keepdims=True) * (1.0 / EMB)
        old = jnp.sum(jnp.where(eye, accum_ref[i:i + 1, :], 0.0), axis=1, keepdims=True)
        new = old + mean
        table_out[s] = table_ref[s] - grad * (RATE / (jnp.sqrt(new) + EPSILON))
        accum_out[i:i + 1, :] = jnp.sum(jnp.where(eye, new, 0.0), axis=0, keepdims=True)


def ring(size, shift):
    return [(i, (i + shift) % size) for i in range(size)]


def per_device(inputs, cotangent, cross_down, cross_up, cross_bias, indices, emb_table, row_accum):
    x = lax.axis_index("x")
    c = lax.axis_index("c")
    zl = lax.axis_index("zl")
    swap = ring(NC, 1)

    idx = jnp.transpose(indices, (1, 0, 2)).reshape(TABLES, BLOCK * HOT)
    sample = lax.broadcasted_iota(jnp.int32, idx.shape, 1) // HOT
    owner = idx >> 10
    place = (owner & 3) * 8 + ((owner >> 2) & 1) * 4 + (((owner >> 3) - x - zl) & 3)
    keys = lax.sort((place << 17) | ((idx & 1023) << 7) | sample, dimension=1, is_stable=False)

    hidden = dot(inputs, cross_down, ((1,), (0,))).astype(jnp.bfloat16)
    upward = cotangent.astype(jnp.float32)
    grad_scale = (upward * inputs.astype(jnp.float32)).astype(jnp.bfloat16)
    grad_hidden = dot(grad_scale, cross_up, ((1,), (1,))).astype(jnp.bfloat16)
    cross_scale = dot(hidden, cross_up, ((1,), (0,))) + cross_bias
    grad_input = upward * (cross_scale + 1.0) + dot(grad_hidden, cross_down, ((1,), (1,)))
    dense_part = grad_input[:, :EMB].astype(jnp.bfloat16)
    pooled = grad_input[:, EMB:].astype(jnp.bfloat16).reshape(BLOCK, TABLES, EMB)

    keys = keys.reshape(TABLES, NZL, NC, 1, 128)
    fields = jnp.concatenate(
        [keys & 127, (keys >> 12) & 31, (keys >> 7) & 31, jnp.zeros((TABLES, NZL, NC, 5, 128), jnp.int32)], axis=3
    ).astype(jnp.bfloat16).reshape(TABLES, NZL, META, 128)
    blocks = jnp.broadcast_to(jnp.transpose(pooled, (1, 0, 2))[:, None], (TABLES, NZL, BLOCK, EMB))
    sent = jnp.concatenate([blocks, fields], axis=2).reshape(TABLES * NZL, BLOCK + META, EMB)
    own = lax.all_to_all(sent, ("y", "zh", "zl"), split_axis=0, concat_axis=0, tiled=True)
    other = lax.ppermute(own, "c", swap)

    partial = pl.pallas_call(
        expand_kernel,
        out_shape=jax.ShapeDtypeStruct((NX, ROWS, EMB), jnp.bfloat16),
        in_specs=[
            pl.BlockSpec(memory_space=pltpu.SMEM),
            pl.BlockSpec(memory_space=pltpu.VMEM),
            pl.BlockSpec(memory_space=pltpu.VMEM),
        ],
        out_specs=pl.BlockSpec(memory_space=pltpu.VMEM),
        scratch_shapes=[
            pltpu.VMEM((NX, 16, 128, EMB), jnp.bfloat16),
            pltpu.VMEM((NX, 16, 8, 128), jnp.float32),
        ],
        compiler_params=pltpu.CompilerParams(vmem_limit_bytes=32 * 1024 * 1024),
        cost_estimate=pl.CostEstimate(flops=2_500_000_000, bytes_accessed=3_500_000, transcendentals=0),
    )(c.astype(jnp.int32).reshape(1), own, other)
    arrived = [lax.ppermute(partial[d], "x", ring(NX, d)) for d in range(1, NX)]

    spread = lax.broadcasted_iota(jnp.int32, (512, 256), 0)
    column = lax.broadcasted_iota(jnp.int32, (512, 256), 1)

    def rows_of(core):
        choose = (spread == (column // 16) * 32 + core * 16 + column % 16).astype(jnp.bfloat16)
        return [dot(v, choose, ((1,), (0,))).astype(jnp.bfloat16) for v in (grad_hidden, hidden)]

    kept = rows_of(c)
    other_in = lax.ppermute(inputs, "c", swap)
    other_scale = lax.ppermute(grad_scale, "c", swap)
    other_cols = lax.ppermute(jnp.concatenate(rows_of(1 - c), axis=1), "c", swap)
    top = dot(
        jnp.concatenate([kept[0], other_cols[:, :256]], axis=0), jnp.concatenate([inputs, other_in], axis=0), ((0,), (0,))
    )
    bottom = dot(
        jnp.concatenate([kept[1], other_cols[:, 256:]], axis=0), jnp.concatenate([grad_scale, other_scale], axis=0), ((0,), (0,))
    )
    terms = jnp.concatenate([top, bottom], axis=0).astype(jnp.bfloat16).reshape(NY, 128, 1152)
    terms = lax.all_to_all(terms, "y", split_axis=0, concat_axis=0, tiled=True)
    terms = jnp.sum(terms.astype(jnp.float32), axis=0).astype(jnp.bfloat16)
    terms = jnp.transpose(terms.reshape(NZH, NX, NZL, 4, 1152), (0, 2, 1, 3, 4)).reshape(32, 4, 1152)
    terms = lax.all_to_all(terms, ("zh", "zl", "x"), split_axis=0, concat_axis=0, tiled=True)
    weight_total = jnp.sum(terms.astype(jnp.float32), axis=0)

    table_new, accum_new = pl.pallas_call(
        update_kernel,
        out_shape=(
            jax.ShapeDtypeStruct((ROWS, EMB), jnp.float32),
            jax.ShapeDtypeStruct((8, 128), jnp.float32),
        ),
        in_specs=[pl.BlockSpec(memory_space=pltpu.VMEM)] * 6,
        out_specs=(pl.BlockSpec(memory_space=pltpu.VMEM),) * 2,
        compiler_params=pltpu.CompilerParams(vmem_limit_bytes=16 * 1024 * 1024),
        cost_estimate=pl.CostEstimate(flops=2_000_000, bytes_accessed=2_100_000, transcendentals=0),
    )(partial[0], *arrived, emb_table, row_accum.reshape(8, 128))
    return (table_new, accum_new.reshape(ROWS), dense_part, weight_total)


def solution(mesh):
    fine = Mesh(mesh.devices.reshape(NY, NZH, NX, NC, NZL), AXES)
    in_specs = (
        P(AXES, None), P(AXES, None), P(), P(), P(), P(AXES, None, None), P(AXES, None), P(AXES),
    )
    out_specs = (P(AXES, None), P(AXES), P(AXES, None), P(AXES, None))
    return jax.shard_map(per_device, mesh=fine, in_specs=in_specs, out_specs=out_specs, check_vma=False)
```

time: 543 us -> 133 us (0.24)
  waiting for transfers between devices: 314 us -> 32.5 us
  local copies, waits for them, and re-layouts: 92.3 us -> 8.92 us
  other arithmetic: 61.2 us -> 8.69 us
  starting transfers between devices: 51.2 us -> 28.5 us
  blocking collectives: 0 us -> 19.5 us
  Pallas kernels: 0 us -> 11.6 us
    unnamed x2 -> x0, waiting for transfers between devices: 276 us -> none
    gather x3 -> x0, local copies, waits for them, and re-layouts: 78.4 us -> none  [the longest x2 50.4 us: per_device(): jnp.take_along_axis(within, ranking, axis=1)]
    scatter-add x1 -> x0, other arithmetic: 45 us -> none  [per_device(): jax.ops.segment_sum(row_grads.reshape(-1, EMB).astype(jnp.float32), local...]
    all_to_all x4 -> x2, starting transfers between devices: 51.2 us -> 18.5 us  [the longest x1 12 us: per_device(): lax.all_to_all(sent, ('y', 'zh', 'zl'), split_axis=0, concat_axis=0, tile...]
    all_to_all x0 -> x1, blocking collectives: none -> 19.5 us  [per_device(): terms = lax.all_to_all(terms, 'y', split_axis=0, concat_axis=0, tiled=True)]
    all_to_all x4 -> x2, waiting for transfers between devices: 37.6 us -> 21.4 us  [the longest x1 21.4 us: per_device(): lax.all_to_all(sent, ('y', 'zh', 'zl'), split_axis=0, concat_axis=0, tile...]
    pallas_call x0 -> x2, Pallas kernels: none -> 11.6 us  [the longest x1 10.3 us: per_device(): pl.pallas_call(expand_kernel, out_shape=jax.ShapeDtypeStruct((NX, ROWS, E...]
    ppermute x0 -> x7, waiting for transfers between devices: none -> 11.1 us  [the longest x3 11.1 us: per_device(): arrived = [lax.ppermute(partial[d], 'x', ring(NX, d)) for d in range(1, NX)]]
  transfers between devices with their start and end apart: 5 -> 9, of which waited for: 3 -> 3; matrix products, arithmetic and copies ran while one was open for 9% -> 11% of each run, Pallas kernels for 0% -> 8%
where the time goes in v1:
time: 133 us; the launch traced here: 132 us
  waiting for transfers between devices  32.5 us (24%)
  starting transfers between devices  28.5 us (21%)
  blocking collectives  19.5 us (15%)
  between operations  14.4 us (11%)
  Pallas kernels  11.6 us (9%)
  local copies, waits for them, and re-layouts  8.92 us (7%)
  other arithmetic  8.69 us (7%)
  matrix products  7.97 us (6%)
    all_to_all x1, waiting for transfers between devices, per_device(): lax.all_to_all(sent, ('y', 'zh', 'zl'), split_axis=0, concat_axis=0, tile...  21.4 us
    all_to_all x1, blocking collectives, per_device(): terms = lax.all_to_all(terms, 'y', split_axis=0, concat_axis=0, tiled=True)  19.5 us
    all_to_all x1, starting transfers between devices, per_device(): lax.all_to_all(sent, ('y', 'zh', 'zl'), split_axis=0, concat_axis=0, tile...  12 us
    ppermute x3, waiting for transfers between devices, per_device(): arrived = [lax.ppermute(partial[d], 'x', ring(NX, d)) for d in range(1, NX)]  11.1 us
    pallas_call x1, Pallas kernels, per_device(): pl.pallas_call(expand_kernel, out_shape=jax.ShapeDtypeStruct((NX, ROWS, E...  10.3 us
    dot_general x10, matrix products, dot(): lax.dot_general(a, b, ((dims[0], dims[1]), ((), ())), preferred_element_t...  7.97 us
    all_to_all x1, starting transfers between devices, per_device(): lax.all_to_all(terms, ('zh', 'zl', 'x'), split_axis=0, concat_axis=0, til...  6.43 us
    ppermute x1, starting transfers between devices, per_device(): other = lax.ppermute(own, 'c', swap)  4.77 us
  transfers between devices with their start and end apart: 9, of which 3 were waited for; matrix products, arithmetic and copies ran while one was open for 11% of the time, Pallas kernels for 8%

profile of v1, /device:TPU:1, one launch (start us, length us, event | category | flops | bytes accessed | tf_op | source)
XLA Modules:
  0.0 132.0 jit_solution(13798749961940676955)
XLA Ops:
  7.2 0.0 sort.9.cloned.1.call-start
  7.3 0.9 or_bitcast_fusion
  8.2 0.2 copy.19
  8.4 0.3 reshape.131
  8.7 0.6 select_or_fusion
  9.3 0.0 sort.9.cloned.1.call-update
  9.3 1.3 convolution_convert_fusion.3
  10.7 1.0 fusion.3
  11.7 0.5 convolution_convert_fusion.2
  12.3 0.4 fusion.1
  12.6 0.5 fusion.2
  13.2 0.7 copy-done.5
  14.0 0.1 pad.17.clone
  14.1 1.6 %sort.9.cloned.1.call-done = s32[8,1024]{1,0:T(8,128)} async-done(((s32[8,1024]{1,0:T(8,128)}), s32[8,1024]{1,0:T(8,128)}) %sort.9.cloned.1.call-update) | async-done | bytes 32784 | tf_op jit(solution)/shard_map/sort | solution.py:96
  15.6 0.8 and_convert_fusion.2
  16.5 0.1 maximum_maximum_fusion
  16.6 0.2 broadcast_in_dim.4
  16.9 1.1 pad_maximum_fusion
  18.0 12.0 %all-to-all-start = ((bf16[32,144,128]{2,1,0:T(8,128)(2,1)}), bf16[32,144,128]{2,1,0:T(8,128)(2,1)S(1)}, u32[]{:S(2)}, u32[]{:S(2)}) async-start(bf16[32,144,128]{2,1,0:T(8,128)(2,1)} %pad_maximum_fusion), calls=%async_computation | async-start | bytes 2359296 | tf_op jit(solution)/shard_map/all_to_all | solution.py:113
  30.1 1.0 collective-permute-start.6
  31.1 0.1 collective-permute-start.5
  31.2 0.2 convolution_convert_fusion.5
  31.5 0.2 convolution_convert_fusion.6
  31.8 0.5 collective-permute-start.4
  32.3 0.2 convolution_convert_fusion.4
  32.5 0.9 convolution_convert_fusion.7
  33.4 0.6 fusion.30
  34.0 2.2 %convolution_convert_fusion = bf16[256,1152]{1,0:T(8,128)(2,1)} fusion(bf16[128,1152]{1,0:T(8,128)(2,1)} %collective-permute-done.6, bf16[128,1152]{1,0:T(8,128)(2,1)S(1)} %fusion.3, bf16[128,256]{1,0:T(8,128)(2,1)S(1)} %get-tuple-element.13, bf16[128,256]{1,0:T(8,128)(2,1)S(1)} %convolution_convert_fusion.4), kind=kOutput, calls=%fused_computation | convolution fusion | flops 152731648 | bytes 1310720 | tf_op jit(solution)/shard_map/dot_general | solution.py:22
  36.2 21.4 %all-to-all-done.own_ref = bf16[32,144,128]{2,1,0:T(8,128)(2,1)S(1)} async-done(((bf16[32,144,128]{2,1,0:T(8,128)(2,1)}), bf16[32,144,128]{2,1,0:T(8,128)(2,1)S(1)}, u32[]{:S(2)}, u32[]{:S(2)}) %all-to-all-start) | async-done | bytes 1179680 | tf_op jit(solution)/shard_map/all_to_all | solution.py:113
  57.6 4.8 %collective-permute-start = (bf16[32,144,128]{2,1,0:T(8,128)(2,1)S(1)}, bf16[32,144,128]{2,1,0:T(8,128)(2,1)S(1)}, u32[]{:S(2)}, u32[]{:S(2)}) collective-permute-start(bf16[32,144,128]{2,1,0:T(8,128)(2,1)S(1)} %all-to-all-done.own_ref), channel_id=1, source_target_pairs={{0,4},{4,0},{1,5},{5,1},{2,6},{6,2},{3,7},{7,3},{8,12},{12,8},{9,1... | collective-permute-start | bytes 3538952 | tf_op jit(solution)/shard_map/ppermute | solution.py:114
  62.4 1.5 %convolution_convert_fusion.1 = bf16[256,1152]{1,0:T(8,128)(2,1)S(1)} fusion(bf16[128,1152]{1,0:T(8,128)(2,1)} %collective-permute-done.5, bf16[128,1152]{1,0:T(8,128)(2,1)} %param.8, bf16[128,256]{1,0:T(8,128)(2,1)} %get-tuple-element.12, bf16[128,256]{1,0:T(8,128)(2,1)} %convolution_convert_fusion.7), kind=kOutput, calls=%fused_computation.1 | convolution fusion | flops 152731648 | bytes 1310720 | tf_op jit(solution)/shard_map/dot_general | solution.py:22
  63.9 0.1 pad_maximum_fusion.1
  64.0 19.5 %all_to_all.15 = bf16[4,128,1152]{2,1,0:T(8,128)(2,1)} all-to-all(bf16[4,128,1152]{2,1,0:T(8,128)(2,1)S(1)} %bitcast.39), channel_id=1, replica_groups=mesh['y'=4,'zh'=2,'x'=4,'c'=2,'zl'=4] {'y'}, dimensions={0} | all-to-all | bytes 2359296 | tf_op jit(solution)/shard_map/all_to_all | solution.py:152
  83.4 2.2 %reduce_sum.21 = bf16[128,1152]{1,0:T(8,128)(2,1)} reduce(bf16[4,128,1152]{2,1,0:T(8,128)(2,1)} %all_to_all.15, bf16[]{:T(256)} %constant.94.clone.1), dimensions={0}, to_apply=%region_1.2 | reduce | flops 442368 | bytes 1474562 | tf_op jit(solution)/shard_map/reduce_sum | solution.py:153
  85.7 1.8 %reshape.123 = bf16[2,4,4,4,1152]{4,3,2,1,0:T(4,128)(2,1)} reshape(bf16[128,1152]{1,0:T(8,128)(2,1)} %reduce_sum.21) | data formatting | bytes 589824 | tf_op jit(solution)/shard_map/reshape | solution.py:154
  87.4 1.8 %copy.23 = bf16[2,4,4,4,1152]{4,3,2,1,0:T(4,128)(2,1)} copy(bf16[2,4,4,4,1152]{4,3,1,2,0:T(4,128)(2,1)} %bitcast.42) | data formatting | bytes 589824 | tf_op jit(solution)/shard_map/transpose | solution.py:154
  89.2 6.4 %all-to-all-start.2 = ((bf16[32,4,1152]{2,1,0:T(4,128)(2,1)}), bf16[32,4,1152]{2,1,0:T(4,128)(2,1)}, u32[]{:S(2)}, u32[]{:S(2)}) async-start(bf16[32,4,1152]{2,1,0:T(4,128)(2,1)} %bitcast.41), calls=%async_computation.2 | async-start | bytes 589824 | tf_op jit(solution)/shard_map/all_to_all | solution.py:155
  95.7 10.3 %shard_map.111 = bf16[4,1024,128]{2,1,0:T(8,128)(2,1)S(1)} custom-call(s32[1]{0:T(128)} %bitcast.core_ref, bf16[32,144,128]{2,1,0:T(8,128)(2,1)S(1)} %all-to-all-done.own_ref, bf16[32,144,128]{2,1,0:T(8,128)(2,1)S(1)} %collective-permute-done.other_ref), custom_call_target="tpu_custom_call" | custom-call | flops 2500000000 | bytes 3500000 | tf_op jit(solution)/shard_map/pallas_call | solution.py:116
  106.0 0.1 slice_bitcast_fusion
  106.1 2.4 %collective-permute-start.3 = (bf16[1024,128]{1,0:T(8,128)(2,1)S(1)}, bf16[1024,128]{1,0:T(8,128)(2,1)S(1)}, u32[]{:S(2)}, u32[]{:S(2)}) collective-permute-start(bf16[1024,128]{1,0:T(8,128)(2,1)S(1)} %get-tuple-element.8), channel_id=1, source_target_pairs={{0,24},{8,0},{16,8},{24,16},{1,25},{9,1},{17,9},{25,17},{2,26},{10... | collective-permute-start | bytes 786440 | tf_op jit(solution)/shard_map/ppermute | solution.py:132
  108.5 0.6 collective-permute-start.2
  109.1 0.6 collective-permute-start.1
  109.7 1.4 %slice.39 = bf16[128,128]{1,0:T(8,128)(2,1)} slice(bf16[128,1152]{1,0:T(8,128)(2,1)} %copy-done.5), slice={[0:128], [0:128]} | slice | bytes 65536 | tf_op jit(solution)/shard_map/slice | solution.py:104
  111.1 1.7 %convert_reduce_fusion = f32[4,1152]{1,0:T(4,128)} fusion(bf16[32,4,1152]{2,1,0:T(4,128)(2,1)} %all-to-all-done.2), kind=kLoop, calls=%fused_computation.25 | loop fusion | flops 290304 | bytes 313344 | tf_op jit(solution)/shard_map/reduce_sum | solution.py:156
  112.8 0.0 collective-permute-done.3.d_ref
  112.8 3.1 %collective-permute-done.2.c_ref = bf16[1024,128]{1,0:T(8,128)(2,1)S(1)} collective-permute-done((bf16[1024,128]{1,0:T(8,128)(2,1)S(1)}, bf16[1024,128]{1,0:T(8,128)(2,1)S(1)}, u32[]{:S(2)}, u32[]{:S(2)}) %collective-permute-start.2) | collective-permute-done | bytes 262176 | tf_op jit(solution)/shard_map/ppermute | solution.py:132
  115.9 7.9 %collective-permute-done.1.b_ref = bf16[1024,128]{1,0:T(8,128)(2,1)S(1)} collective-permute-done((bf16[1024,128]{1,0:T(8,128)(2,1)S(1)}, bf16[1024,128]{1,0:T(8,128)(2,1)S(1)}, u32[]{:S(2)}, u32[]{:S(2)}) %collective-permute-start.1) | collective-permute-done | bytes 262176 | tf_op jit(solution)/shard_map/ppermute | solution.py:132
  123.9 1.3 shard_map.112
  (33 shorter events, 0.3 us)
Async XLA Ops:
  7.2 4.6 %copy-start = (bf16[512,1152]{1,0:T(8,128)(2,1)S(1)}, bf16[512,1152]{1,0:T(8,128)(2,1)}, u32[]{:S(2)}) copy-start(bf16[512,1152]{1,0:T(8,128)(2,1)} %param.11) | copy-start | bytes 3538948
  7.2 2.2 %copy-start.3 = (bf16[1152,512]{1,0:T(8,128)(2,1)S(1)}, bf16[1152,512]{1,0:T(8,128)(2,1)}, u32[]{:S(2)}) copy-start(bf16[1152,512]{1,0:T(8,128)(2,1)} %param.10) | copy-start | bytes 3538948
  7.2 8.4 %sort.9.cloned.1.call-start = ((), (), s32[]{:S(2)}) async-start(), calls=%async_computation.3 | async-start | bytes 98336 | tf_op jit(solution)/shard_map/sort | solution.py:96
  8.4 2.3 %copy-start.4 = (bf16[128,1152]{1,0:T(8,128)(2,1)S(1)}, bf16[128,1152]{1,0:T(8,128)(2,1)}, u32[]{:S(2)}) copy-start(bf16[128,1152]{1,0:T(8,128)(2,1)} %param.9) | copy-start | bytes 884740
  10.7 1.6 %copy-start.7 = (f32[1152]{0:T(1024)S(1)}, f32[1152]{0:T(1024)}, u32[]{:S(2)}) copy-start(f32[1152]{0:T(1024)} %param.12) | copy-start | bytes 13828
  13.1 0.7 copy-start.5
  18.0 39.6 %all-to-all-start = ((bf16[32,144,128]{2,1,0:T(8,128)(2,1)}), bf16[32,144,128]{2,1,0:T(8,128)(2,1)S(1)}, u32[]{:S(2)}, u32[]{:S(2)}) async-start(bf16[32,144,128]{2,1,0:T(8,128)(2,1)} %pad_maximum_fusion), calls=%async_computation | async-start | bytes 2359296 | tf_op jit(solution)/shard_map/all_to_all | solution.py:113
  30.1 4.0 %collective-permute-start.6 = (bf16[128,1152]{1,0:T(8,128)(2,1)S(1)}, bf16[128,1152]{1,0:T(8,128)(2,1)}, u32[]{:S(2)}, u32[]{:S(2)}) collective-permute-start(bf16[128,1152]{1,0:T(8,128)(2,1)S(1)} %fusion.3), channel_id=1, source_target_pairs={{0,4},{4,0},{1,5},{5,1},{2,6},{6,2},{3,7},{7,3},{8,12},{12,8},{9,1... | collective-permute-start | bytes 884744 | tf_op jit(solution)/shard_map/ppermute | solution.py:143
  31.1 31.3 %collective-permute-start.5 = (bf16[128,1152]{1,0:T(8,128)(2,1)}, bf16[128,1152]{1,0:T(8,128)(2,1)}, u32[]{:S(2)}, u32[]{:S(2)}) collective-permute-start(bf16[128,1152]{1,0:T(8,128)(2,1)} %param.8), channel_id=1, source_target_pairs={{0,4},{4,0},{1,5},{5,1},{2,6},{6,2},{3,7},{7,3},{8,12},{12,8},{9,1... | collective-permute-start | bytes 884744 | tf_op jit(solution)/shard_map/ppermute | solution.py:142
  31.8 1.6 %collective-permute-start.4 = (bf16[128,512]{1,0:T(8,128)(2,1)S(1)}, bf16[128,512]{1,0:T(8,128)(2,1)S(1)}, u32[]{:S(2)}, u32[]{:S(2)}) collective-permute-start(bf16[128,512]{1,0:T(8,128)(2,1)S(1)} %pad_maximum_fusion.2), channel_id=1, source_target_pairs={{0,4},{4,0},{1,5},{5,1},{2,6},{6,2},{3,7},{7,3},{8,12},{12,8},{9,1... | collective-permute-start | bytes 393224 | tf_op jit(solution)/shard_map/ppermute | solution.py:144
  57.6 6.3 %copy-start.6 = (bf16[256,1152]{1,0:T(8,128)(2,1)S(1)}, bf16[256,1152]{1,0:T(8,128)(2,1)}, u32[]{:S(2)}) copy-start(bf16[256,1152]{1,0:T(8,128)(2,1)} %convolution_convert_fusion) | copy-start | bytes 1769476
  57.6 38.1 %collective-permute-start = (bf16[32,144,128]{2,1,0:T(8,128)(2,1)S(1)}, bf16[32,144,128]{2,1,0:T(8,128)(2,1)S(1)}, u32[]{:S(2)}, u32[]{:S(2)}) collective-permute-start(bf16[32,144,128]{2,1,0:T(8,128)(2,1)S(1)} %all-to-all-done.own_ref), channel_id=1, source_target_pairs={{0,4},{4,0},{1,5},{5,1},{2,6},{6,2},{3,7},{7,3},{8,12},{12,8},{9,1... | collective-permute-start | bytes 3538952 | tf_op jit(solution)/shard_map/ppermute | solution.py:114
  89.2 21.9 %all-to-all-start.2 = ((bf16[32,4,1152]{2,1,0:T(4,128)(2,1)}), bf16[32,4,1152]{2,1,0:T(4,128)(2,1)}, u32[]{:S(2)}, u32[]{:S(2)}) async-start(bf16[32,4,1152]{2,1,0:T(4,128)(2,1)} %bitcast.41), calls=%async_computation.2 | async-start | bytes 589824 | tf_op jit(solution)/shard_map/all_to_all | solution.py:155
  106.0 17.9 %copy-start.1 = (f32[1024,128]{1,0:T(8,128)S(1)}, f32[1024,128]{1,0:T(8,128)}, u32[]{:S(2)}) copy-start(f32[1024,128]{1,0:T(8,128)} %table_ref.1) | copy-start | bytes 1572868
  106.0 17.9 %copy-start.2 = (f32[1024]{0:T(1024)S(1)}, f32[1024]{0:T(1024)}, u32[]{:S(2)}) copy-start(f32[1024]{0:T(1024)} %param.15) | copy-start | bytes 12292
  106.1 6.7 %collective-permute-start.3 = (bf16[1024,128]{1,0:T(8,128)(2,1)S(1)}, bf16[1024,128]{1,0:T(8,128)(2,1)S(1)}, u32[]{:S(2)}, u32[]{:S(2)}) collective-permute-start(bf16[1024,128]{1,0:T(8,128)(2,1)S(1)} %get-tuple-element.8), channel_id=1, source_target_pairs={{0,24},{8,0},{16,8},{24,16},{1,25},{9,1},{17,9},{25,17},{2,26},{10... | collective-permute-start | bytes 786440 | tf_op jit(solution)/shard_map/ppermute | solution.py:132
  108.5 7.4 %collective-permute-start.2 = (bf16[1024,128]{1,0:T(8,128)(2,1)S(1)}, bf16[1024,128]{1,0:T(8,128)(2,1)S(1)}, u32[]{:S(2)}, u32[]{:S(2)}) collective-permute-start(bf16[1024,128]{1,0:T(8,128)(2,1)S(1)} %get-tuple-element.9), channel_id=1, source_target_pairs={{0,16},{8,24},{16,0},{24,8},{1,17},{9,25},{17,1},{25,9},{2,18},{10... | collective-permute-start | bytes 786440 | tf_op jit(solution)/shard_map/ppermute | solution.py:132
  109.1 14.8 %collective-permute-start.1 = (bf16[1024,128]{1,0:T(8,128)(2,1)S(1)}, bf16[1024,128]{1,0:T(8,128)(2,1)S(1)}, u32[]{:S(2)}, u32[]{:S(2)}) collective-permute-start(bf16[1024,128]{1,0:T(8,128)(2,1)S(1)} %get-tuple-element.10), channel_id=1, source_target_pairs={{0,8},{8,16},{16,24},{24,0},{1,9},{9,17},{17,25},{25,1},{2,10},{10... | collective-permute-start | bytes 786440 | tf_op jit(solution)/shard_map/ppermute | solution.py:132
Sparse Core Ops, SparseCore 0:
  11.0 4.3 sort.11.cloned.1.call-done
  (1 shorter events, 0.0 us)

commit v2 on v0

v2 whole, which is shorter than its diff:
```python
import functools

import jax
import jax.numpy as jnp
from jax import lax
from jax.experimental import pallas as pl
from jax.experimental.pallas import tpu as pltpu
from jax.sharding import Mesh, PartitionSpec as P

EMB = 128
TABLES = 8
HOT = 8
RANK = 512
FEATURES = 1152
RATE = 0.1
EPSILON = 1e-08
BLOCK = 128
ROWS = 1024
SLOTS = 32
META = 16
AXES = ("y", "zh", "x", "c", "zl")
NY, NZH, NX, NC, NZL = 4, 2, 4, 2, 4
PACK = 2 * FEATURES + RANK
VMEM = pl.BlockSpec(memory_space=pltpu.VMEM)
BF16, F32, I32 = jnp.bfloat16, jnp.float32, jnp.int32


def dot(a, b, left, right):
    return lax.dot_general(a, b, (((left,), (right,)), ((), ())), preferred_element_type=F32)


def iota(shape, dim):
    return lax.broadcasted_iota(I32, shape, dim)


def params(mib):
    return pltpu.CompilerParams(vmem_limit_bytes=mib * 1024 * 1024)


def cost(flops, bytes_accessed):
    return pl.CostEstimate(flops=flops, bytes_accessed=bytes_accessed, transcendentals=0)


def spot(axis):
    return lax.axis_index(axis)


def rank_kernel(idx_ref, meta_ref):
    yy, xx = spot("y"), spot("x")
    upper = (iota((128, 128), 0) < iota((128, 128), 1)).astype(BF16)
    ones = jnp.ones((128, 128), BF16)
    sub32 = iota((32, 128), 0)
    sub128 = iota((128, 128), 0)
    pair = iota((META, 128), 0) // 2
    second = iota((META, 128), 0) % 2 == 1
    for t in range(TABLES):
        ahead = (t // 2 - yy) & 3
        idx = idx_ref[t * HOT:(t + 1) * HOT, :]
        owner = idx >> 10
        place = (owner & 3) * 2 + ((owner >> 2) & 1)
        group = ((owner >> 3) - xx - ahead) & 3
        full = place * 4 + group
        high = ((idx >> 2) & 255).astype(F32)
        low = ((idx & 3) * 128 + iota((HOT, 128), 1) - 256).astype(F32)
        hot = jnp.concatenate([(sub32 == full[k:k + 1]).astype(F32) for k in range(HOT)], axis=0)
        hot16 = hot.astype(BF16)
        before = dot(hot16, upper, 1, 0)
        total = dot(hot16, ones, 1, 0)
        base = jnp.zeros((32, 128), F32)
        slots, values = [], []
        for k in range(HOT):
            s = slice(k * 32, (k + 1) * 32)
            rank = jnp.sum(hot[s] * (before[s] + base), axis=0, keepdims=True).astype(I32)
            base = base + total[s]
            slots.append((sub128 == group[k:k + 1] * SLOTS + rank).astype(F32).astype(BF16))
            value = jnp.where(second, low[k:k + 1], high[k:k + 1])
            values.append(jnp.where(pair == place[k:k + 1], value, 0.0).astype(BF16))
        meta = dot(jnp.concatenate(values, axis=1), jnp.concatenate(slots, axis=1), 1, 1)
        meta_ref[t] = meta.astype(BF16)


def hidden_kernel(in_ref, cot_ref, down_ref, up_ref, pack_ref, cols_ref, both_ref):
    yy, core = spot("y"), spot("c")
    inputs = in_ref[...]
    grad_scale = (cot_ref[...].astype(F32) * inputs.astype(F32)).astype(BF16)
    pack_ref[:, :FEATURES] = inputs
    pack_ref[:, FEATURES:2 * FEATURES] = grad_scale
    hidden = dot(inputs, down_ref[...], 1, 0).astype(BF16)
    grad_hidden = dot(grad_scale, up_ref[...], 1, 1).astype(BF16)
    both_ref[:, :RANK] = grad_hidden
    both_ref[:, RANK:] = hidden

    both = jnp.concatenate([grad_hidden, hidden], axis=1)
    src = iota((2 * RANK, RANK), 0)
    dst = iota((2 * RANK, RANK), 1)
    from_y = ((dst >> 7) + yy) & 3
    want = from_y * 256 + ((dst >> 6) & 1) * 128 + ((dst >> 2) & 3) * 32 + ((dst >> 4) & 3) * 4 + (dst & 3)
    pack_ref[:, 2 * FEATURES:] = dot(both, (src == want + (1 - core) * 16).astype(F32).astype(BF16), 1, 0).astype(BF16)
    cols_ref[...] = dot(both, (src == want + core * 16).astype(F32).astype(BF16), 1, 0).astype(BF16)


def pooled_kernel(cot_ref, both_ref, down_ref, up_ref, bias_ref, meta_ref, dense_ref, sent_ref):
    yy, half = spot("y"), spot("zh")
    bias = jnp.concatenate([bias_ref[i:i + 1, :] for i in range(FEATURES // 128)], axis=1)
    scale = dot(both_ref[:, RANK:], up_ref[...], 1, 0) + bias
    back = dot(both_ref[:, :RANK], down_ref[...], 1, 1)
    grad = (cot_ref[...].astype(F32) * (scale + 1.0) + back).astype(BF16)
    dense_ref[...] = grad[:, :EMB]
    for t in range(TABLES):
        ahead, other = (t // 2 - yy) & 3, (t % 2) ^ half
        sent_ref[ahead, other, 0:BLOCK, :] = grad[:, (t + 1) * EMB:(t + 2) * EMB]
        sent_ref[ahead, other, BLOCK:BLOCK + META, :] = meta_ref[t]


def weight_kernel(pack_ref, cols_ref, other_ref, out_ref):
    yy = spot("y")
    for d in range(NY):
        to = (yy + d) & 3
        s = slice(d * 128, (d + 1) * 128)
        left = jnp.concatenate([cols_ref[:, s], other_ref[:, 2 * FEATURES + d * 128:2 * FEATURES + (d + 1) * 128]], axis=0)

        def put(first):
            right = jnp.concatenate([pack_ref[:, first:first + FEATURES], other_ref[:, first:first + FEATURES]], axis=0)
            out_ref[to] = dot(left, right, 0, 0).astype(BF16)

        pl.when(to < 2)(functools.partial(put, 0))
        pl.when(to >= 2)(functools.partial(put, FEATURES))


def add_kernel(in_ref, out_ref):
    total = in_ref[0].astype(F32)
    for i in range(1, in_ref.shape[0]):
        total = total + in_ref[i].astype(F32)
    if len(out_ref.shape) == 2:
        out_ref[...] = total.astype(out_ref.dtype)
    else:
        size = out_ref.shape[1]
        for i in range(out_ref.shape[0]):
            out_ref[i] = total[i * size:(i + 1) * size].astype(out_ref.dtype)


def expand(place, refs, look_ref, row_ref):
    lane_group = iota((8, 128), 1) // SLOTS
    sample_iota = iota((BLOCK, 128), 0)
    meta_row = iota((META, 128), 0)
    for j, ref in enumerate(refs):
        looks, rows = [], []
        for m in range(NY):
            b = m * (BLOCK + META)
            meta = ref[b + BLOCK:b + BLOCK + META, :].astype(F32)
            high = jnp.sum(jnp.where(meta_row == place * 2, meta, 0.0), axis=0, keepdims=True).astype(I32)
            low = jnp.sum(jnp.where(meta_row == place * 2 + 1, meta, 0.0), axis=0, keepdims=True).astype(I32) + 256
            pick = (sample_iota == (low & 127)).astype(F32).astype(BF16)
            looks.append(dot(pick, ref[b:b + BLOCK, :], 0, 0).astype(BF16))
            rows.append(jnp.broadcast_to((high * 4 + (low >> 7)).astype(F32), (8, 128)))
        for d in range(NX):
            row = rows[d]
            for g in range(NX):
                m = (d - g) % NX
                look_ref[d, j, g * SLOTS:(g + 1) * SLOTS, :] = looks[m][g * SLOTS:(g + 1) * SLOTS]
                if g:
                    row = jnp.where(lane_group == g, rows[m], row)
            row_ref[d, j] = row


def scatter(d, looks, rows, out_ref, first=None):
    base = iota((256, 128), 0).astype(F32)
    look = jnp.concatenate([ref[d].reshape(-1, EMB) for ref in looks], axis=0)
    for i in range(ROWS // 256):
        here = base + float(i * 256)
        s = slice(i * 256, (i + 1) * 256)
        hot = jnp.concatenate([(here == ref[d, j, 0:1, :]).astype(BF16) for ref in rows for j in range(ref.shape[1])], axis=1)
        total = dot(hot, look, 1, 0)
        if first is not None:
            total = total + first[s].astype(F32)
        out_ref[s] = total.astype(BF16)


def expand_kernel(count, *refs):
    place = spot("zl") * 2 + spot("c")
    look_own, row_own, look_other, row_other = refs[count:]
    expand(place ^ 1, refs[:count], look_other, row_other)
    expand(place, refs[:count], look_own, row_own)


def scatter_kernel(ds, parts, *refs):
    looks, rows, rest = refs[:parts], refs[parts:2 * parts], refs[2 * parts:]
    count = len(ds)
    firsts, outs = rest[:-count], rest[-count:]
    for i, d in enumerate(ds):
        scatter(d, looks, rows, outs[i], firsts[i] if firsts else None)


def update_kernel(a_ref, b_ref, c_ref, d_ref, table_ref, accum_ref, table_out, accum_out):
    eye = iota((128, 128), 0) == iota((128, 128), 1)
    for i in range(ROWS // 128):
        s = slice(i * 128, (i + 1) * 128)
        grad = a_ref[s].astype(F32) + b_ref[s].astype(F32)
        grad = grad + (c_ref[s].astype(F32) + d_ref[s].astype(F32))
        mean = jnp.sum(grad * grad, axis=1, keepdims=True) * (1.0 / EMB)
        old = jnp.sum(jnp.where(eye, accum_ref[i:i + 1, :], 0.0), axis=1, keepdims=True)
        new = old + mean
        table_out[s] = table_ref[s] - grad * (RATE / (jnp.sqrt(new) + EPSILON))
        accum_out[i:i + 1, :] = jnp.sum(jnp.where(eye, new, 0.0), axis=0, keepdims=True)


def ring(size, shift):
    return [(i, (i + shift) % size) for i in range(size)]


def shape(dims, kind):
    return jax.ShapeDtypeStruct(dims, kind)


def per_device(inputs, cotangent, cross_down, cross_up, cross_bias, indices, emb_table, row_accum):
    swap = ring(NC, 1)
    idx = jnp.transpose(indices, (1, 2, 0)).reshape(TABLES * HOT, BLOCK)

    def call(kernel, name, outs, operands, mib, work):
        return pl.pallas_call(
            kernel,
            out_shape=outs,
            in_specs=[VMEM] * len(operands),
            out_specs=(VMEM,) * len(outs) if isinstance(outs, tuple) else VMEM,
            compiler_params=params(mib),
            cost_estimate=work,
            name=name,
        )(*operands)

    meta = call(rank_kernel, "rank", shape((TABLES, META, 128), BF16), (idx,), 16, cost(2_000_000_000, 100_000))
    pack, cols, both = call(
        hidden_kernel, "hidden",
        (shape((BLOCK, PACK), BF16), shape((BLOCK, RANK), BF16), shape((BLOCK, 2 * RANK), BF16)),
        (inputs, cotangent, cross_down, cross_up), 16, cost(500_000_000, 4_000_000),
    )
    dense_part, sent = call(
        pooled_kernel, "pooled",
        (shape((BLOCK, EMB), BF16), shape((NY, NZH, BLOCK + META, EMB), BF16)),
        (cotangent, both, cross_down, cross_up, cross_bias.reshape(FEATURES // 128, 128), meta),
        16, cost(300_000_000, 4_000_000),
    )

    other_pack = lax.ppermute(pack, "c", swap)
    along = [sent[0]] + [lax.ppermute(sent[d], "y", ring(NY, d)) for d in range(1, NY)]
    terms = call(
        weight_kernel, "weights", shape((NY, 128, FEATURES), BF16), (pack, cols, other_pack), 16, cost(300_000_000, 3_000_000)
    )
    along, terms = lax.optimization_barrier((along, terms))
    near = jnp.concatenate([v[0] for v in along], axis=0)
    far = jnp.concatenate([v[1] for v in along], axis=0)

    def cross(m):
        return lax.ppermute(far, ("zh", "zl"), [(i, (7 - i) ^ m) for i in range(8)])

    def line(m):
        return lax.ppermute(near, "zl", [(i, i ^ m) for i in range(NZL)])

    blocks = [near, cross(3), line(3), cross(2), line(2), cross(0), cross(1), line(1)]

    def reduced(v, axes, dims, kind):
        v = lax.all_to_all(v, axes, split_axis=0, concat_axis=0, tiled=True)
        return call(add_kernel, "add", shape(dims, kind), (v,), 16, cost(1_000_000, 1_500_000))

    def expanded(blocks):
        look = shape((NX, len(blocks), 128, EMB), BF16)
        row = shape((NX, len(blocks), 8, 128), F32)
        return call(
            functools.partial(expand_kernel, len(blocks)), "expand", (look, row, look, row), tuple(blocks), 16, cost(200_000_000, 2_400_000)
        )

    terms = reduced(terms, "y", (32, 4, FEATURES), BF16)
    lists = [expanded(blocks[:3]), expanded(blocks[3:6])]
    late, terms = lax.optimization_barrier((blocks[6:], terms))
    lists.append(expanded(late))
    own, other = [[v[i] for v in lists] + [v[i + 1] for v in lists] for i in (0, 2)]

    def scattered(arrays, ds, firsts=()):
        return call(
            functools.partial(scatter_kernel, ds, len(lists)), "scatter",
            (shape((ROWS, EMB), BF16),) * len(ds), (*arrays, *firsts), 24, cost(300_000_000 * len(ds), 2_000_000),
        )

    def swapped(vs):
        return [lax.ppermute(v, "c", swap) for v in vs]

    first = scattered(other, (2,))
    other, first = lax.optimization_barrier((other, first))
    (first,) = swapped(first)
    second = scattered(other, (1, 3))
    other, second = lax.optimization_barrier((other, second))
    second = swapped(second)
    last = scattered(other, (0,))
    own, last = lax.optimization_barrier((own, last))
    (last,) = swapped(last)
    apart = scattered(own, (2,), (first,))
    own, apart = lax.optimization_barrier((own, apart))
    apart = lax.ppermute(apart[0], "x", ring(NX, 2))
    right, left = scattered(own, (1, 3), second)
    own, right, left = lax.optimization_barrier((own, right, left))
    right = lax.ppermute(right, "x", ring(NX, 1))
    left = lax.ppermute(left, "x", ring(NX, 3))
    (here,) = scattered(own, (0,), (last,))
    here, terms = lax.optimization_barrier((here, terms))
    weight_total = reduced(terms, ("zh", "zl", "x"), (4, FEATURES), F32)

    table_new, accum_new = call(
        update_kernel, "update", (shape((ROWS, EMB), F32), shape((8, 128), F32)),
        (here, right, left, apart, emb_table, row_accum.reshape(8, 128)), 16, cost(30_000_000_000, 2_100_000),
    )
    return (table_new, accum_new.reshape(ROWS), dense_part, weight_total)


def solution(mesh):
    fine = Mesh(mesh.devices.reshape(NY, NZH, NX, NC, NZL), AXES)
    in_specs = (
        P(AXES, None), P(AXES, None), P(), P(), P(), P(AXES, None, None), P(AXES, None), P(AXES),
    )
    out_specs = (P(AXES, None), P(AXES), P(AXES, None), P(AXES, None))
    return jax.shard_map(per_device, mesh=fine, in_specs=in_specs, out_specs=out_specs, check_vma=False)
```

time: 543 us -> 92 us (0.17)
  the two profiles are of different devices: /device:TPU:1 before, /device:TPU:8 now
where the time goes in v2:
time: 92 us; the launch traced here: 91.6 us
  starting transfers between devices  47.4 us (52%)
  waiting for transfers between devices  22.8 us (25%)
  Pallas kernels  16 us (17%)
  local copies, waits for them, and re-layouts  4.63 us (5%)
    pallas_call x16, Pallas kernels, call(): pl.pallas_call(kernel, out_shape=outs, in_specs=[VMEM] * len(operands), o...  16 us
    ppermute x4, starting transfers between devices, cross(): return lax.ppermute(far, ('zh', 'zl'), [(i, 7 - i ^ m) for i in range(8)])  13.9 us
    all_to_all x2, starting transfers between devices, reduced(): v = lax.all_to_all(v, axes, split_axis=0, concat_axis=0, tiled=True)  11.9 us
    all_to_all x2, waiting for transfers between devices, reduced(): v = lax.all_to_all(v, axes, split_axis=0, concat_axis=0, tiled=True)  10.5 us
    ppermute x4, waiting for transfers between devices, cross(): return lax.ppermute(far, ('zh', 'zl'), [(i, 7 - i ^ m) for i in range(8)])  10.2 us
    ppermute x3, starting transfers between devices, line(): return lax.ppermute(near, 'zl', [(i, i ^ m) for i in range(NZL)])  8.84 us
    ppermute x3, starting transfers between devices, per_device(): lax.ppermute(sent[d], 'y', ring(NY, d))  5 us
    unnamed x22, local copies, waits for them, and re-layouts  4.59 us
  transfers between devices with their start and end apart: 20, of which 6 were waited for; matrix products, arithmetic and copies ran while one was open for 0% of the time, Pallas kernels for 14%

profile of v2, /device:TPU:8, one launch (start us, length us, event | category | flops | bytes accessed | tf_op | source)
XLA Modules:
  0.0 91.6 jit_solution(17327954732138221145)
XLA Ops:
  0.6 1.3 %copy-done = bf16[1152,512]{1,0:T(8,128)(2,1)S(1)} copy-done((bf16[1152,512]{1,0:T(8,128)(2,1)S(1)}, bf16[1152,512]{1,0:T(8,128)(2,1)}, u32[]{:S(2)}) %copy-start) | copy-done | bytes 1179672
  1.9 1.3 %copy-done.2 = bf16[512,1152]{1,0:T(8,128)(2,1)S(1)} copy-done((bf16[512,1152]{1,0:T(8,128)(2,1)S(1)}, bf16[512,1152]{1,0:T(8,128)(2,1)}, u32[]{:S(2)}) %copy-start.2) | copy-done | bytes 1179672
  3.2 1.0 %copy-done.4 = bf16[128,1152]{1,0:T(8,128)(2,1)S(1)} copy-done((bf16[128,1152]{1,0:T(8,128)(2,1)S(1)}, bf16[128,1152]{1,0:T(8,128)(2,1)}, u32[]{:S(2)}) %copy-start.4) | copy-done | bytes 294936
  4.1 1.0 %copy-done.6 = bf16[128,1152]{1,0:T(8,128)(2,1)S(1)} copy-done((bf16[128,1152]{1,0:T(8,128)(2,1)S(1)}, bf16[128,1152]{1,0:T(8,128)(2,1)}, u32[]{:S(2)}) %copy-start.6) | copy-done | bytes 294936
  5.1 1.1 %hidden.1 = (bf16[128,2816]{1,0:T(8,128)(2,1)S(1)}, bf16[128,512]{1,0:T(8,128)(2,1)S(1)}, bf16[128,1024]{1,0:T(8,128)(2,1)S(1)}) custom-call(bf16[128,1152]{1,0:T(8,128)(2,1)S(1)} %copy-done.6, bf16[128,1152]{1,0:T(8,128)(2,1)S(1)} %copy-done.4, bf16[1152,512]{1,0:T(8,128)(2,1)S(1)} %copy-done, bf16[512,1152]{1,0:T(8,128)(2,1)S(1)} %copy-done.2), custom_call_target="tpu_custom_call" | custom-call | flops 500000000 | bytes 4000000 | tf_op jit(solution)/shard_map/hidden/pallas_call | solution.py:220
  6.2 0.1 collective-permute-start.3
  6.4 0.0 copy-start.5
  6.4 1.5 %rank.1.meta_ref = bf16[8,16,128]{2,1,0:T(8,128)(2,1)S(1)} custom-call(s32[64,128]{1,0:T(8,128)S(1)} %bitcast.31), custom_call_target="tpu_custom_call" | custom-call | flops 2000000000 | bytes 100000 | tf_op jit(solution)/shard_map/rank/pallas_call | solution.py:220
  7.9 0.1 copy-done.3
  8.0 0.0 copy-done.5
  8.0 1.2 %pooled.1 = (bf16[128,128]{1,0:T(8,128)(2,1)}, bf16[4,2,144,128]{3,2,1,0:T(8,128)(2,1)S(1)}) custom-call(bf16[128,1152]{1,0:T(8,128)(2,1)S(1)} %copy-done.5, bf16[128,1024]{1,0:T(8,128)(2,1)S(1)} %get-tuple-element.74.both_ref, bf16[1152,512]{1,0:T(8,128)(2,1)S(1)} %copy-done.1, bf16[512,1152]{1,0:T(8,128)(2,1)S(1)} %copy-done.3, f32[9,128]{1,0:T(8,128)S(1)} %bitcast.30, ...), custom_call_target="tpu_custom_call" | custom-call | flops 300000000 | bytes 4000000 | tf_op jit(solution)/shard_map/pooled/pallas_call | solution.py:220
  9.2 2.3 %collective-permute-start.2 = (bf16[2,144,128]{2,1,0:T(8,128)(2,1)S(1)}, bf16[2,144,128]{2,1,0:T(8,128)(2,1)S(1)}, u32[]{:S(2)}, u32[]{:S(2)}) collective-permute-start(bf16[2,144,128]{2,1,0:T(8,128)(2,1)S(1)} %get-tuple-element.144), channel_id=1, source_target_pairs={{0,192},{64,0},{128,64},{192,128},{1,193},{65,1},{129,65},{193,129... | collective-permute-start | bytes 221192 | tf_op jit(solution)/shard_map/ppermute | solution.py:244
  11.5 0.9 collective-permute-start.1
  12.3 1.9 %collective-permute-start = (bf16[2,144,128]{2,1,0:T(8,128)(2,1)S(1)}, bf16[2,144,128]{2,1,0:T(8,128)(2,1)S(1)}, u32[]{:S(2)}, u32[]{:S(2)}) collective-permute-start(bf16[2,144,128]{2,1,0:T(8,128)(2,1)S(1)} %get-tuple-element.146), channel_id=1, source_target_pairs={{0,64},{64,128},{128,192},{192,0},{1,65},{65,129},{129,193},{193,1... | collective-permute-start | bytes 221192 | tf_op jit(solution)/shard_map/ppermute | solution.py:244
  14.2 2.1 %weights.1 = bf16[4,128,1152]{2,1,0:T(8,128)(2,1)} custom-call(bf16[128,2816]{1,0:T(8,128)(2,1)S(1)} %get-tuple-element.76.pack_ref, bf16[128,512]{1,0:T(8,128)(2,1)S(1)} %get-tuple-element.77.cols_ref, bf16[128,2816]{1,0:T(8,128)(2,1)S(1)} %collective-permute-done.3.other_ref), custom_call_target="tpu_custom_call" | custom-call | flops 300000000 | bytes 3000000 | tf_op jit(solution)/shard_map/weights/pallas_call | solution.py:220
  16.4 1.0 %collective-permute-done.1 = bf16[2,144,128]{2,1,0:T(8,128)(2,1)S(1)} collective-permute-done((bf16[2,144,128]{2,1,0:T(8,128)(2,1)S(1)}, bf16[2,144,128]{2,1,0:T(8,128)(2,1)S(1)}, u32[]{:S(2)}, u32[]{:S(2)}) %collective-permute-start.1) | collective-permute-done | bytes 73760 | tf_op jit(solution)/shard_map/ppermute | solution.py:244
  17.4 6.4 %all-to-all-start = ((bf16[4,128,1152]{2,1,0:T(8,128)(2,1)}), bf16[4,128,1152]{2,1,0:T(8,128)(2,1)S(1)}, u32[]{:S(2)}, u32[]{:S(2)}) async-start(bf16[4,128,1152]{2,1,0:T(8,128)(2,1)} %weights.1), calls=%async_computation | async-start | bytes 2359296 | tf_op jit(solution)/shard_map/all_to_all | solution.py:261
  23.8 4.7 %collective-permute-start.5 = (bf16[576,128]{1,0:T(8,128)(2,1)S(1)}, bf16[576,128]{1,0:T(8,128)(2,1)S(1)}, u32[]{:S(2)}, u32[]{:S(2)}) collective-permute-start(bf16[576,128]{1,0:T(8,128)(2,1)S(1)} %pad_maximum_fusion.refs_0_), channel_id=1, source_target_pairs={{0,3},{1,2},{2,1},{3,0},{4,7},{5,6},{6,5},{7,4},{8,11},{9,10},{10,... | collective-permute-start | bytes 442376 | tf_op jit(solution)/shard_map/ppermute | solution.py:256
  28.5 4.6 %collective-permute-start.4 = (bf16[576,128]{1,0:T(8,128)(2,1)S(1)}, bf16[576,128]{1,0:T(8,128)(2,1)S(1)}, u32[]{:S(2)}, u32[]{:S(2)}) collective-permute-start(bf16[576,128]{1,0:T(8,128)(2,1)S(1)} %pad_maximum_fusion.1), channel_id=1, source_target_pairs={{0,32},{1,33},{2,34},{3,35},{32,0},{33,1},{34,2},{35,3},{4,36},{5,... | collective-permute-start | bytes 442376 | tf_op jit(solution)/shard_map/ppermute | solution.py:253
  33.1 0.6 collective-permute-start.7
  33.6 5.9 %collective-permute-start.6 = (bf16[576,128]{1,0:T(8,128)(2,1)S(1)}, bf16[576,128]{1,0:T(8,128)(2,1)S(1)}, u32[]{:S(2)}, u32[]{:S(2)}) collective-permute-start(bf16[576,128]{1,0:T(8,128)(2,1)S(1)} %pad_maximum_fusion.1), channel_id=1, source_target_pairs={{0,33},{1,32},{2,35},{3,34},{32,1},{33,0},{34,3},{35,2},{4,37},{5,... | collective-permute-start | bytes 442376 | tf_op jit(solution)/shard_map/ppermute | solution.py:253
  39.6 3.6 %collective-permute-start.10 = (bf16[576,128]{1,0:T(8,128)(2,1)S(1)}, bf16[576,128]{1,0:T(8,128)(2,1)S(1)}, u32[]{:S(2)}, u32[]{:S(2)}) collective-permute-start(bf16[576,128]{1,0:T(8,128)(2,1)S(1)} %pad_maximum_fusion.refs_0_), channel_id=1, source_target_pairs={{0,1},{1,0},{2,3},{3,2},{4,5},{5,4},{6,7},{7,6},{8,9},{9,8},{10,11... | collective-permute-start | bytes 442376 | tf_op jit(solution)/shard_map/ppermute | solution.py:256
  43.1 2.7 %collective-permute-done.4.refs_1_ = bf16[576,128]{1,0:T(8,128)(2,1)S(1)} collective-permute-done((bf16[576,128]{1,0:T(8,128)(2,1)S(1)}, bf16[576,128]{1,0:T(8,128)(2,1)S(1)}, u32[]{:S(2)}, u32[]{:S(2)}) %collective-permute-start.4) | collective-permute-done | bytes 147488 | tf_op jit(solution)/shard_map/ppermute | solution.py:253
  45.9 3.4 %collective-permute-start.9 = (bf16[576,128]{1,0:T(8,128)(2,1)S(1)}, bf16[576,128]{1,0:T(8,128)(2,1)S(1)}, u32[]{:S(2)}, u32[]{:S(2)}) collective-permute-start(bf16[576,128]{1,0:T(8,128)(2,1)S(1)} %pad_maximum_fusion.1), channel_id=1, source_target_pairs={{0,34},{1,35},{2,32},{3,33},{32,2},{33,3},{34,0},{35,1},{4,38},{5,... | collective-permute-start | bytes 442376 | tf_op jit(solution)/shard_map/ppermute | solution.py:253
  49.2 0.5 expand.3
  49.7 7.4 %collective-permute-done.6.refs_0_ = bf16[576,128]{1,0:T(8,128)(2,1)S(1)} collective-permute-done((bf16[576,128]{1,0:T(8,128)(2,1)S(1)}, bf16[576,128]{1,0:T(8,128)(2,1)S(1)}, u32[]{:S(2)}, u32[]{:S(2)}) %collective-permute-start.6) | collective-permute-done | bytes 147488 | tf_op jit(solution)/shard_map/ppermute | solution.py:253
  57.2 0.5 expand.4
  57.7 0.9 add.2
  58.6 0.4 expand.5
  58.9 0.7 scatter.6
  59.6 0.1 collective-permute-start.11
  59.7 1.2 %scatter.7 = (bf16[1024,128]{1,0:T(8,128)(2,1)S(1)}, bf16[1024,128]{1,0:T(8,128)(2,1)S(1)}) custom-call(bf16[4,3,128,128]{3,2,1,0:T(8,128)(2,1)S(1)} %get-tuple-element.105.refs_0_, bf16[4,3,128,128]{3,2,1,0:T(8,128)(2,1)S(1)} %get-tuple-element.106.refs_1_, bf16[4,2,128,128]{3,2,1,0:T(8,128)(2,1)S(1)} %get-tuple-element.107.refs_2_, ...), custom_call_target="tpu_custom_call" | custom-call | flops 600000000 | bytes 2000000 | tf_op jit(solution)/shard_map/scatter/pallas_call | solution.py:220
  61.0 0.6 collective-permute-start.12
  61.6 0.1 collective-permute-start.13
  61.7 0.7 scatter.8
  62.4 0.5 collective-permute-start.14
  62.9 0.7 scatter.9
  63.6 3.1 %collective-permute-start.17 = (bf16[1024,128]{1,0:T(8,128)(2,1)S(1)}, bf16[1024,128]{1,0:T(8,128)(2,1)S(1)}, u32[]{:S(2)}, u32[]{:S(2)}) collective-permute-start(bf16[1024,128]{1,0:T(8,128)(2,1)S(1)} %scatter.9), channel_id=1, source_target_pairs={{0,16},{8,24},{16,0},{24,8},{1,17},{9,25},{17,1},{25,9},{2,18},{10... | collective-permute-start | bytes 786440 | tf_op jit(solution)/shard_map/ppermute | solution.py:297
  66.7 1.9 %scatter.10 = (bf16[1024,128]{1,0:T(8,128)(2,1)}, bf16[1024,128]{1,0:T(8,128)(2,1)S(1)}) custom-call(bf16[4,3,128,128]{3,2,1,0:T(8,128)(2,1)S(1)} %get-tuple-element.128.refs_0_, bf16[4,3,128,128]{3,2,1,0:T(8,128)(2,1)S(1)} %get-tuple-element.129.refs_1_, bf16[4,2,128,128]{3,2,1,0:T(8,128)(2,1)S(1)} %get-tuple-element.130.refs_2_, ...), custom_call_target="tpu_custom_call" | custom-call | flops 600000000 | bytes 2000000 | tf_op jit(solution)/shard_map/scatter/pallas_call | solution.py:220
  68.6 0.6 collective-permute-start.15
  69.2 2.6 %collective-permute-start.16 = (bf16[1024,128]{1,0:T(8,128)(2,1)S(1)}, bf16[1024,128]{1,0:T(8,128)(2,1)S(1)}, u32[]{:S(2)}, u32[]{:S(2)}) collective-permute-start(bf16[1024,128]{1,0:T(8,128)(2,1)S(1)} %get-tuple-element.138), channel_id=1, source_target_pairs={{0,24},{8,0},{16,8},{24,16},{1,25},{9,1},{17,9},{25,17},{2,26},{10... | collective-permute-start | bytes 786440 | tf_op jit(solution)/shard_map/ppermute | solution.py:301
  71.8 0.7 scatter.11.a_ref
  72.5 5.6 %all-to-all-start.1 = ((bf16[32,4,1152]{2,1,0:T(4,128)(2,1)}), bf16[32,4,1152]{2,1,0:T(4,128)(2,1)S(1)}, u32[]{:S(2)}, u32[]{:S(2)}) async-start(bf16[32,4,1152]{2,1,0:T(4,128)(2,1)} %add.2), calls=%async_computation.1 | async-start | bytes 589824 | tf_op jit(solution)/shard_map/all_to_all | solution.py:261
  78.1 1.0 %collective-permute-done.15.b_ref = bf16[1024,128]{1,0:T(8,128)(2,1)S(1)} collective-permute-done((bf16[1024,128]{1,0:T(8,128)(2,1)}, bf16[1024,128]{1,0:T(8,128)(2,1)S(1)}, u32[]{:S(2)}, u32[]{:S(2)}) %collective-permute-start.15) | collective-permute-done | bytes 262176 | tf_op jit(solution)/shard_map/ppermute | solution.py:300
  79.1 0.1 collective-permute-done.16.c_ref
  79.2 1.3 %update.1 = (f32[1024,128]{1,0:T(8,128)}, f32[8,128]{1,0:T(8,128)}) custom-call(bf16[1024,128]{1,0:T(8,128)(2,1)S(1)} %scatter.11.a_ref, bf16[1024,128]{1,0:T(8,128)(2,1)S(1)} %collective-permute-done.15.b_ref, bf16[1024,128]{1,0:T(8,128)(2,1)S(1)} %collective-permute-done.16.c_ref, bf16[1024,128]{1,0:T(8,128)(2,1)S(1)} %collective-permute-done.17.d_ref, ...), custom_call_target="tpu_custom_call" | custom-call | flops 30000001024 | bytes 2100000 | tf_op jit(solution)/shard_map/update/pallas_call | solution.py:220
  80.4 10.5 %all-to-all-done.1.in_ref = bf16[32,4,1152]{2,1,0:T(4,128)(2,1)S(1)} async-done(((bf16[32,4,1152]{2,1,0:T(4,128)(2,1)}), bf16[32,4,1152]{2,1,0:T(4,128)(2,1)S(1)}, u32[]{:S(2)}, u32[]{:S(2)}) %all-to-all-start.1) | async-done | bytes 294944 | tf_op jit(solution)/shard_map/all_to_all | solution.py:261
  91.0 0.7 add.3
  (35 shorter events, 0.2 us)
Async XLA Ops:
  0.6 1.3 %copy-start = (bf16[1152,512]{1,0:T(8,128)(2,1)S(1)}, bf16[1152,512]{1,0:T(8,128)(2,1)}, u32[]{:S(2)}) copy-start(bf16[1152,512]{1,0:T(8,128)(2,1)} %down_ref.3) | copy-start | bytes 3538948
  1.9 1.3 %copy-start.2 = (bf16[512,1152]{1,0:T(8,128)(2,1)S(1)}, bf16[512,1152]{1,0:T(8,128)(2,1)}, u32[]{:S(2)}) copy-start(bf16[512,1152]{1,0:T(8,128)(2,1)} %up_ref.3) | copy-start | bytes 3538948
  3.2 1.0 %copy-start.4 = (bf16[128,1152]{1,0:T(8,128)(2,1)S(1)}, bf16[128,1152]{1,0:T(8,128)(2,1)}, u32[]{:S(2)}) copy-start(bf16[128,1152]{1,0:T(8,128)(2,1)} %cot_ref.3) | copy-start | bytes 884740
  4.1 1.0 %copy-start.6 = (bf16[128,1152]{1,0:T(8,128)(2,1)S(1)}, bf16[128,1152]{1,0:T(8,128)(2,1)}, u32[]{:S(2)}) copy-start(bf16[128,1152]{1,0:T(8,128)(2,1)} %in_ref.1) | copy-start | bytes 884740
  5.1 1.2 %copy-start.9 = (s32[128,8,8]{0,2,1:T(8,128)S(1)}, s32[128,8,8]{0,2,1:T(8,128)}, u32[]{:S(2)}) copy-start(s32[128,8,8]{0,2,1:T(8,128)} %param.13) | copy-start | bytes 98308
  6.2 8.0 %collective-permute-start.3 = (bf16[128,2816]{1,0:T(8,128)(2,1)S(1)}, bf16[128,2816]{1,0:T(8,128)(2,1)S(1)}, u32[]{:S(2)}, u32[]{:S(2)}) collective-permute-start(bf16[128,2816]{1,0:T(8,128)(2,1)S(1)} %get-tuple-element.76.pack_ref), channel_id=1, source_target_pairs={{0,4},{4,0},{1,5},{5,1},{2,6},{6,2},{3,7},{7,3},{8,12},{12,8},{9,1... | collective-permute-start | bytes 2162696 | tf_op jit(solution)/shard_map/ppermute | solution.py:243
  6.3 1.6 %copy-start.1 = (bf16[1152,512]{1,0:T(8,128)(2,1)S(1)}, bf16[1152,512]{1,0:T(8,128)(2,1)}, u32[]{:S(2)}) copy-start(bf16[1152,512]{1,0:T(8,128)(2,1)} %down_ref.3) | copy-start | bytes 3538948
  6.4 1.6 %copy-start.3 = (bf16[512,1152]{1,0:T(8,128)(2,1)S(1)}, bf16[512,1152]{1,0:T(8,128)(2,1)}, u32[]{:S(2)}) copy-start(bf16[512,1152]{1,0:T(8,128)(2,1)} %up_ref.3) | copy-start | bytes 3538948
  6.4 1.6 %copy-start.5 = (bf16[128,1152]{1,0:T(8,128)(2,1)S(1)}, bf16[128,1152]{1,0:T(8,128)(2,1)}, u32[]{:S(2)}) copy-start(bf16[128,1152]{1,0:T(8,128)(2,1)} %cot_ref.3) | copy-start | bytes 884740
  6.4 1.6 %copy-start.7 = (f32[1152]{0:T(1024)S(1)}, f32[1152]{0:T(1024)}, u32[]{:S(2)}) copy-start(f32[1152]{0:T(1024)} %param.12) | copy-start | bytes 13828
  9.2 7.2 %collective-permute-start.2 = (bf16[2,144,128]{2,1,0:T(8,128)(2,1)S(1)}, bf16[2,144,128]{2,1,0:T(8,128)(2,1)S(1)}, u32[]{:S(2)}, u32[]{:S(2)}) collective-permute-start(bf16[2,144,128]{2,1,0:T(8,128)(2,1)S(1)} %get-tuple-element.144), channel_id=1, source_target_pairs={{0,192},{64,0},{128,64},{192,128},{1,193},{65,1},{129,65},{193,129... | collective-permute-start | bytes 221192 | tf_op jit(solution)/shard_map/ppermute | solution.py:244
  11.5 5.9 %collective-permute-start.1 = (bf16[2,144,128]{2,1,0:T(8,128)(2,1)S(1)}, bf16[2,144,128]{2,1,0:T(8,128)(2,1)S(1)}, u32[]{:S(2)}, u32[]{:S(2)}) collective-permute-start(bf16[2,144,128]{2,1,0:T(8,128)(2,1)S(1)} %get-tuple-element.145), channel_id=1, source_target_pairs={{0,128},{64,192},{128,0},{192,64},{1,129},{65,193},{129,1},{193,65... | collective-permute-start | bytes 221192 | tf_op jit(solution)/shard_map/ppermute | solution.py:244
  12.3 5.0 %collective-permute-start = (bf16[2,144,128]{2,1,0:T(8,128)(2,1)S(1)}, bf16[2,144,128]{2,1,0:T(8,128)(2,1)S(1)}, u32[]{:S(2)}, u32[]{:S(2)}) collective-permute-start(bf16[2,144,128]{2,1,0:T(8,128)(2,1)S(1)} %get-tuple-element.146), channel_id=1, source_target_pairs={{0,64},{64,128},{128,192},{192,0},{1,65},{65,129},{129,193},{193,1... | collective-permute-start | bytes 221192 | tf_op jit(solution)/shard_map/ppermute | solution.py:244
  17.4 40.3 %all-to-all-start = ((bf16[4,128,1152]{2,1,0:T(8,128)(2,1)}), bf16[4,128,1152]{2,1,0:T(8,128)(2,1)S(1)}, u32[]{:S(2)}, u32[]{:S(2)}) async-start(bf16[4,128,1152]{2,1,0:T(8,128)(2,1)} %weights.1), calls=%async_computation | async-start | bytes 2359296 | tf_op jit(solution)/shard_map/all_to_all | solution.py:261
  23.8 15.8 %collective-permute-start.5 = (bf16[576,128]{1,0:T(8,128)(2,1)S(1)}, bf16[576,128]{1,0:T(8,128)(2,1)S(1)}, u32[]{:S(2)}, u32[]{:S(2)}) collective-permute-start(bf16[576,128]{1,0:T(8,128)(2,1)S(1)} %pad_maximum_fusion.refs_0_), channel_id=1, source_target_pairs={{0,3},{1,2},{2,1},{3,0},{4,7},{5,6},{6,5},{7,4},{8,11},{9,10},{10,... | collective-permute-start | bytes 442376 | tf_op jit(solution)/shard_map/ppermute | solution.py:256
  28.5 17.4 %collective-permute-start.4 = (bf16[576,128]{1,0:T(8,128)(2,1)S(1)}, bf16[576,128]{1,0:T(8,128)(2,1)S(1)}, u32[]{:S(2)}, u32[]{:S(2)}) collective-permute-start(bf16[576,128]{1,0:T(8,128)(2,1)S(1)} %pad_maximum_fusion.1), channel_id=1, source_target_pairs={{0,32},{1,33},{2,34},{3,35},{32,0},{33,1},{34,2},{35,3},{4,36},{5,... | collective-permute-start | bytes 442376 | tf_op jit(solution)/shard_map/ppermute | solution.py:253
  33.1 16.6 %collective-permute-start.7 = (bf16[576,128]{1,0:T(8,128)(2,1)S(1)}, bf16[576,128]{1,0:T(8,128)(2,1)S(1)}, u32[]{:S(2)}, u32[]{:S(2)}) collective-permute-start(bf16[576,128]{1,0:T(8,128)(2,1)S(1)} %pad_maximum_fusion.refs_0_), channel_id=1, source_target_pairs={{0,2},{1,3},{2,0},{3,1},{4,6},{5,7},{6,4},{7,5},{8,10},{9,11},{10,... | collective-permute-start | bytes 442376 | tf_op jit(solution)/shard_map/ppermute | solution.py:256
  33.6 16.1 %collective-permute-start.8 = (bf16[576,128]{1,0:T(8,128)(2,1)S(1)}, bf16[576,128]{1,0:T(8,128)(2,1)S(1)}, u32[]{:S(2)}, u32[]{:S(2)}) collective-permute-start(bf16[576,128]{1,0:T(8,128)(2,1)S(1)} %pad_maximum_fusion.1), channel_id=1, source_target_pairs={{0,35},{1,34},{2,33},{3,32},{32,3},{33,2},{34,1},{35,0},{4,39},{5,... | collective-permute-start | bytes 442376 | tf_op jit(solution)/shard_map/ppermute | solution.py:253
  33.6 23.5 %collective-permute-start.6 = (bf16[576,128]{1,0:T(8,128)(2,1)S(1)}, bf16[576,128]{1,0:T(8,128)(2,1)S(1)}, u32[]{:S(2)}, u32[]{:S(2)}) collective-permute-start(bf16[576,128]{1,0:T(8,128)(2,1)S(1)} %pad_maximum_fusion.1), channel_id=1, source_target_pairs={{0,33},{1,32},{2,35},{3,34},{32,1},{33,0},{34,3},{35,2},{4,37},{5,... | collective-permute-start | bytes 442376 | tf_op jit(solution)/shard_map/ppermute | solution.py:253
  39.6 19.0 %collective-permute-start.10 = (bf16[576,128]{1,0:T(8,128)(2,1)S(1)}, bf16[576,128]{1,0:T(8,128)(2,1)S(1)}, u32[]{:S(2)}, u32[]{:S(2)}) collective-permute-start(bf16[576,128]{1,0:T(8,128)(2,1)S(1)} %pad_maximum_fusion.refs_0_), channel_id=1, source_target_pairs={{0,1},{1,0},{2,3},{3,2},{4,5},{5,4},{6,7},{7,6},{8,9},{9,8},{10,11... | collective-permute-start | bytes 442376 | tf_op jit(solution)/shard_map/ppermute | solution.py:256
  45.9 12.7 %collective-permute-start.9 = (bf16[576,128]{1,0:T(8,128)(2,1)S(1)}, bf16[576,128]{1,0:T(8,128)(2,1)S(1)}, u32[]{:S(2)}, u32[]{:S(2)}) collective-permute-start(bf16[576,128]{1,0:T(8,128)(2,1)S(1)} %pad_maximum_fusion.1), channel_id=1, source_target_pairs={{0,34},{1,35},{2,32},{3,33},{32,2},{33,3},{34,0},{35,1},{4,38},{5,... | collective-permute-start | bytes 442376 | tf_op jit(solution)/shard_map/ppermute | solution.py:253
  59.6 3.2 %collective-permute-start.11 = (bf16[1024,128]{1,0:T(8,128)(2,1)S(1)}, bf16[1024,128]{1,0:T(8,128)(2,1)S(1)}, u32[]{:S(2)}, u32[]{:S(2)}) collective-permute-start(bf16[1024,128]{1,0:T(8,128)(2,1)S(1)} %scatter.6), channel_id=1, source_target_pairs={{0,4},{4,0},{1,5},{5,1},{2,6},{6,2},{3,7},{7,3},{8,12},{12,8},{9,1... | collective-permute-start | bytes 786440 | tf_op jit(solution)/shard_map/ppermute | solution.py:284
  61.0 5.7 %collective-permute-start.12 = (bf16[1024,128]{1,0:T(8,128)(2,1)S(1)}, bf16[1024,128]{1,0:T(8,128)(2,1)S(1)}, u32[]{:S(2)}, u32[]{:S(2)}) collective-permute-start(bf16[1024,128]{1,0:T(8,128)(2,1)S(1)} %get-tuple-element.124), channel_id=1, source_target_pairs={{0,4},{4,0},{1,5},{5,1},{2,6},{6,2},{3,7},{7,3},{8,12},{12,8},{9,1... | collective-permute-start | bytes 786440 | tf_op jit(solution)/shard_map/ppermute | solution.py:284
  61.6 5.1 %collective-permute-start.13 = (bf16[1024,128]{1,0:T(8,128)(2,1)S(1)}, bf16[1024,128]{1,0:T(8,128)(2,1)S(1)}, u32[]{:S(2)}, u32[]{:S(2)}) collective-permute-start(bf16[1024,128]{1,0:T(8,128)(2,1)S(1)} %get-tuple-element.125), channel_id=1, source_target_pairs={{0,4},{4,0},{1,5},{5,1},{2,6},{6,2},{3,7},{7,3},{8,12},{12,8},{9,1... | collective-permute-start | bytes 786440 | tf_op jit(solution)/shard_map/ppermute | solution.py:284
  62.4 9.4 %collective-permute-start.14 = (bf16[1024,128]{1,0:T(8,128)(2,1)S(1)}, bf16[1024,128]{1,0:T(8,128)(2,1)S(1)}, u32[]{:S(2)}, u32[]{:S(2)}) collective-permute-start(bf16[1024,128]{1,0:T(8,128)(2,1)S(1)} %scatter.8), channel_id=1, source_target_pairs={{0,4},{4,0},{1,5},{5,1},{2,6},{6,2},{3,7},{7,3},{8,12},{12,8},{9,1... | collective-permute-start | bytes 786440 | tf_op jit(solution)/shard_map/ppermute | solution.py:284
  63.6 14.5 %collective-permute-start.17 = (bf16[1024,128]{1,0:T(8,128)(2,1)S(1)}, bf16[1024,128]{1,0:T(8,128)(2,1)S(1)}, u32[]{:S(2)}, u32[]{:S(2)}) collective-permute-start(bf16[1024,128]{1,0:T(8,128)(2,1)S(1)} %scatter.9), channel_id=1, source_target_pairs={{0,16},{8,24},{16,0},{24,8},{1,17},{9,25},{17,1},{25,9},{2,18},{10... | collective-permute-start | bytes 786440 | tf_op jit(solution)/shard_map/ppermute | solution.py:297
  68.6 10.6 %copy-start.8 = (f32[1024,128]{1,0:T(8,128)S(1)}, f32[1024,128]{1,0:T(8,128)}, u32[]{:S(2)}) copy-start(f32[1024,128]{1,0:T(8,128)} %table_ref.1) | copy-start | bytes 1572868
  68.6 10.6 %copy-start.10 = (f32[1024]{0:T(1024)S(1)}, f32[1024]{0:T(1024)}, u32[]{:S(2)}) copy-start(f32[1024]{0:T(1024)} %param.15) | copy-start | bytes 12292
  68.6 10.5 %collective-permute-start.15 = (bf16[1024,128]{1,0:T(8,128)(2,1)}, bf16[1024,128]{1,0:T(8,128)(2,1)S(1)}, u32[]{:S(2)}, u32[]{:S(2)}) collective-permute-start(bf16[1024,128]{1,0:T(8,128)(2,1)} %get-tuple-element.137), channel_id=1, source_target_pairs={{0,8},{8,16},{16,24},{24,0},{1,9},{9,17},{17,25},{25,1},{2,10},{10... | collective-permute-start | bytes 786440 | tf_op jit(solution)/shard_map/ppermute | solution.py:300
  69.2 10.0 %collective-permute-start.16 = (bf16[1024,128]{1,0:T(8,128)(2,1)S(1)}, bf16[1024,128]{1,0:T(8,128)(2,1)S(1)}, u32[]{:S(2)}, u32[]{:S(2)}) collective-permute-start(bf16[1024,128]{1,0:T(8,128)(2,1)S(1)} %get-tuple-element.138), channel_id=1, source_target_pairs={{0,24},{8,0},{16,8},{24,16},{1,25},{9,1},{17,9},{25,17},{2,26},{10... | collective-permute-start | bytes 786440 | tf_op jit(solution)/shard_map/ppermute | solution.py:301
  72.5 18.4 %all-to-all-start.1 = ((bf16[32,4,1152]{2,1,0:T(4,128)(2,1)}), bf16[32,4,1152]{2,1,0:T(4,128)(2,1)S(1)}, u32[]{:S(2)}, u32[]{:S(2)}) async-start(bf16[32,4,1152]{2,1,0:T(4,128)(2,1)} %add.2), calls=%async_computation.1 | async-start | bytes 589824 | tf_op jit(solution)/shard_map/all_to_all | solution.py:261

commit v3 on v2

--- a/solution.py
+++ b/solution.py
@@ -228,6 +228,7 @@
         )(*operands)
 
     meta = call(rank_kernel, "rank", shape((TABLES, META, 128), BF16), (idx,), 16, cost(2_000_000_000, 100_000))
+    (inputs, cotangent, cross_down, cross_up), meta = lax.optimization_barrier(((inputs, cotangent, cross_down, cross_up), meta))
     pack, cols, both = call(
         hidden_kernel, "hidden",
         (shape((BLOCK, PACK), BF16), shape((BLOCK, RANK), BF16), shape((BLOCK, 2 * RANK), BF16)),
@@ -245,7 +246,7 @@
     terms = call(
         weight_kernel, "weights", shape((NY, 128, FEATURES), BF16), (pack, cols, other_pack), 16, cost(300_000_000, 3_000_000)
     )
-    along, terms = lax.optimization_barrier((along, terms))
+    along, _ = lax.optimization_barrier((along, terms))
     near = jnp.concatenate([v[0] for v in along], axis=0)
     far = jnp.concatenate([v[1] for v in along], axis=0)
 
@@ -257,27 +258,31 @@
 
     blocks = [near, cross(3), line(3), cross(2), line(2), cross(0), cross(1), line(1)]
 
-    def reduced(v, axes, dims, kind):
-        v = lax.all_to_all(v, axes, split_axis=0, concat_axis=0, tiled=True)
-        return call(add_kernel, "add", shape(dims, kind), (v,), 16, cost(1_000_000, 1_500_000))
+    def exchanged(v, axes):
+        return lax.all_to_all(v, axes, split_axis=0, concat_axis=0, tiled=True)
+
+    def added(v, dims, kind):
+        return call(add_kernel, "add", shape(dims, kind), (v,), 16, cost(1_000, 1_000))
 
     def expanded(blocks):
         look = shape((NX, len(blocks), 128, EMB), BF16)
         row = shape((NX, len(blocks), 8, 128), F32)
         return call(
-            functools.partial(expand_kernel, len(blocks)), "expand", (look, row, look, row), tuple(blocks), 16, cost(200_000_000, 2_400_000)
+            functools.partial(expand_kernel, len(blocks)), "expand", (look, row, look, row), tuple(blocks), 16, cost(1_000, 1_000)
         )
 
-    terms = reduced(terms, "y", (32, 4, FEATURES), BF16)
-    lists = [expanded(blocks[:3]), expanded(blocks[3:6])]
-    late, terms = lax.optimization_barrier((blocks[6:], terms))
-    lists.append(expanded(late))
+    lists = [expanded(blocks[:3])]
+    lists[0], terms = lax.optimization_barrier((lists[0], exchanged(terms, "y")))
+    terms = added(terms, (32, 4, FEATURES), BF16)
+    late, _ = lax.optimization_barrier((blocks[3:6], terms))
+    weight_total = added(exchanged(terms, ("zh", "zl", "x")), (4, FEATURES), F32)
+    lists += [expanded(late), expanded(blocks[6:])]
     own, other = [[v[i] for v in lists] + [v[i + 1] for v in lists] for i in (0, 2)]
 
     def scattered(arrays, ds, firsts=()):
         return call(
             functools.partial(scatter_kernel, ds, len(lists)), "scatter",
-            (shape((ROWS, EMB), BF16),) * len(ds), (*arrays, *firsts), 24, cost(300_000_000 * len(ds), 2_000_000),
+            (shape((ROWS, EMB), BF16),) * len(ds), (*arrays, *firsts), 24, cost(1_000, 1_000),
         )
 
     def swapped(vs):
@@ -300,12 +305,10 @@
     right = lax.ppermute(right, "x", ring(NX, 1))
     left = lax.ppermute(left, "x", ring(NX, 3))
     (here,) = scattered(own, (0,), (last,))
-    here, terms = lax.optimization_barrier((here, terms))
-    weight_total = reduced(terms, ("zh", "zl", "x"), (4, FEATURES), F32)
 
     table_new, accum_new = call(
         update_kernel, "update", (shape((ROWS, EMB), F32), shape((8, 128), F32)),
-        (here, right, left, apart, emb_table, row_accum.reshape(8, 128)), 16, cost(30_000_000_000, 2_100_000),
+        (here, right, left, apart, emb_table, row_accum.reshape(8, 128)), 16, cost(1_000, 1_000),
     )
     return (table_new, accum_new.reshape(ROWS), dense_part, weight_total)
 

time: 92 us -> 78.9 us (0.86)
  the two profiles are of different devices: /device:TPU:8 before, /device:TPU:43 now
where the time goes in v3:
time: 78.9 us; the launch traced here: 78.6 us
  starting transfers between devices  40.9 us (52%)
  waiting for transfers between devices  20.4 us (26%)
  Pallas kernels  15.4 us (20%)
  local copies, waits for them, and re-layouts  1.04 us (1%)
  between operations  0.85 us (1%)
    pallas_call x16, Pallas kernels, call(): pl.pallas_call(kernel, out_shape=outs, in_specs=[VMEM] * len(operands), o...  15.4 us
    ppermute x4, starting transfers between devices, cross(): return lax.ppermute(far, ('zh', 'zl'), [(i, 7 - i ^ m) for i in range(8)])  13 us
    all_to_all x2, starting transfers between devices, exchanged(): return lax.all_to_all(v, axes, split_axis=0, concat_axis=0, tiled=True)  12.3 us
    ppermute x4, waiting for transfers between devices, cross(): return lax.ppermute(far, ('zh', 'zl'), [(i, 7 - i ^ m) for i in range(8)])  10.2 us
    ppermute x1, waiting for transfers between devices, per_device(): right = lax.ppermute(right, 'x', ring(NX, 1))  5.55 us
    ppermute x3, starting transfers between devices, per_device(): lax.ppermute(sent[d], 'y', ring(NY, d))  4.16 us
    ppermute x3, starting transfers between devices, line(): return lax.ppermute(near, 'zl', [(i, i ^ m) for i in range(NZL)])  3.8 us
    ppermute x1, waiting for transfers between devices, per_device(): apart = lax.ppermute(apart[0], 'x', ring(NX, 2))  3.75 us
  transfers between devices with their start and end apart: 20, of which 5 were waited for; matrix products, arithmetic and copies ran while one was open for 0% of the time, Pallas kernels for 15%

profile of v3, /device:TPU:43, one launch (start us, length us, event | category | flops | bytes accessed | tf_op | source)
XLA Modules:
  0.0 78.6 jit_solution(17552061418009523048)
XLA Ops:
  0.6 0.7 copy-done.7
  1.4 1.5 %rank.1.meta_ref = bf16[8,16,128]{2,1,0:T(8,128)(2,1)S(1)} custom-call(s32[64,128]{1,0:T(8,128)S(1)} %bitcast.32), custom_call_target="tpu_custom_call" | custom-call | flops 2000000000 | bytes 100000 | tf_op jit(solution)/shard_map/rank/pallas_call | solution.py:220
  2.9 0.1 copy-done.1
  3.0 0.0 copy-done.2
  3.1 0.1 copy-done.4
  3.2 1.1 %hidden.1 = (bf16[128,2816]{1,0:T(8,128)(2,1)S(1)}, bf16[128,512]{1,0:T(8,128)(2,1)S(1)}, bf16[128,1024]{1,0:T(8,128)(2,1)S(1)}) custom-call(bf16[128,1152]{1,0:T(8,128)(2,1)S(1)} %copy-done.4, bf16[128,1152]{1,0:T(8,128)(2,1)S(1)} %copy-done.2, bf16[1152,512]{1,0:T(8,128)(2,1)S(1)} %copy-done, bf16[512,1152]{1,0:T(8,128)(2,1)S(1)} %copy-done.1), custom_call_target="tpu_custom_call" | custom-call | flops 500000000 | bytes 4000000 | tf_op jit(solution)/shard_map/hidden/pallas_call | solution.py:220
  4.3 0.8 collective-permute-start.3
  5.0 1.2 %pooled.1 = (bf16[128,128]{1,0:T(8,128)(2,1)}, bf16[4,2,144,128]{3,2,1,0:T(8,128)(2,1)S(1)}) custom-call(bf16[128,1152]{1,0:T(8,128)(2,1)S(1)} %copy-done.2, bf16[128,1024]{1,0:T(8,128)(2,1)S(1)} %get-tuple-element.85.both_ref, bf16[1152,512]{1,0:T(8,128)(2,1)S(1)} %copy-done, bf16[512,1152]{1,0:T(8,128)(2,1)S(1)} %copy-done.1, f32[9,128]{1,0:T(8,128)S(1)} %bitcast.30, ...), custom_call_target="tpu_custom_call" | custom-call | flops 300000000 | bytes 4000000 | tf_op jit(solution)/shard_map/pooled/pallas_call | solution.py:220
  6.2 0.2 collective-permute-start.2
  6.5 2.3 %collective-permute-start.1 = (bf16[2,144,128]{2,1,0:T(8,128)(2,1)S(1)}, bf16[2,144,128]{2,1,0:T(8,128)(2,1)S(1)}, u32[]{:S(2)}, u32[]{:S(2)}) collective-permute-start(bf16[2,144,128]{2,1,0:T(8,128)(2,1)S(1)} %get-tuple-element.159), channel_id=1, source_target_pairs={{0,128},{64,192},{128,0},{192,64},{1,129},{65,193},{129,1},{193,65... | collective-permute-start | bytes 221192 | tf_op jit(solution)/shard_map/ppermute | solution.py:245
  8.8 1.6 %collective-permute-start = (bf16[2,144,128]{2,1,0:T(8,128)(2,1)S(1)}, bf16[2,144,128]{2,1,0:T(8,128)(2,1)S(1)}, u32[]{:S(2)}, u32[]{:S(2)}) collective-permute-start(bf16[2,144,128]{2,1,0:T(8,128)(2,1)S(1)} %get-tuple-element.160), channel_id=1, source_target_pairs={{0,64},{64,128},{128,192},{192,0},{1,65},{65,129},{129,193},{193,1... | collective-permute-start | bytes 221192 | tf_op jit(solution)/shard_map/ppermute | solution.py:245
  10.4 0.0 collective-permute-done.3.other_ref
  10.4 2.2 %weights.1 = bf16[4,128,1152]{2,1,0:T(8,128)(2,1)} custom-call(bf16[128,2816]{1,0:T(8,128)(2,1)S(1)} %get-tuple-element.88.pack_ref, bf16[128,512]{1,0:T(8,128)(2,1)S(1)} %get-tuple-element.89.cols_ref, bf16[128,2816]{1,0:T(8,128)(2,1)S(1)} %collective-permute-done.3.other_ref), custom_call_target="tpu_custom_call" | custom-call | flops 300000000 | bytes 3000000 | tf_op jit(solution)/shard_map/weights/pallas_call | solution.py:220
  12.6 3.5 %all-to-all-start = ((bf16[4,128,1152]{2,1,0:T(8,128)(2,1)}), bf16[4,128,1152]{2,1,0:T(8,128)(2,1)S(1)}, u32[]{:S(2)}, u32[]{:S(2)}) async-start(bf16[4,128,1152]{2,1,0:T(8,128)(2,1)} %weights.1), calls=%async_computation | async-start | bytes 2359296 | tf_op jit(solution)/shard_map/all_to_all | solution.py:262
  16.2 1.7 %collective-permute-start.5 = (bf16[576,128]{1,0:T(8,128)(2,1)S(1)}, bf16[576,128]{1,0:T(8,128)(2,1)S(1)}, u32[]{:S(2)}, u32[]{:S(2)}) collective-permute-start(bf16[576,128]{1,0:T(8,128)(2,1)S(1)} %pad_maximum_fusion.refs_0_), channel_id=1, source_target_pairs={{0,3},{1,2},{2,1},{3,0},{4,7},{5,6},{6,5},{7,4},{8,11},{9,10},{10,... | collective-permute-start | bytes 442376 | tf_op jit(solution)/shard_map/ppermute | solution.py:257
  17.9 5.2 %collective-permute-start.4 = (bf16[576,128]{1,0:T(8,128)(2,1)S(1)}, bf16[576,128]{1,0:T(8,128)(2,1)S(1)}, u32[]{:S(2)}, u32[]{:S(2)}) collective-permute-start(bf16[576,128]{1,0:T(8,128)(2,1)S(1)} %pad_maximum_fusion.1), channel_id=1, source_target_pairs={{0,32},{1,33},{2,34},{3,35},{32,0},{33,1},{34,2},{35,3},{4,36},{5,... | collective-permute-start | bytes 442376 | tf_op jit(solution)/shard_map/ppermute | solution.py:254
  23.1 1.6 %collective-permute-start.10 = (bf16[576,128]{1,0:T(8,128)(2,1)S(1)}, bf16[576,128]{1,0:T(8,128)(2,1)S(1)}, u32[]{:S(2)}, u32[]{:S(2)}) collective-permute-start(bf16[576,128]{1,0:T(8,128)(2,1)S(1)} %pad_maximum_fusion.refs_0_), channel_id=1, source_target_pairs={{0,1},{1,0},{2,3},{3,2},{4,5},{5,4},{6,7},{7,6},{8,9},{9,8},{10,11... | collective-permute-start | bytes 442376 | tf_op jit(solution)/shard_map/ppermute | solution.py:257
  24.8 0.4 collective-permute-start.7
  25.2 1.0 %collective-permute-start.9 = (bf16[576,128]{1,0:T(8,128)(2,1)S(1)}, bf16[576,128]{1,0:T(8,128)(2,1)S(1)}, u32[]{:S(2)}, u32[]{:S(2)}) collective-permute-start(bf16[576,128]{1,0:T(8,128)(2,1)S(1)} %pad_maximum_fusion.1), channel_id=1, source_target_pairs={{0,34},{1,35},{2,32},{3,33},{32,2},{33,3},{34,0},{35,1},{4,38},{5,... | collective-permute-start | bytes 442376 | tf_op jit(solution)/shard_map/ppermute | solution.py:254
  26.2 5.9 %collective-permute-start.8 = (bf16[576,128]{1,0:T(8,128)(2,1)S(1)}, bf16[576,128]{1,0:T(8,128)(2,1)S(1)}, u32[]{:S(2)}, u32[]{:S(2)}) collective-permute-start(bf16[576,128]{1,0:T(8,128)(2,1)S(1)} %pad_maximum_fusion.1), channel_id=1, source_target_pairs={{0,35},{1,34},{2,33},{3,32},{32,3},{33,2},{34,1},{35,0},{4,39},{5,... | collective-permute-start | bytes 442376 | tf_op jit(solution)/shard_map/ppermute | solution.py:254
  32.2 0.8 %collective-permute-start.6 = (bf16[576,128]{1,0:T(8,128)(2,1)S(1)}, bf16[576,128]{1,0:T(8,128)(2,1)S(1)}, u32[]{:S(2)}, u32[]{:S(2)}) collective-permute-start(bf16[576,128]{1,0:T(8,128)(2,1)S(1)} %pad_maximum_fusion.1), channel_id=1, source_target_pairs={{0,33},{1,32},{2,35},{3,34},{32,1},{33,0},{34,3},{35,2},{4,37},{5,... | collective-permute-start | bytes 442376 | tf_op jit(solution)/shard_map/ppermute | solution.py:254
  33.0 0.5 expand.3
  33.5 0.9 %add.2 = bf16[32,4,1152]{2,1,0:T(4,128)(2,1)} custom-call(bf16[4,128,1152]{2,1,0:T(8,128)(2,1)S(1)} %all-to-all-done.in_ref), custom_call_target="tpu_custom_call" | custom-call | flops 1000 | bytes 1000 | tf_op jit(solution)/shard_map/add/pallas_call | solution.py:220
  34.3 8.8 %all-to-all-start.1 = ((bf16[32,4,1152]{2,1,0:T(4,128)(2,1)}), bf16[32,4,1152]{2,1,0:T(4,128)(2,1)S(1)}, u32[]{:S(2)}, u32[]{:S(2)}) async-start(bf16[32,4,1152]{2,1,0:T(4,128)(2,1)} %add.2), calls=%async_computation.1 | async-start | bytes 589824 | tf_op jit(solution)/shard_map/all_to_all | solution.py:262
  43.1 0.4 expand.5
  43.5 4.2 %collective-permute-done.8.refs_2_ = bf16[576,128]{1,0:T(8,128)(2,1)S(1)} collective-permute-done((bf16[576,128]{1,0:T(8,128)(2,1)S(1)}, bf16[576,128]{1,0:T(8,128)(2,1)S(1)}, u32[]{:S(2)}, u32[]{:S(2)}) %collective-permute-start.8) | collective-permute-done | bytes 147488 | tf_op jit(solution)/shard_map/ppermute | solution.py:254
  47.8 6.0 %collective-permute-done.6.refs_0_ = bf16[576,128]{1,0:T(8,128)(2,1)S(1)} collective-permute-done((bf16[576,128]{1,0:T(8,128)(2,1)S(1)}, bf16[576,128]{1,0:T(8,128)(2,1)S(1)}, u32[]{:S(2)}, u32[]{:S(2)}) %collective-permute-start.6) | collective-permute-done | bytes 147488 | tf_op jit(solution)/shard_map/ppermute | solution.py:254
  53.8 0.5 expand.4
  54.2 0.7 scatter.6
  54.9 2.8 %collective-permute-start.11 = (bf16[1024,128]{1,0:T(8,128)(2,1)S(1)}, bf16[1024,128]{1,0:T(8,128)(2,1)S(1)}, u32[]{:S(2)}, u32[]{:S(2)}) collective-permute-start(bf16[1024,128]{1,0:T(8,128)(2,1)S(1)} %scatter.6), channel_id=1, source_target_pairs={{0,4},{4,0},{1,5},{5,1},{2,6},{6,2},{3,7},{7,3},{8,12},{12,8},{9,1... | collective-permute-start | bytes 786440 | tf_op jit(solution)/shard_map/ppermute | solution.py:289
  57.7 1.2 %scatter.7 = (bf16[1024,128]{1,0:T(8,128)(2,1)S(1)}, bf16[1024,128]{1,0:T(8,128)(2,1)S(1)}) custom-call(bf16[4,3,128,128]{3,2,1,0:T(8,128)(2,1)S(1)} %get-tuple-element.122.refs_0_, bf16[4,3,128,128]{3,2,1,0:T(8,128)(2,1)S(1)} %get-tuple-element.123.refs_1_, bf16[4,2,128,128]{3,2,1,0:T(8,128)(2,1)S(1)} %get-tuple-element.124.refs_2_, ...), custom_call_target="tpu_custom_call" | custom-call | flops 1000 | bytes 1000 | tf_op jit(solution)/shard_map/scatter/pallas_call | solution.py:220
  59.0 0.1 collective-permute-start.12
  59.1 0.5 collective-permute-start.13
  59.6 0.7 scatter.8
  60.3 0.2 collective-permute-start.14
  60.5 0.7 scatter.9
  61.2 1.8 %collective-permute-start.17 = (bf16[1024,128]{1,0:T(8,128)(2,1)S(1)}, bf16[1024,128]{1,0:T(8,128)(2,1)S(1)}, u32[]{:S(2)}, u32[]{:S(2)}) collective-permute-start(bf16[1024,128]{1,0:T(8,128)(2,1)S(1)} %scatter.9), channel_id=1, source_target_pairs={{0,16},{8,24},{16,0},{24,8},{1,17},{9,25},{17,1},{25,9},{2,18},{10... | collective-permute-start | bytes 786440 | tf_op jit(solution)/shard_map/ppermute | solution.py:302
  63.0 1.2 %scatter.10 = (bf16[1024,128]{1,0:T(8,128)(2,1)S(1)}, bf16[1024,128]{1,0:T(8,128)(2,1)S(1)}) custom-call(bf16[4,3,128,128]{3,2,1,0:T(8,128)(2,1)S(1)} %get-tuple-element.145.refs_0_, bf16[4,3,128,128]{3,2,1,0:T(8,128)(2,1)S(1)} %get-tuple-element.146.refs_1_, bf16[4,2,128,128]{3,2,1,0:T(8,128)(2,1)S(1)} %get-tuple-element.147.refs_2_, ...), custom_call_target="tpu_custom_call" | custom-call | flops 1000 | bytes 1000 | tf_op jit(solution)/shard_map/scatter/pallas_call | solution.py:220
  64.3 0.0 copy-start.3
  64.3 0.0 copy-start.6
  64.3 0.1 collective-permute-start.15
  64.4 1.5 %collective-permute-start.16 = (bf16[1024,128]{1,0:T(8,128)(2,1)S(1)}, bf16[1024,128]{1,0:T(8,128)(2,1)S(1)}, u32[]{:S(2)}, u32[]{:S(2)}) collective-permute-start(bf16[1024,128]{1,0:T(8,128)(2,1)S(1)} %get-tuple-element.153), channel_id=1, source_target_pairs={{0,24},{8,0},{16,8},{24,16},{1,25},{9,1},{17,9},{25,17},{2,26},{10... | collective-permute-start | bytes 786440 | tf_op jit(solution)/shard_map/ppermute | solution.py:306
  65.8 0.7 scatter.11.a_ref
  66.5 3.8 %collective-permute-done.17.d_ref = bf16[1024,128]{1,0:T(8,128)(2,1)S(1)} collective-permute-done((bf16[1024,128]{1,0:T(8,128)(2,1)S(1)}, bf16[1024,128]{1,0:T(8,128)(2,1)S(1)}, u32[]{:S(2)}, u32[]{:S(2)}) %collective-permute-start.17) | collective-permute-done | bytes 262176 | tf_op jit(solution)/shard_map/ppermute | solution.py:302
  70.3 5.6 %collective-permute-done.15.b_ref = bf16[1024,128]{1,0:T(8,128)(2,1)S(1)} collective-permute-done((bf16[1024,128]{1,0:T(8,128)(2,1)S(1)}, bf16[1024,128]{1,0:T(8,128)(2,1)S(1)}, u32[]{:S(2)}, u32[]{:S(2)}) %collective-permute-start.15) | collective-permute-done | bytes 262176 | tf_op jit(solution)/shard_map/ppermute | solution.py:305
  75.8 0.8 collective-permute-done.16.c_ref
  76.6 1.3 %update.1 = (f32[1024,128]{1,0:T(8,128)}, f32[8,128]{1,0:T(8,128)}) custom-call(bf16[1024,128]{1,0:T(8,128)(2,1)S(1)} %scatter.11.a_ref, bf16[1024,128]{1,0:T(8,128)(2,1)S(1)} %collective-permute-done.15.b_ref, bf16[1024,128]{1,0:T(8,128)(2,1)S(1)} %collective-permute-done.16.c_ref, bf16[1024,128]{1,0:T(8,128)(2,1)S(1)} %collective-permute-done.17.d_ref, ...), custom_call_target="tpu_custom_call" | custom-call | flops 1000 | bytes 1000 | tf_op jit(solution)/shard_map/update/pallas_call | solution.py:220
  77.9 0.7 add.3
  (29 shorter events, 0.1 us)
Async XLA Ops:
  0.6 0.8 copy-start.7
  1.4 1.5 %copy-start = (bf16[1152,512]{1,0:T(8,128)(2,1)S(1)}, bf16[1152,512]{1,0:T(8,128)(2,1)}, u32[]{:S(2)}) copy-start(bf16[1152,512]{1,0:T(8,128)(2,1)} %down_ref.1) | copy-start | bytes 3538948
  1.4 1.6 %copy-start.1 = (bf16[512,1152]{1,0:T(8,128)(2,1)S(1)}, bf16[512,1152]{1,0:T(8,128)(2,1)}, u32[]{:S(2)}) copy-start(bf16[512,1152]{1,0:T(8,128)(2,1)} %up_ref.1) | copy-start | bytes 3538948
  1.4 1.7 %copy-start.2 = (bf16[128,1152]{1,0:T(8,128)(2,1)S(1)}, bf16[128,1152]{1,0:T(8,128)(2,1)}, u32[]{:S(2)}) copy-start(bf16[128,1152]{1,0:T(8,128)(2,1)} %cot_ref.1) | copy-start | bytes 884740
  1.4 1.8 %copy-start.4 = (bf16[128,1152]{1,0:T(8,128)(2,1)S(1)}, bf16[128,1152]{1,0:T(8,128)(2,1)}, u32[]{:S(2)}) copy-start(bf16[128,1152]{1,0:T(8,128)(2,1)} %in_ref) | copy-start | bytes 884740
  3.2 1.9 %copy-start.5 = (f32[1152]{0:T(1024)S(1)}, f32[1152]{0:T(1024)}, u32[]{:S(2)}) copy-start(f32[1152]{0:T(1024)} %param.12) | copy-start | bytes 13828
  4.3 6.1 %collective-permute-start.3 = (bf16[128,2816]{1,0:T(8,128)(2,1)S(1)}, bf16[128,2816]{1,0:T(8,128)(2,1)S(1)}, u32[]{:S(2)}, u32[]{:S(2)}) collective-permute-start(bf16[128,2816]{1,0:T(8,128)(2,1)S(1)} %get-tuple-element.88.pack_ref), channel_id=1, source_target_pairs={{0,4},{4,0},{1,5},{5,1},{2,6},{6,2},{3,7},{7,3},{8,12},{12,8},{9,1... | collective-permute-start | bytes 2162696 | tf_op jit(solution)/shard_map/ppermute | solution.py:244
  6.2 9.9 %collective-permute-start.2 = (bf16[2,144,128]{2,1,0:T(8,128)(2,1)S(1)}, bf16[2,144,128]{2,1,0:T(8,128)(2,1)S(1)}, u32[]{:S(2)}, u32[]{:S(2)}) collective-permute-start(bf16[2,144,128]{2,1,0:T(8,128)(2,1)S(1)} %get-tuple-element.158), channel_id=1, source_target_pairs={{0,192},{64,0},{128,64},{192,128},{1,193},{65,1},{129,65},{193,129... | collective-permute-start | bytes 221192 | tf_op jit(solution)/shard_map/ppermute | solution.py:245
  6.5 9.6 %collective-permute-start.1 = (bf16[2,144,128]{2,1,0:T(8,128)(2,1)S(1)}, bf16[2,144,128]{2,1,0:T(8,128)(2,1)S(1)}, u32[]{:S(2)}, u32[]{:S(2)}) collective-permute-start(bf16[2,144,128]{2,1,0:T(8,128)(2,1)S(1)} %get-tuple-element.159), channel_id=1, source_target_pairs={{0,128},{64,192},{128,0},{192,64},{1,129},{65,193},{129,1},{193,65... | collective-permute-start | bytes 221192 | tf_op jit(solution)/shard_map/ppermute | solution.py:245
  8.8 7.3 %collective-permute-start = (bf16[2,144,128]{2,1,0:T(8,128)(2,1)S(1)}, bf16[2,144,128]{2,1,0:T(8,128)(2,1)S(1)}, u32[]{:S(2)}, u32[]{:S(2)}) collective-permute-start(bf16[2,144,128]{2,1,0:T(8,128)(2,1)S(1)} %get-tuple-element.160), channel_id=1, source_target_pairs={{0,64},{64,128},{128,192},{192,0},{1,65},{65,129},{129,193},{193,1... | collective-permute-start | bytes 221192 | tf_op jit(solution)/shard_map/ppermute | solution.py:245
  12.6 20.9 %all-to-all-start = ((bf16[4,128,1152]{2,1,0:T(8,128)(2,1)}), bf16[4,128,1152]{2,1,0:T(8,128)(2,1)S(1)}, u32[]{:S(2)}, u32[]{:S(2)}) async-start(bf16[4,128,1152]{2,1,0:T(8,128)(2,1)} %weights.1), calls=%async_computation | async-start | bytes 2359296 | tf_op jit(solution)/shard_map/all_to_all | solution.py:262
  16.2 10.0 %collective-permute-start.5 = (bf16[576,128]{1,0:T(8,128)(2,1)S(1)}, bf16[576,128]{1,0:T(8,128)(2,1)S(1)}, u32[]{:S(2)}, u32[]{:S(2)}) collective-permute-start(bf16[576,128]{1,0:T(8,128)(2,1)S(1)} %pad_maximum_fusion.refs_0_), channel_id=1, source_target_pairs={{0,3},{1,2},{2,1},{3,0},{4,7},{5,6},{6,5},{7,4},{8,11},{9,10},{10,... | collective-permute-start | bytes 442376 | tf_op jit(solution)/shard_map/ppermute | solution.py:257
  17.9 14.2 %collective-permute-start.4 = (bf16[576,128]{1,0:T(8,128)(2,1)S(1)}, bf16[576,128]{1,0:T(8,128)(2,1)S(1)}, u32[]{:S(2)}, u32[]{:S(2)}) collective-permute-start(bf16[576,128]{1,0:T(8,128)(2,1)S(1)} %pad_maximum_fusion.1), channel_id=1, source_target_pairs={{0,32},{1,33},{2,34},{3,35},{32,0},{33,1},{34,2},{35,3},{4,36},{5,... | collective-permute-start | bytes 442376 | tf_op jit(solution)/shard_map/ppermute | solution.py:254
  23.1 20.0 %collective-permute-start.10 = (bf16[576,128]{1,0:T(8,128)(2,1)S(1)}, bf16[576,128]{1,0:T(8,128)(2,1)S(1)}, u32[]{:S(2)}, u32[]{:S(2)}) collective-permute-start(bf16[576,128]{1,0:T(8,128)(2,1)S(1)} %pad_maximum_fusion.refs_0_), channel_id=1, source_target_pairs={{0,1},{1,0},{2,3},{3,2},{4,5},{5,4},{6,7},{7,6},{8,9},{9,8},{10,11... | collective-permute-start | bytes 442376 | tf_op jit(solution)/shard_map/ppermute | solution.py:257
  24.8 18.7 %collective-permute-start.7 = (bf16[576,128]{1,0:T(8,128)(2,1)S(1)}, bf16[576,128]{1,0:T(8,128)(2,1)S(1)}, u32[]{:S(2)}, u32[]{:S(2)}) collective-permute-start(bf16[576,128]{1,0:T(8,128)(2,1)S(1)} %pad_maximum_fusion.refs_0_), channel_id=1, source_target_pairs={{0,2},{1,3},{2,0},{3,1},{4,6},{5,7},{6,4},{7,5},{8,10},{9,11},{10,... | collective-permute-start | bytes 442376 | tf_op jit(solution)/shard_map/ppermute | solution.py:257
  25.2 17.9 %collective-permute-start.9 = (bf16[576,128]{1,0:T(8,128)(2,1)S(1)}, bf16[576,128]{1,0:T(8,128)(2,1)S(1)}, u32[]{:S(2)}, u32[]{:S(2)}) collective-permute-start(bf16[576,128]{1,0:T(8,128)(2,1)S(1)} %pad_maximum_fusion.1), channel_id=1, source_target_pairs={{0,34},{1,35},{2,32},{3,33},{32,2},{33,3},{34,0},{35,1},{4,38},{5,... | collective-permute-start | bytes 442376 | tf_op jit(solution)/shard_map/ppermute | solution.py:254
  26.2 21.5 %collective-permute-start.8 = (bf16[576,128]{1,0:T(8,128)(2,1)S(1)}, bf16[576,128]{1,0:T(8,128)(2,1)S(1)}, u32[]{:S(2)}, u32[]{:S(2)}) collective-permute-start(bf16[576,128]{1,0:T(8,128)(2,1)S(1)} %pad_maximum_fusion.1), channel_id=1, source_target_pairs={{0,35},{1,34},{2,33},{3,32},{32,3},{33,2},{34,1},{35,0},{4,39},{5,... | collective-permute-start | bytes 442376 | tf_op jit(solution)/shard_map/ppermute | solution.py:254
  32.2 21.6 %collective-permute-start.6 = (bf16[576,128]{1,0:T(8,128)(2,1)S(1)}, bf16[576,128]{1,0:T(8,128)(2,1)S(1)}, u32[]{:S(2)}, u32[]{:S(2)}) collective-permute-start(bf16[576,128]{1,0:T(8,128)(2,1)S(1)} %pad_maximum_fusion.1), channel_id=1, source_target_pairs={{0,33},{1,32},{2,35},{3,34},{32,1},{33,0},{34,3},{35,2},{4,37},{5,... | collective-permute-start | bytes 442376 | tf_op jit(solution)/shard_map/ppermute | solution.py:254
  34.3 43.6 %all-to-all-start.1 = ((bf16[32,4,1152]{2,1,0:T(4,128)(2,1)}), bf16[32,4,1152]{2,1,0:T(4,128)(2,1)S(1)}, u32[]{:S(2)}, u32[]{:S(2)}) async-start(bf16[32,4,1152]{2,1,0:T(4,128)(2,1)} %add.2), calls=%async_computation.1 | async-start | bytes 589824 | tf_op jit(solution)/shard_map/all_to_all | solution.py:262
  54.9 5.5 %collective-permute-start.11 = (bf16[1024,128]{1,0:T(8,128)(2,1)S(1)}, bf16[1024,128]{1,0:T(8,128)(2,1)S(1)}, u32[]{:S(2)}, u32[]{:S(2)}) collective-permute-start(bf16[1024,128]{1,0:T(8,128)(2,1)S(1)} %scatter.6), channel_id=1, source_target_pairs={{0,4},{4,0},{1,5},{5,1},{2,6},{6,2},{3,7},{7,3},{8,12},{12,8},{9,1... | collective-permute-start | bytes 786440 | tf_op jit(solution)/shard_map/ppermute | solution.py:289
  59.0 4.0 %collective-permute-start.12 = (bf16[1024,128]{1,0:T(8,128)(2,1)S(1)}, bf16[1024,128]{1,0:T(8,128)(2,1)S(1)}, u32[]{:S(2)}, u32[]{:S(2)}) collective-permute-start(bf16[1024,128]{1,0:T(8,128)(2,1)S(1)} %get-tuple-element.141), channel_id=1, source_target_pairs={{0,4},{4,0},{1,5},{5,1},{2,6},{6,2},{3,7},{7,3},{8,12},{12,8},{9,1... | collective-permute-start | bytes 786440 | tf_op jit(solution)/shard_map/ppermute | solution.py:289
  59.1 3.9 %collective-permute-start.13 = (bf16[1024,128]{1,0:T(8,128)(2,1)S(1)}, bf16[1024,128]{1,0:T(8,128)(2,1)S(1)}, u32[]{:S(2)}, u32[]{:S(2)}) collective-permute-start(bf16[1024,128]{1,0:T(8,128)(2,1)S(1)} %get-tuple-element.142), channel_id=1, source_target_pairs={{0,4},{4,0},{1,5},{5,1},{2,6},{6,2},{3,7},{7,3},{8,12},{12,8},{9,1... | collective-permute-start | bytes 786440 | tf_op jit(solution)/shard_map/ppermute | solution.py:289
  60.3 5.5 %collective-permute-start.14 = (bf16[1024,128]{1,0:T(8,128)(2,1)S(1)}, bf16[1024,128]{1,0:T(8,128)(2,1)S(1)}, u32[]{:S(2)}, u32[]{:S(2)}) collective-permute-start(bf16[1024,128]{1,0:T(8,128)(2,1)S(1)} %scatter.8), channel_id=1, source_target_pairs={{0,4},{4,0},{1,5},{5,1},{2,6},{6,2},{3,7},{7,3},{8,12},{12,8},{9,1... | collective-permute-start | bytes 786440 | tf_op jit(solution)/shard_map/ppermute | solution.py:289
  61.2 9.1 %collective-permute-start.17 = (bf16[1024,128]{1,0:T(8,128)(2,1)S(1)}, bf16[1024,128]{1,0:T(8,128)(2,1)S(1)}, u32[]{:S(2)}, u32[]{:S(2)}) collective-permute-start(bf16[1024,128]{1,0:T(8,128)(2,1)S(1)} %scatter.9), channel_id=1, source_target_pairs={{0,16},{8,24},{16,0},{24,8},{1,17},{9,25},{17,1},{25,9},{2,18},{10... | collective-permute-start | bytes 786440 | tf_op jit(solution)/shard_map/ppermute | solution.py:302
  64.3 12.4 %copy-start.3 = (f32[1024,128]{1,0:T(8,128)S(1)}, f32[1024,128]{1,0:T(8,128)}, u32[]{:S(2)}) copy-start(f32[1024,128]{1,0:T(8,128)} %table_ref.1) | copy-start | bytes 1572868
  64.3 12.3 %copy-start.6 = (f32[1024]{0:T(1024)S(1)}, f32[1024]{0:T(1024)}, u32[]{:S(2)}) copy-start(f32[1024]{0:T(1024)} %param.15) | copy-start | bytes 12292
  64.3 11.6 %collective-permute-start.15 = (bf16[1024,128]{1,0:T(8,128)(2,1)S(1)}, bf16[1024,128]{1,0:T(8,128)(2,1)S(1)}, u32[]{:S(2)}, u32[]{:S(2)}) collective-permute-start(bf16[1024,128]{1,0:T(8,128)(2,1)S(1)} %get-tuple-element.152), channel_id=1, source_target_pairs={{0,8},{8,16},{16,24},{24,0},{1,9},{9,17},{17,25},{25,1},{2,10},{10... | collective-permute-start | bytes 786440 | tf_op jit(solution)/shard_map/ppermute | solution.py:305
  64.4 12.2 %collective-permute-start.16 = (bf16[1024,128]{1,0:T(8,128)(2,1)S(1)}, bf16[1024,128]{1,0:T(8,128)(2,1)S(1)}, u32[]{:S(2)}, u32[]{:S(2)}) collective-permute-start(bf16[1024,128]{1,0:T(8,128)(2,1)S(1)} %get-tuple-element.153), channel_id=1, source_target_pairs={{0,24},{8,0},{16,8},{24,16},{1,25},{9,1},{17,9},{25,17},{2,26},{10... | collective-permute-start | bytes 786440 | tf_op jit(solution)/shard_map/ppermute | solution.py:306

commit v4 on v3

--- a/solution.py
+++ b/solution.py
@@ -163,7 +163,7 @@
             row_ref[d, j] = row
 
 
-def scatter(d, looks, rows, out_ref, first=None):
+def scatter(d, looks, rows, out_ref, firsts=()):
     base = iota((256, 128), 0).astype(F32)
     look = jnp.concatenate([ref[d].reshape(-1, EMB) for ref in looks], axis=0)
     for i in range(ROWS // 256):
@@ -171,9 +171,9 @@
         s = slice(i * 256, (i + 1) * 256)
         hot = jnp.concatenate([(here == ref[d, j, 0:1, :]).astype(BF16) for ref in rows for j in range(ref.shape[1])], axis=1)
         total = dot(hot, look, 1, 0)
-        if first is not None:
+        for first in firsts:
             total = total + first[s].astype(F32)
-        out_ref[s] = total.astype(BF16)
+        out_ref[s] = total.astype(out_ref.dtype)
 
 
 def expand_kernel(count, *refs):
@@ -183,12 +183,12 @@
     expand(place, refs[:count], look_own, row_own)
 
 
-def scatter_kernel(ds, parts, *refs):
-    looks, rows, rest = refs[:parts], refs[parts:2 * parts], refs[2 * parts:]
+def scatter_kernel(ds, *refs):
+    look, row, rest = refs[0], refs[1], refs[2:]
     count = len(ds)
     firsts, outs = rest[:-count], rest[-count:]
     for i, d in enumerate(ds):
-        scatter(d, looks, rows, outs[i], firsts[i] if firsts else None)
+        scatter(d, (look,), (row,), outs[i], firsts[i::count])
 
 
 def update_kernel(a_ref, b_ref, c_ref, d_ref, table_ref, accum_ref, table_out, accum_out):
@@ -256,7 +256,12 @@
     def line(m):
         return lax.ppermute(near, "zl", [(i, i ^ m) for i in range(NZL)])
 
-    blocks = [near, cross(3), line(3), cross(2), line(2), cross(0), cross(1), line(1)]
+    def pass_on(v):
+        return lax.ppermute(v, "zl", [(i, i ^ 1) for i in range(NZL)])
+
+    sent_on = [cross(2), cross(0), line(2)]
+    blocks = [near] + sent_on + [line(1)]
+    passed = [pass_on(v) for v in sent_on]
 
     def exchanged(v, axes):
         return lax.all_to_all(v, axes, split_axis=0, concat_axis=0, tiled=True)
@@ -271,40 +276,40 @@
             functools.partial(expand_kernel, len(blocks)), "expand", (look, row, look, row), tuple(blocks), 16, cost(1_000, 1_000)
         )
 
-    lists = [expanded(blocks[:3])]
-    lists[0], terms = lax.optimization_barrier((lists[0], exchanged(terms, "y")))
-    terms = added(terms, (32, 4, FEATURES), BF16)
-    late, _ = lax.optimization_barrier((blocks[3:6], terms))
-    weight_total = added(exchanged(terms, ("zh", "zl", "x")), (4, FEATURES), F32)
-    lists += [expanded(late), expanded(blocks[6:])]
-    own, other = [[v[i] for v in lists] + [v[i + 1] for v in lists] for i in (0, 2)]
-
-    def scattered(arrays, ds, firsts=()):
+    def scattered(arrays, ds, firsts=(), kind=BF16):
         return call(
-            functools.partial(scatter_kernel, ds, len(lists)), "scatter",
-            (shape((ROWS, EMB), BF16),) * len(ds), (*arrays, *firsts), 24, cost(1_000, 1_000),
+            functools.partial(scatter_kernel, ds), "scatter",
+            (shape((ROWS, EMB), kind),) * len(ds), (*arrays, *firsts), 24, cost(1_000, 1_000),
         )
 
     def swapped(vs):
         return [lax.ppermute(v, "c", swap) for v in vs]
 
-    first = scattered(other, (2,))
+    early = expanded(blocks)
+    early, terms = lax.optimization_barrier((early, exchanged(terms, "y")))
+    terms = added(terms, (32, 4, FEATURES), BF16)
+    weight_total = added(exchanged(terms, ("zh", "zl", "x")), (4, FEATURES), F32)
+    order = (2, 1, 3, 0)
+    base_own = scattered(early[:2], order, kind=F32)
+    base_other = scattered(early[2:], order, kind=F32)
+    late, base_own, base_other, _ = lax.optimization_barrier((passed, base_own, base_other, terms))
+    late = expanded(late)
+    own, other = late[:2], late[2:]
+
+    first = scattered(other, (2,), base_other[:1])
     other, first = lax.optimization_barrier((other, first))
     (first,) = swapped(first)
-    second = scattered(other, (1, 3))
-    other, second = lax.optimization_barrier((other, second))
-    second = swapped(second)
-    last = scattered(other, (0,))
-    own, last = lax.optimization_barrier((own, last))
-    (last,) = swapped(last)
-    apart = scattered(own, (2,), (first,))
+    rest = scattered(other, (1, 3, 0), base_other[1:])
+    own, rest = lax.optimization_barrier((own, rest))
+    rest = swapped(rest)
+    apart = scattered(own, (2,), (base_own[0], first))
     own, apart = lax.optimization_barrier((own, apart))
     apart = lax.ppermute(apart[0], "x", ring(NX, 2))
-    right, left = scattered(own, (1, 3), second)
+    right, left = scattered(own, (1, 3), (*base_own[1:3], *rest[:2]))
     own, right, left = lax.optimization_barrier((own, right, left))
     right = lax.ppermute(right, "x", ring(NX, 1))
     left = lax.ppermute(left, "x", ring(NX, 3))
-    (here,) = scattered(own, (0,), (last,))
+    (here,) = scattered(own, (0,), (base_own[3], rest[2]))
 
     table_new, accum_new = call(
         update_kernel, "update", (shape((ROWS, EMB), F32), shape((8, 128), F32)),

time: 78.9 us -> 76.1 us (0.965)
  the two profiles are of different devices: /device:TPU:43 before, /device:TPU:1 now
where the time goes in v4:
time: 76.1 us; the launch traced here: 75.8 us
  starting transfers between devices  37.4 us (49%)
  waiting for transfers between devices  21.1 us (28%)
  Pallas kernels  15.4 us (20%)
  local copies, waits for them, and re-layouts  1.04 us (1%)
  between operations  0.83 us (1%)
    pallas_call x16, Pallas kernels, call(): pl.pallas_call(kernel, out_shape=outs, in_specs=[VMEM] * len(operands), o...  15.4 us
    all_to_all x2, starting transfers between devices, exchanged(): return lax.all_to_all(v, axes, split_axis=0, concat_axis=0, tiled=True)  12.4 us
    ppermute x2, waiting for transfers between devices, cross(): return lax.ppermute(far, ('zh', 'zl'), [(i, 7 - i ^ m) for i in range(8)])  9.14 us
    ppermute x1, waiting for transfers between devices, per_device(): apart = lax.ppermute(apart[0], 'x', ring(NX, 2))  6.68 us
    ppermute x2, starting transfers between devices, cross(): return lax.ppermute(far, ('zh', 'zl'), [(i, 7 - i ^ m) for i in range(8)])  6.38 us
    ppermute x1, waiting for transfers between devices, per_device(): right = lax.ppermute(right, 'x', ring(NX, 1))  4.3 us
    ppermute x4, starting transfers between devices, swapped(): return [lax.ppermute(v, 'c', swap) for v in vs]  3.93 us
    ppermute x1, starting transfers between devices, per_device(): other_pack = lax.ppermute(pack, 'c', swap)  3.33 us
  transfers between devices with their start and end apart: 20, of which 6 were waited for; matrix products, arithmetic and copies ran while one was open for 0% of the time, Pallas kernels for 16%

profile of v4, /device:TPU:1, one launch (start us, length us, event | category | flops | bytes accessed | tf_op | source)
XLA Modules:
  0.0 75.8 jit_solution(2291684035152478751)
XLA Ops:
  0.6 0.7 copy-done.7
  1.4 1.5 %rank.1.meta_ref = bf16[8,16,128]{2,1,0:T(8,128)(2,1)S(1)} custom-call(s32[64,128]{1,0:T(8,128)S(1)} %bitcast.32), custom_call_target="tpu_custom_call" | custom-call | flops 2000000000 | bytes 100000 | tf_op jit(solution)/shard_map/rank/pallas_call | solution.py:220
  2.9 0.1 copy-done.1
  3.0 0.0 copy-done.2
  3.1 0.1 copy-done.4
  3.2 1.1 %hidden.1 = (bf16[128,2816]{1,0:T(8,128)(2,1)S(1)}, bf16[128,512]{1,0:T(8,128)(2,1)S(1)}, bf16[128,1024]{1,0:T(8,128)(2,1)S(1)}) custom-call(bf16[128,1152]{1,0:T(8,128)(2,1)S(1)} %copy-done.4, bf16[128,1152]{1,0:T(8,128)(2,1)S(1)} %copy-done.2, bf16[1152,512]{1,0:T(8,128)(2,1)S(1)} %copy-done, bf16[512,1152]{1,0:T(8,128)(2,1)S(1)} %copy-done.1), custom_call_target="tpu_custom_call" | custom-call | flops 500000000 | bytes 4000000 | tf_op jit(solution)/shard_map/hidden/pallas_call | solution.py:220
  4.3 3.3 %collective-permute-start.3 = (bf16[128,2816]{1,0:T(8,128)(2,1)S(1)}, bf16[128,2816]{1,0:T(8,128)(2,1)S(1)}, u32[]{:S(2)}, u32[]{:S(2)}) collective-permute-start(bf16[128,2816]{1,0:T(8,128)(2,1)S(1)} %get-tuple-element.79.pack_ref), channel_id=1, source_target_pairs={{0,4},{4,0},{1,5},{5,1},{2,6},{6,2},{3,7},{7,3},{8,12},{12,8},{9,1... | collective-permute-start | bytes 2162696 | tf_op jit(solution)/shard_map/ppermute | solution.py:244
  7.6 1.2 %pooled.1 = (bf16[128,128]{1,0:T(8,128)(2,1)}, bf16[4,2,144,128]{3,2,1,0:T(8,128)(2,1)S(1)}) custom-call(bf16[128,1152]{1,0:T(8,128)(2,1)S(1)} %copy-done.2, bf16[128,1024]{1,0:T(8,128)(2,1)S(1)} %get-tuple-element.76.both_ref, bf16[1152,512]{1,0:T(8,128)(2,1)S(1)} %copy-done, bf16[512,1152]{1,0:T(8,128)(2,1)S(1)} %copy-done.1, f32[9,128]{1,0:T(8,128)S(1)} %bitcast.30, ...), custom_call_target="tpu_custom_call" | custom-call | flops 300000000 | bytes 4000000 | tf_op jit(solution)/shard_map/pooled/pallas_call | solution.py:220
  8.8 1.1 %collective-permute-start.2 = (bf16[2,144,128]{2,1,0:T(8,128)(2,1)S(1)}, bf16[2,144,128]{2,1,0:T(8,128)(2,1)S(1)}, u32[]{:S(2)}, u32[]{:S(2)}) collective-permute-start(bf16[2,144,128]{2,1,0:T(8,128)(2,1)S(1)} %get-tuple-element.140), channel_id=1, source_target_pairs={{0,192},{64,0},{128,64},{192,128},{1,193},{65,1},{129,65},{193,129... | collective-permute-start | bytes 221192 | tf_op jit(solution)/shard_map/ppermute | solution.py:245
  9.9 0.4 collective-permute-start.1
  10.2 0.7 collective-permute-start
  10.9 0.0 collective-permute-done.3.other_ref
  10.9 2.2 %weights.1 = bf16[4,128,1152]{2,1,0:T(8,128)(2,1)} custom-call(bf16[128,2816]{1,0:T(8,128)(2,1)S(1)} %get-tuple-element.79.pack_ref, bf16[128,512]{1,0:T(8,128)(2,1)S(1)} %get-tuple-element.80.cols_ref, bf16[128,2816]{1,0:T(8,128)(2,1)S(1)} %collective-permute-done.3.other_ref), custom_call_target="tpu_custom_call" | custom-call | flops 300000000 | bytes 3000000 | tf_op jit(solution)/shard_map/weights/pallas_call | solution.py:220
  13.1 4.3 %all-to-all-start = ((bf16[4,128,1152]{2,1,0:T(8,128)(2,1)}), bf16[4,128,1152]{2,1,0:T(8,128)(2,1)S(1)}, u32[]{:S(2)}, u32[]{:S(2)}) async-start(bf16[4,128,1152]{2,1,0:T(8,128)(2,1)} %weights.1), calls=%async_computation | async-start | bytes 2359296 | tf_op jit(solution)/shard_map/all_to_all | solution.py:267
  17.4 5.4 %collective-permute-start.6 = (bf16[576,128]{1,0:T(8,128)(2,1)S(1)}, bf16[576,128]{1,0:T(8,128)(2,1)S(1)}, u32[]{:S(2)}, u32[]{:S(2)}) collective-permute-start(bf16[576,128]{1,0:T(8,128)(2,1)S(1)} %pad_maximum_fusion), channel_id=1, source_target_pairs={{0,35},{1,34},{2,33},{3,32},{32,3},{33,2},{34,1},{35,0},{4,39},{5,... | collective-permute-start | bytes 442376 | tf_op jit(solution)/shard_map/ppermute | solution.py:254
  22.8 1.0 %collective-permute-start.4 = (bf16[576,128]{1,0:T(8,128)(2,1)S(1)}, bf16[576,128]{1,0:T(8,128)(2,1)S(1)}, u32[]{:S(2)}, u32[]{:S(2)}) collective-permute-start(bf16[576,128]{1,0:T(8,128)(2,1)S(1)} %pad_maximum_fusion), channel_id=1, source_target_pairs={{0,33},{1,32},{2,35},{3,34},{32,1},{33,0},{34,3},{35,2},{4,37},{5,... | collective-permute-start | bytes 442376 | tf_op jit(solution)/shard_map/ppermute | solution.py:254
  23.8 1.3 %collective-permute-start.8 = (bf16[576,128]{1,0:T(8,128)(2,1)S(1)}, bf16[576,128]{1,0:T(8,128)(2,1)S(1)}, u32[]{:S(2)}, u32[]{:S(2)}) collective-permute-start(bf16[576,128]{1,0:T(8,128)(2,1)S(1)} %pad_maximum_fusion.1.refs_0_), channel_id=1, source_target_pairs={{0,2},{1,3},{2,0},{3,1},{4,6},{5,7},{6,4},{7,5},{8,10},{9,11},{10,... | collective-permute-start | bytes 442376 | tf_op jit(solution)/shard_map/ppermute | solution.py:257
  25.1 0.7 collective-permute-start.10
  25.9 5.9 %collective-permute-done.6.refs_2_ = bf16[576,128]{1,0:T(8,128)(2,1)S(1)} collective-permute-done((bf16[576,128]{1,0:T(8,128)(2,1)S(1)}, bf16[576,128]{1,0:T(8,128)(2,1)S(1)}, u32[]{:S(2)}, u32[]{:S(2)}) %collective-permute-start.6) | collective-permute-done | bytes 147488 | tf_op jit(solution)/shard_map/ppermute | solution.py:254
  31.7 3.3 %collective-permute-done.4.refs_1_ = bf16[576,128]{1,0:T(8,128)(2,1)S(1)} collective-permute-done((bf16[576,128]{1,0:T(8,128)(2,1)S(1)}, bf16[576,128]{1,0:T(8,128)(2,1)S(1)}, u32[]{:S(2)}, u32[]{:S(2)}) %collective-permute-start.4) | collective-permute-done | bytes 147488 | tf_op jit(solution)/shard_map/ppermute | solution.py:254
  35.0 2.8 %collective-permute-start.5 = (bf16[576,128]{1,0:T(8,128)(2,1)S(1)}, bf16[576,128]{1,0:T(8,128)(2,1)S(1)}, u32[]{:S(2)}, u32[]{:S(2)}) collective-permute-start(bf16[576,128]{1,0:T(8,128)(2,1)S(1)} %collective-permute-done.4.refs_1_), channel_id=1, source_target_pairs={{0,1},{1,0},{2,3},{3,2},{4,5},{5,4},{6,7},{7,6},{8,9},{9,8},{10,11... | collective-permute-start | bytes 442376 | tf_op jit(solution)/shard_map/ppermute | solution.py:260
  37.8 0.0 collective-permute-start.9
  37.9 0.7 expand.2
  38.6 0.9 %add.2 = bf16[32,4,1152]{2,1,0:T(4,128)(2,1)} custom-call(bf16[4,128,1152]{2,1,0:T(8,128)(2,1)S(1)} %all-to-all-done.in_ref), custom_call_target="tpu_custom_call" | custom-call | flops 1000 | bytes 1000 | tf_op jit(solution)/shard_map/add/pallas_call | solution.py:220
  39.5 8.1 %all-to-all-start.1 = ((bf16[32,4,1152]{2,1,0:T(4,128)(2,1)}), bf16[32,4,1152]{2,1,0:T(4,128)(2,1)S(1)}, u32[]{:S(2)}, u32[]{:S(2)}) async-start(bf16[32,4,1152]{2,1,0:T(4,128)(2,1)} %add.2), calls=%async_computation.1 | async-start | bytes 589824 | tf_op jit(solution)/shard_map/all_to_all | solution.py:267
  47.6 1.5 %scatter.7 = (f32[1024,128]{1,0:T(8,128)S(1)}, f32[1024,128]{1,0:T(8,128)S(1)}, f32[1024,128]{1,0:T(8,128)S(1)}, f32[1024,128]{1,0:T(8,128)S(1)}) custom-call(bf16[4,5,128,128]{3,2,1,0:T(8,128)(2,1)S(1)} %get-tuple-element.89.refs_0_, f32[4,5,8,128]{3,2,1,0:T(8,128)S(1)} %get-tuple-element.90.refs_1_), custom_call_target="tpu_custom_call" | custom-call | flops 1000 | bytes 1000 | tf_op jit(solution)/shard_map/scatter/pallas_call | solution.py:220
  49.1 1.5 %scatter.8 = (f32[1024,128]{1,0:T(8,128)S(1)}, f32[1024,128]{1,0:T(8,128)S(1)}, f32[1024,128]{1,0:T(8,128)S(1)}, f32[1024,128]{1,0:T(8,128)S(1)}) custom-call(bf16[4,5,128,128]{3,2,1,0:T(8,128)(2,1)S(1)} %get-tuple-element.95.refs_0_, f32[4,5,8,128]{3,2,1,0:T(8,128)S(1)} %get-tuple-element.96.refs_1_), custom_call_target="tpu_custom_call" | custom-call | flops 1000 | bytes 1000 | tf_op jit(solution)/shard_map/scatter/pallas_call | solution.py:220
  50.7 0.5 expand.3
  51.2 0.4 scatter.9
  51.5 3.2 %collective-permute-start.11 = (bf16[1024,128]{1,0:T(8,128)(2,1)S(1)}, bf16[1024,128]{1,0:T(8,128)(2,1)S(1)}, u32[]{:S(2)}, u32[]{:S(2)}) collective-permute-start(bf16[1024,128]{1,0:T(8,128)(2,1)S(1)} %scatter.9), channel_id=1, source_target_pairs={{0,4},{4,0},{1,5},{5,1},{2,6},{6,2},{3,7},{7,3},{8,12},{12,8},{9,1... | collective-permute-start | bytes 786440 | tf_op jit(solution)/shard_map/ppermute | solution.py:286
  54.8 0.8 %scatter.10 = (bf16[1024,128]{1,0:T(8,128)(2,1)S(1)}, bf16[1024,128]{1,0:T(8,128)(2,1)S(1)}, bf16[1024,128]{1,0:T(8,128)(2,1)S(1)}) custom-call(bf16[4,3,128,128]{3,2,1,0:T(8,128)(2,1)S(1)} %get-tuple-element.110.refs_0_, f32[4,3,8,128]{3,2,1,0:T(8,128)S(1)} %get-tuple-element.111.refs_1_, f32[1024,128]{1,0:T(8,128)S(1)} %get-tuple-element.112.refs_2_, ...), custom_call_target="tpu_custom_call" | custom-call | flops 1000 | bytes 1000 | tf_op jit(solution)/shard_map/scatter/pallas_call | solution.py:220
  55.5 0.1 collective-permute-start.12
  55.6 0.5 collective-permute-start.13
  56.1 0.1 collective-permute-start.14
  56.2 0.4 scatter.11
  56.6 0.6 collective-permute-done.12.refs_4_
  57.1 0.4 collective-permute-done.13.refs_5_
  57.5 0.6 scatter.12
  58.1 0.0 copy-start.3
  58.1 0.0 copy-start.6
  58.1 1.4 %collective-permute-start.15 = (bf16[1024,128]{1,0:T(8,128)(2,1)S(1)}, bf16[1024,128]{1,0:T(8,128)(2,1)S(1)}, u32[]{:S(2)}, u32[]{:S(2)}) collective-permute-start(bf16[1024,128]{1,0:T(8,128)(2,1)S(1)} %get-tuple-element.134), channel_id=1, source_target_pairs={{0,8},{8,16},{16,24},{24,0},{1,9},{9,17},{17,25},{25,1},{2,10},{10... | collective-permute-start | bytes 786440 | tf_op jit(solution)/shard_map/ppermute | solution.py:310
  59.5 1.3 %collective-permute-start.16 = (bf16[1024,128]{1,0:T(8,128)(2,1)S(1)}, bf16[1024,128]{1,0:T(8,128)(2,1)S(1)}, u32[]{:S(2)}, u32[]{:S(2)}) collective-permute-start(bf16[1024,128]{1,0:T(8,128)(2,1)S(1)} %get-tuple-element.135), channel_id=1, source_target_pairs={{0,24},{8,0},{16,8},{24,16},{1,25},{9,1},{17,9},{25,17},{2,26},{10... | collective-permute-start | bytes 786440 | tf_op jit(solution)/shard_map/ppermute | solution.py:311
  60.9 1.6 %collective-permute-start.17 = (bf16[1024,128]{1,0:T(8,128)(2,1)S(1)}, bf16[1024,128]{1,0:T(8,128)(2,1)S(1)}, u32[]{:S(2)}, u32[]{:S(2)}) collective-permute-start(bf16[1024,128]{1,0:T(8,128)(2,1)S(1)} %scatter.11), channel_id=1, source_target_pairs={{0,16},{8,24},{16,0},{24,8},{1,17},{9,25},{17,1},{25,9},{2,18},{10... | collective-permute-start | bytes 786440 | tf_op jit(solution)/shard_map/ppermute | solution.py:307
  62.5 0.4 scatter.13.a_ref
  62.9 4.3 %collective-permute-done.15.b_ref = bf16[1024,128]{1,0:T(8,128)(2,1)S(1)} collective-permute-done((bf16[1024,128]{1,0:T(8,128)(2,1)S(1)}, bf16[1024,128]{1,0:T(8,128)(2,1)S(1)}, u32[]{:S(2)}, u32[]{:S(2)}) %collective-permute-start.15) | collective-permute-done | bytes 262176 | tf_op jit(solution)/shard_map/ppermute | solution.py:310
  67.2 6.7 %collective-permute-done.17.d_ref = bf16[1024,128]{1,0:T(8,128)(2,1)S(1)} collective-permute-done((bf16[1024,128]{1,0:T(8,128)(2,1)S(1)}, bf16[1024,128]{1,0:T(8,128)(2,1)S(1)}, u32[]{:S(2)}, u32[]{:S(2)}) %collective-permute-start.17) | collective-permute-done | bytes 262176 | tf_op jit(solution)/shard_map/ppermute | solution.py:307
  73.9 1.3 %update.1 = (f32[1024,128]{1,0:T(8,128)}, f32[8,128]{1,0:T(8,128)}) custom-call(bf16[1024,128]{1,0:T(8,128)(2,1)S(1)} %scatter.13.a_ref, bf16[1024,128]{1,0:T(8,128)(2,1)S(1)} %collective-permute-done.15.b_ref, bf16[1024,128]{1,0:T(8,128)(2,1)S(1)} %collective-permute-done.16.c_ref, bf16[1024,128]{1,0:T(8,128)(2,1)S(1)} %collective-permute-done.17.d_ref, ...), custom_call_target="tpu_custom_call" | custom-call | flops 1000 | bytes 1000 | tf_op jit(solution)/shard_map/update/pallas_call | solution.py:220
  75.1 0.7 add.3
  (29 shorter events, 0.1 us)
Async XLA Ops:
  0.6 0.8 %copy-start.7 = (s32[128,8,8]{0,2,1:T(8,128)S(1)}, s32[128,8,8]{0,2,1:T(8,128)}, u32[]{:S(2)}) copy-start(s32[128,8,8]{0,2,1:T(8,128)} %param.13) | copy-start | bytes 98308
  1.4 1.5 %copy-start = (bf16[1152,512]{1,0:T(8,128)(2,1)S(1)}, bf16[1152,512]{1,0:T(8,128)(2,1)}, u32[]{:S(2)}) copy-start(bf16[1152,512]{1,0:T(8,128)(2,1)} %down_ref.1) | copy-start | bytes 3538948
  1.4 1.6 %copy-start.1 = (bf16[512,1152]{1,0:T(8,128)(2,1)S(1)}, bf16[512,1152]{1,0:T(8,128)(2,1)}, u32[]{:S(2)}) copy-start(bf16[512,1152]{1,0:T(8,128)(2,1)} %up_ref.1) | copy-start | bytes 3538948
  1.4 1.7 %copy-start.2 = (bf16[128,1152]{1,0:T(8,128)(2,1)S(1)}, bf16[128,1152]{1,0:T(8,128)(2,1)}, u32[]{:S(2)}) copy-start(bf16[128,1152]{1,0:T(8,128)(2,1)} %cot_ref.1) | copy-start | bytes 884740
  1.4 1.8 %copy-start.4 = (bf16[128,1152]{1,0:T(8,128)(2,1)S(1)}, bf16[128,1152]{1,0:T(8,128)(2,1)}, u32[]{:S(2)}) copy-start(bf16[128,1152]{1,0:T(8,128)(2,1)} %in_ref) | copy-start | bytes 884740
  3.2 4.5 %copy-start.5 = (f32[1152]{0:T(1024)S(1)}, f32[1152]{0:T(1024)}, u32[]{:S(2)}) copy-start(f32[1152]{0:T(1024)} %param.12) | copy-start | bytes 13828
  4.3 6.6 %collective-permute-start.3 = (bf16[128,2816]{1,0:T(8,128)(2,1)S(1)}, bf16[128,2816]{1,0:T(8,128)(2,1)S(1)}, u32[]{:S(2)}, u32[]{:S(2)}) collective-permute-start(bf16[128,2816]{1,0:T(8,128)(2,1)S(1)} %get-tuple-element.79.pack_ref), channel_id=1, source_target_pairs={{0,4},{4,0},{1,5},{5,1},{2,6},{6,2},{3,7},{7,3},{8,12},{12,8},{9,1... | collective-permute-start | bytes 2162696 | tf_op jit(solution)/shard_map/ppermute | solution.py:244
  8.8 8.6 %collective-permute-start.2 = (bf16[2,144,128]{2,1,0:T(8,128)(2,1)S(1)}, bf16[2,144,128]{2,1,0:T(8,128)(2,1)S(1)}, u32[]{:S(2)}, u32[]{:S(2)}) collective-permute-start(bf16[2,144,128]{2,1,0:T(8,128)(2,1)S(1)} %get-tuple-element.140), channel_id=1, source_target_pairs={{0,192},{64,0},{128,64},{192,128},{1,193},{65,1},{129,65},{193,129... | collective-permute-start | bytes 221192 | tf_op jit(solution)/shard_map/ppermute | solution.py:245
  9.9 7.5 %collective-permute-start.1 = (bf16[2,144,128]{2,1,0:T(8,128)(2,1)S(1)}, bf16[2,144,128]{2,1,0:T(8,128)(2,1)S(1)}, u32[]{:S(2)}, u32[]{:S(2)}) collective-permute-start(bf16[2,144,128]{2,1,0:T(8,128)(2,1)S(1)} %get-tuple-element.141), channel_id=1, source_target_pairs={{0,128},{64,192},{128,0},{192,64},{1,129},{65,193},{129,1},{193,65... | collective-permute-start | bytes 221192 | tf_op jit(solution)/shard_map/ppermute | solution.py:245
  10.2 7.1 %collective-permute-start = (bf16[2,144,128]{2,1,0:T(8,128)(2,1)S(1)}, bf16[2,144,128]{2,1,0:T(8,128)(2,1)S(1)}, u32[]{:S(2)}, u32[]{:S(2)}) collective-permute-start(bf16[2,144,128]{2,1,0:T(8,128)(2,1)S(1)} %get-tuple-element.142), channel_id=1, source_target_pairs={{0,64},{64,128},{128,192},{192,0},{1,65},{65,129},{129,193},{193,1... | collective-permute-start | bytes 221192 | tf_op jit(solution)/shard_map/ppermute | solution.py:245
  13.1 25.5 %all-to-all-start = ((bf16[4,128,1152]{2,1,0:T(8,128)(2,1)}), bf16[4,128,1152]{2,1,0:T(8,128)(2,1)S(1)}, u32[]{:S(2)}, u32[]{:S(2)}) async-start(bf16[4,128,1152]{2,1,0:T(8,128)(2,1)} %weights.1), calls=%async_computation | async-start | bytes 2359296 | tf_op jit(solution)/shard_map/all_to_all | solution.py:267
  17.4 14.3 %collective-permute-start.6 = (bf16[576,128]{1,0:T(8,128)(2,1)S(1)}, bf16[576,128]{1,0:T(8,128)(2,1)S(1)}, u32[]{:S(2)}, u32[]{:S(2)}) collective-permute-start(bf16[576,128]{1,0:T(8,128)(2,1)S(1)} %pad_maximum_fusion), channel_id=1, source_target_pairs={{0,35},{1,34},{2,33},{3,32},{32,3},{33,2},{34,1},{35,0},{4,39},{5,... | collective-permute-start | bytes 442376 | tf_op jit(solution)/shard_map/ppermute | solution.py:254
  22.8 12.2 %collective-permute-start.4 = (bf16[576,128]{1,0:T(8,128)(2,1)S(1)}, bf16[576,128]{1,0:T(8,128)(2,1)S(1)}, u32[]{:S(2)}, u32[]{:S(2)}) collective-permute-start(bf16[576,128]{1,0:T(8,128)(2,1)S(1)} %pad_maximum_fusion), channel_id=1, source_target_pairs={{0,33},{1,32},{2,35},{3,34},{32,1},{33,0},{34,3},{35,2},{4,37},{5,... | collective-permute-start | bytes 442376 | tf_op jit(solution)/shard_map/ppermute | solution.py:254
  23.8 14.0 %collective-permute-start.8 = (bf16[576,128]{1,0:T(8,128)(2,1)S(1)}, bf16[576,128]{1,0:T(8,128)(2,1)S(1)}, u32[]{:S(2)}, u32[]{:S(2)}) collective-permute-start(bf16[576,128]{1,0:T(8,128)(2,1)S(1)} %pad_maximum_fusion.1.refs_0_), channel_id=1, source_target_pairs={{0,2},{1,3},{2,0},{3,1},{4,6},{5,7},{6,4},{7,5},{8,10},{9,11},{10,... | collective-permute-start | bytes 442376 | tf_op jit(solution)/shard_map/ppermute | solution.py:257
  25.1 12.7 %collective-permute-start.10 = (bf16[576,128]{1,0:T(8,128)(2,1)S(1)}, bf16[576,128]{1,0:T(8,128)(2,1)S(1)}, u32[]{:S(2)}, u32[]{:S(2)}) collective-permute-start(bf16[576,128]{1,0:T(8,128)(2,1)S(1)} %pad_maximum_fusion.1.refs_0_), channel_id=1, source_target_pairs={{0,1},{1,0},{2,3},{3,2},{4,5},{5,4},{6,7},{7,6},{8,9},{9,8},{10,11... | collective-permute-start | bytes 442376 | tf_op jit(solution)/shard_map/ppermute | solution.py:257
  31.7 18.9 %collective-permute-start.7 = (bf16[576,128]{1,0:T(8,128)(2,1)S(1)}, bf16[576,128]{1,0:T(8,128)(2,1)S(1)}, u32[]{:S(2)}, u32[]{:S(2)}) collective-permute-start(bf16[576,128]{1,0:T(8,128)(2,1)S(1)} %collective-permute-done.6.refs_2_), channel_id=1, source_target_pairs={{0,1},{1,0},{2,3},{3,2},{4,5},{5,4},{6,7},{7,6},{8,9},{9,8},{10,11... | collective-permute-start | bytes 442376 | tf_op jit(solution)/shard_map/ppermute | solution.py:260
  35.0 15.7 %collective-permute-start.5 = (bf16[576,128]{1,0:T(8,128)(2,1)S(1)}, bf16[576,128]{1,0:T(8,128)(2,1)S(1)}, u32[]{:S(2)}, u32[]{:S(2)}) collective-permute-start(bf16[576,128]{1,0:T(8,128)(2,1)S(1)} %collective-permute-done.4.refs_1_), channel_id=1, source_target_pairs={{0,1},{1,0},{2,3},{3,2},{4,5},{5,4},{6,7},{7,6},{8,9},{9,8},{10,11... | collective-permute-start | bytes 442376 | tf_op jit(solution)/shard_map/ppermute | solution.py:260
  37.8 12.8 %collective-permute-start.9 = (bf16[576,128]{1,0:T(8,128)(2,1)S(1)}, bf16[576,128]{1,0:T(8,128)(2,1)S(1)}, u32[]{:S(2)}, u32[]{:S(2)}) collective-permute-start(bf16[576,128]{1,0:T(8,128)(2,1)S(1)} %collective-permute-done.8.refs_3_), channel_id=1, source_target_pairs={{0,1},{1,0},{2,3},{3,2},{4,5},{5,4},{6,7},{7,6},{8,9},{9,8},{10,11... | collective-permute-start | bytes 442376 | tf_op jit(solution)/shard_map/ppermute | solution.py:260
  39.5 35.7 %all-to-all-start.1 = ((bf16[32,4,1152]{2,1,0:T(4,128)(2,1)}), bf16[32,4,1152]{2,1,0:T(4,128)(2,1)S(1)}, u32[]{:S(2)}, u32[]{:S(2)}) async-start(bf16[32,4,1152]{2,1,0:T(4,128)(2,1)} %add.2), calls=%async_computation.1 | async-start | bytes 589824 | tf_op jit(solution)/shard_map/all_to_all | solution.py:267
  51.5 4.7 %collective-permute-start.11 = (bf16[1024,128]{1,0:T(8,128)(2,1)S(1)}, bf16[1024,128]{1,0:T(8,128)(2,1)S(1)}, u32[]{:S(2)}, u32[]{:S(2)}) collective-permute-start(bf16[1024,128]{1,0:T(8,128)(2,1)S(1)} %scatter.9), channel_id=1, source_target_pairs={{0,4},{4,0},{1,5},{5,1},{2,6},{6,2},{3,7},{7,3},{8,12},{12,8},{9,1... | collective-permute-start | bytes 786440 | tf_op jit(solution)/shard_map/ppermute | solution.py:286
  55.5 1.6 %collective-permute-start.12 = (bf16[1024,128]{1,0:T(8,128)(2,1)S(1)}, bf16[1024,128]{1,0:T(8,128)(2,1)S(1)}, u32[]{:S(2)}, u32[]{:S(2)}) collective-permute-start(bf16[1024,128]{1,0:T(8,128)(2,1)S(1)} %get-tuple-element.126), channel_id=1, source_target_pairs={{0,4},{4,0},{1,5},{5,1},{2,6},{6,2},{3,7},{7,3},{8,12},{12,8},{9,1... | collective-permute-start | bytes 786440 | tf_op jit(solution)/shard_map/ppermute | solution.py:286
  55.6 1.9 %collective-permute-start.13 = (bf16[1024,128]{1,0:T(8,128)(2,1)S(1)}, bf16[1024,128]{1,0:T(8,128)(2,1)S(1)}, u32[]{:S(2)}, u32[]{:S(2)}) collective-permute-start(bf16[1024,128]{1,0:T(8,128)(2,1)S(1)} %get-tuple-element.127), channel_id=1, source_target_pairs={{0,4},{4,0},{1,5},{5,1},{2,6},{6,2},{3,7},{7,3},{8,12},{12,8},{9,1... | collective-permute-start | bytes 786440 | tf_op jit(solution)/shard_map/ppermute | solution.py:286
  56.1 6.4 %collective-permute-start.14 = (bf16[1024,128]{1,0:T(8,128)(2,1)S(1)}, bf16[1024,128]{1,0:T(8,128)(2,1)S(1)}, u32[]{:S(2)}, u32[]{:S(2)}) collective-permute-start(bf16[1024,128]{1,0:T(8,128)(2,1)S(1)} %get-tuple-element.133), channel_id=1, source_target_pairs={{0,4},{4,0},{1,5},{5,1},{2,6},{6,2},{3,7},{7,3},{8,12},{12,8},{9,1... | collective-permute-start | bytes 786440 | tf_op jit(solution)/shard_map/ppermute | solution.py:286
  58.1 15.8 %copy-start.3 = (f32[1024,128]{1,0:T(8,128)S(1)}, f32[1024,128]{1,0:T(8,128)}, u32[]{:S(2)}) copy-start(f32[1024,128]{1,0:T(8,128)} %table_ref.1) | copy-start | bytes 1572868
  58.1 15.8 %copy-start.6 = (f32[1024]{0:T(1024)S(1)}, f32[1024]{0:T(1024)}, u32[]{:S(2)}) copy-start(f32[1024]{0:T(1024)} %param.15) | copy-start | bytes 12292
  58.1 9.1 %collective-permute-start.15 = (bf16[1024,128]{1,0:T(8,128)(2,1)S(1)}, bf16[1024,128]{1,0:T(8,128)(2,1)S(1)}, u32[]{:S(2)}, u32[]{:S(2)}) collective-permute-start(bf16[1024,128]{1,0:T(8,128)(2,1)S(1)} %get-tuple-element.134), channel_id=1, source_target_pairs={{0,8},{8,16},{16,24},{24,0},{1,9},{9,17},{17,25},{25,1},{2,10},{10... | collective-permute-start | bytes 786440 | tf_op jit(solution)/shard_map/ppermute | solution.py:310
  59.5 7.6 %collective-permute-start.16 = (bf16[1024,128]{1,0:T(8,128)(2,1)S(1)}, bf16[1024,128]{1,0:T(8,128)(2,1)S(1)}, u32[]{:S(2)}, u32[]{:S(2)}) collective-permute-start(bf16[1024,128]{1,0:T(8,128)(2,1)S(1)} %get-tuple-element.135), channel_id=1, source_target_pairs={{0,24},{8,0},{16,8},{24,16},{1,25},{9,1},{17,9},{25,17},{2,26},{10... | collective-permute-start | bytes 786440 | tf_op jit(solution)/shard_map/ppermute | solution.py:311
  60.9 13.0 %collective-permute-start.17 = (bf16[1024,128]{1,0:T(8,128)(2,1)S(1)}, bf16[1024,128]{1,0:T(8,128)(2,1)S(1)}, u32[]{:S(2)}, u32[]{:S(2)}) collective-permute-start(bf16[1024,128]{1,0:T(8,128)(2,1)S(1)} %scatter.11), channel_id=1, source_target_pairs={{0,16},{8,24},{16,0},{24,8},{1,17},{9,25},{17,1},{25,9},{2,18},{10... | collective-permute-start | bytes 786440 | tf_op jit(solution)/shard_map/ppermute | solution.py:307

commit v5 on v4

--- a/solution.py
+++ b/solution.py
@@ -80,7 +80,7 @@
 
 
 def hidden_kernel(in_ref, cot_ref, down_ref, up_ref, pack_ref, cols_ref, both_ref):
-    yy, core = spot("y"), spot("c")
+    core = spot("c")
     inputs = in_ref[...]
     grad_scale = (cot_ref[...].astype(F32) * inputs.astype(F32)).astype(BF16)
     pack_ref[:, :FEATURES] = inputs
@@ -93,8 +93,7 @@
     both = jnp.concatenate([grad_hidden, hidden], axis=1)
     src = iota((2 * RANK, RANK), 0)
     dst = iota((2 * RANK, RANK), 1)
-    from_y = ((dst >> 7) + yy) & 3
-    want = from_y * 256 + ((dst >> 6) & 1) * 128 + ((dst >> 2) & 3) * 32 + ((dst >> 4) & 3) * 4 + (dst & 3)
+    want = (dst >> 7) * 256 + ((dst >> 6) & 1) * 128 + ((dst >> 2) & 3) * 32 + ((dst >> 4) & 3) * 4 + (dst & 3)
     pack_ref[:, 2 * FEATURES:] = dot(both, (src == want + (1 - core) * 16).astype(F32).astype(BF16), 1, 0).astype(BF16)
     cols_ref[...] = dot(both, (src == want + core * 16).astype(F32).astype(BF16), 1, 0).astype(BF16)
 
@@ -113,18 +112,13 @@
 
 
 def weight_kernel(pack_ref, cols_ref, other_ref, out_ref):
-    yy = spot("y")
-    for d in range(NY):
-        to = (yy + d) & 3
-        s = slice(d * 128, (d + 1) * 128)
-        left = jnp.concatenate([cols_ref[:, s], other_ref[:, 2 * FEATURES + d * 128:2 * FEATURES + (d + 1) * 128]], axis=0)
-
-        def put(first):
-            right = jnp.concatenate([pack_ref[:, first:first + FEATURES], other_ref[:, first:first + FEATURES]], axis=0)
-            out_ref[to] = dot(left, right, 0, 0).astype(BF16)
-
-        pl.when(to < 2)(functools.partial(put, 0))
-        pl.when(to >= 2)(functools.partial(put, FEATURES))
+    for half in range(2):
+        s = slice(half * 256, (half + 1) * 256)
+        t = slice(half * FEATURES, (half + 1) * FEATURES)
+        theirs = other_ref[:, 2 * FEATURES + half * 256:2 * FEATURES + (half + 1) * 256]
+        left = jnp.concatenate([cols_ref[:, s], theirs], axis=0)
+        right = jnp.concatenate([pack_ref[:, t], other_ref[:, t]], axis=0)
+        out_ref[half * 2:half * 2 + 2] = dot(left, right, 0, 0).astype(BF16).reshape(2, 128, FEATURES)
 
 
 def add_kernel(in_ref, out_ref):
@@ -184,11 +178,11 @@
 
 
 def scatter_kernel(ds, *refs):
-    look, row, rest = refs[0], refs[1], refs[2:]
+    looks, rows, rest = refs[0:4:2], refs[1:4:2], refs[4:]
     count = len(ds)
     firsts, outs = rest[:-count], rest[-count:]
     for i, d in enumerate(ds):
-        scatter(d, (look,), (row,), outs[i], firsts[i::count])
+        scatter(d, looks, rows, outs[i], firsts[i::count])
 
 
 def update_kernel(a_ref, b_ref, c_ref, d_ref, table_ref, accum_ref, table_out, accum_out):
@@ -276,10 +270,10 @@
             functools.partial(expand_kernel, len(blocks)), "expand", (look, row, look, row), tuple(blocks), 16, cost(1_000, 1_000)
         )
 
-    def scattered(arrays, ds, firsts=(), kind=BF16):
+    def scattered(arrays, ds, firsts=()):
         return call(
             functools.partial(scatter_kernel, ds), "scatter",
-            (shape((ROWS, EMB), kind),) * len(ds), (*arrays, *firsts), 24, cost(1_000, 1_000),
+            (shape((ROWS, EMB), BF16),) * len(ds), (*arrays, *firsts), 24, cost(1_000, 1_000),
         )
 
     def swapped(vs):
@@ -289,27 +283,26 @@
     early, terms = lax.optimization_barrier((early, exchanged(terms, "y")))
     terms = added(terms, (32, 4, FEATURES), BF16)
     weight_total = added(exchanged(terms, ("zh", "zl", "x")), (4, FEATURES), F32)
-    order = (2, 1, 3, 0)
-    base_own = scattered(early[:2], order, kind=F32)
-    base_other = scattered(early[2:], order, kind=F32)
-    late, base_own, base_other, _ = lax.optimization_barrier((passed, base_own, base_other, terms))
+    late, _ = lax.optimization_barrier((passed, terms))
     late = expanded(late)
-    own, other = late[:2], late[2:]
-
-    first = scattered(other, (2,), base_other[:1])
+    own, other = [*early[:2], *late[:2]], [*early[2:], *late[2:]]
+
+    first = scattered(other, (2,))
     other, first = lax.optimization_barrier((other, first))
     (first,) = swapped(first)
-    rest = scattered(other, (1, 3, 0), base_other[1:])
+    rest = scattered(other, (1, 3))
     own, rest = lax.optimization_barrier((own, rest))
     rest = swapped(rest)
-    apart = scattered(own, (2,), (base_own[0], first))
+    apart = scattered(own, (2,), (first,))
     own, apart = lax.optimization_barrier((own, apart))
     apart = lax.ppermute(apart[0], "x", ring(NX, 2))
-    right, left = scattered(own, (1, 3), (*base_own[1:3], *rest[:2]))
-    own, right, left = lax.optimization_barrier((own, right, left))
+    right, left = scattered(own, (1, 3), rest)
+    other, right, left = lax.optimization_barrier((other, right, left))
     right = lax.ppermute(right, "x", ring(NX, 1))
     left = lax.ppermute(left, "x", ring(NX, 3))
-    (here,) = scattered(own, (0,), (base_own[3], rest[2]))
+    (here,) = scattered(own, (0,), swapped(scattered(other, (0,))))
+
+    here, weight_total = lax.optimization_barrier((here, weight_total))
 
     table_new, accum_new = call(
         update_kernel, "update", (shape((ROWS, EMB), F32), shape((8, 128), F32)),

time: 76.1 us -> 75.1 us (0.987)
  waiting for transfers between devices: 21.1 us -> 16.1 us
  starting transfers between devices: 37.4 us -> 41.4 us
    ppermute x1, waiting for transfers between devices: 6.68 us -> 2.19 us  [per_device(): apart = lax.ppermute(apart[0], 'x', ring(NX, 2))]
    ppermute x2, waiting for transfers between devices: 9.14 us -> 5.33 us  [cross(): return lax.ppermute(far, ('zh', 'zl'), [(i, 7 - i ^ m) for i in range(8)])]
    ppermute x3, starting transfers between devices: 2.86 us -> 6.61 us  [pass_on(): return lax.ppermute(v, 'zl', [(i, i ^ 1) for i in range(NZL)])]
    ppermute x1, waiting for transfers between devices: 4.3 us -> 6.23 us  [per_device(): right = lax.ppermute(right, 'x', ring(NX, 1))]
    ppermute x2, starting transfers between devices: 2.02 us -> 3.79 us  [line(): return lax.ppermute(near, 'zl', [(i, i ^ m) for i in range(NZL)])]
    ppermute x2, starting transfers between devices: 6.38 us -> 4.85 us  [cross(): return lax.ppermute(far, ('zh', 'zl'), [(i, 7 - i ^ m) for i in range(8)])]
    ppermute x1, starting transfers between devices: 1.64 us -> 3.01 us  [per_device(): apart = lax.ppermute(apart[0], 'x', ring(NX, 2))]
    ppermute x2, waiting for transfers between devices: 0.01 us -> 1.31 us  [line(): return lax.ppermute(near, 'zl', [(i, i ^ m) for i in range(NZL)])]
  transfers between devices with their start and end apart: 20 -> 20, of which waited for: 6 -> 8; matrix products, arithmetic and copies ran while one was open for 0% -> 0% of each run, Pallas kernels for 16% -> 15%
where the time goes in v5:
time: 75.1 us; the launch traced here: 74.7 us
  starting transfers between devices  41.4 us (55%)
  waiting for transfers between devices  16.1 us (21%)
  Pallas kernels  15.3 us (20%)
  local copies, waits for them, and re-layouts  1.04 us (1%)
  between operations  0.81 us (1%)
    pallas_call x15, Pallas kernels, call(): pl.pallas_call(kernel, out_shape=outs, in_specs=[VMEM] * len(operands), o...  15.3 us
    all_to_all x2, starting transfers between devices, exchanged(): return lax.all_to_all(v, axes, split_axis=0, concat_axis=0, tiled=True)  11.7 us
    ppermute x3, starting transfers between devices, pass_on(): return lax.ppermute(v, 'zl', [(i, i ^ 1) for i in range(NZL)])  6.61 us
    ppermute x1, waiting for transfers between devices, per_device(): right = lax.ppermute(right, 'x', ring(NX, 1))  6.23 us
    ppermute x2, waiting for transfers between devices, cross(): return lax.ppermute(far, ('zh', 'zl'), [(i, 7 - i ^ m) for i in range(8)])  5.33 us
    ppermute x2, starting transfers between devices, cross(): return lax.ppermute(far, ('zh', 'zl'), [(i, 7 - i ^ m) for i in range(8)])  4.85 us
    ppermute x2, starting transfers between devices, line(): return lax.ppermute(near, 'zl', [(i, i ^ m) for i in range(NZL)])  3.79 us
    ppermute x4, starting transfers between devices, swapped(): return [lax.ppermute(v, 'c', swap) for v in vs]  3.41 us
  transfers between devices with their start and end apart: 20, of which 8 were waited for; matrix products, arithmetic and copies ran while one was open for 0% of the time, Pallas kernels for 15%

profile of v5, /device:TPU:1, one launch (start us, length us, event | category | flops | bytes accessed | tf_op | source)
XLA Modules:
  0.0 74.7 jit_solution(1136237554834386850)
XLA Ops:
  0.6 0.7 %copy-done.7 = s32[128,8,8]{0,2,1:T(8,128)S(1)} copy-done((s32[128,8,8]{0,2,1:T(8,128)S(1)}, s32[128,8,8]{0,2,1:T(8,128)}, u32[]{:S(2)}) %copy-start.7) | copy-done | bytes 32792
  1.4 1.5 %rank.1.meta_ref = bf16[8,16,128]{2,1,0:T(8,128)(2,1)S(1)} custom-call(s32[64,128]{1,0:T(8,128)S(1)} %bitcast.32), custom_call_target="tpu_custom_call" | custom-call | flops 2000000000 | bytes 100000 | tf_op jit(solution)/shard_map/rank/pallas_call | solution.py:214
  2.9 0.1 copy-done.1
  3.0 0.0 copy-done.2
  3.1 0.1 copy-done.4
  3.2 1.1 %hidden.1 = (bf16[128,2816]{1,0:T(8,128)(2,1)S(1)}, bf16[128,512]{1,0:T(8,128)(2,1)S(1)}, bf16[128,1024]{1,0:T(8,128)(2,1)S(1)}) custom-call(bf16[128,1152]{1,0:T(8,128)(2,1)S(1)} %copy-done.4, bf16[128,1152]{1,0:T(8,128)(2,1)S(1)} %copy-done.2, bf16[1152,512]{1,0:T(8,128)(2,1)S(1)} %copy-done, bf16[512,1152]{1,0:T(8,128)(2,1)S(1)} %copy-done.1), custom_call_target="tpu_custom_call" | custom-call | flops 500000000 | bytes 4000000 | tf_op jit(solution)/shard_map/hidden/pallas_call | solution.py:214
  4.3 3.3 %collective-permute-start.3 = (bf16[128,2816]{1,0:T(8,128)(2,1)S(1)}, bf16[128,2816]{1,0:T(8,128)(2,1)S(1)}, u32[]{:S(2)}, u32[]{:S(2)}) collective-permute-start(bf16[128,2816]{1,0:T(8,128)(2,1)S(1)} %get-tuple-element.71.pack_ref), channel_id=1, source_target_pairs={{0,4},{4,0},{1,5},{5,1},{2,6},{6,2},{3,7},{7,3},{8,12},{12,8},{9,1... | collective-permute-start | bytes 2162696 | tf_op jit(solution)/shard_map/ppermute | solution.py:238
  7.6 1.2 %pooled.1 = (bf16[128,128]{1,0:T(8,128)(2,1)}, bf16[4,2,144,128]{3,2,1,0:T(8,128)(2,1)S(1)}) custom-call(bf16[128,1152]{1,0:T(8,128)(2,1)S(1)} %copy-done.2, bf16[128,1024]{1,0:T(8,128)(2,1)S(1)} %get-tuple-element.68.both_ref, bf16[1152,512]{1,0:T(8,128)(2,1)S(1)} %copy-done, bf16[512,1152]{1,0:T(8,128)(2,1)S(1)} %copy-done.1, f32[9,128]{1,0:T(8,128)S(1)} %bitcast.30, ...), custom_call_target="tpu_custom_call" | custom-call | flops 300000000 | bytes 4000000 | tf_op jit(solution)/shard_map/pooled/pallas_call | solution.py:214
  8.8 1.1 %collective-permute-start.2 = (bf16[2,144,128]{2,1,0:T(8,128)(2,1)S(1)}, bf16[2,144,128]{2,1,0:T(8,128)(2,1)S(1)}, u32[]{:S(2)}, u32[]{:S(2)}) collective-permute-start(bf16[2,144,128]{2,1,0:T(8,128)(2,1)S(1)} %get-tuple-element.124), channel_id=1, source_target_pairs={{0,192},{64,0},{128,64},{192,128},{1,193},{65,1},{129,65},{193,129... | collective-permute-start | bytes 221192 | tf_op jit(solution)/shard_map/ppermute | solution.py:239
  9.9 0.4 collective-permute-start.1
  10.2 0.7 collective-permute-start
  10.9 1.6 %weights.1 = bf16[4,128,1152]{2,1,0:T(8,128)(2,1)} custom-call(bf16[128,2816]{1,0:T(8,128)(2,1)S(1)} %get-tuple-element.71.pack_ref, bf16[128,512]{1,0:T(8,128)(2,1)S(1)} %get-tuple-element.72.cols_ref, bf16[128,2816]{1,0:T(8,128)(2,1)S(1)} %collective-permute-done.3.other_ref), custom_call_target="tpu_custom_call" | custom-call | flops 300000000 | bytes 3000000 | tf_op jit(solution)/shard_map/weights/pallas_call | solution.py:214
  12.5 4.3 %all-to-all-start = ((bf16[4,128,1152]{2,1,0:T(8,128)(2,1)}), bf16[4,128,1152]{2,1,0:T(8,128)(2,1)S(1)}, u32[]{:S(2)}, u32[]{:S(2)}) async-start(bf16[4,128,1152]{2,1,0:T(8,128)(2,1)} %weights.1), calls=%async_computation | async-start | bytes 2359296 | tf_op jit(solution)/shard_map/all_to_all | solution.py:261
  16.8 0.4 collective-permute-done
  17.2 3.0 %collective-permute-start.6 = (bf16[576,128]{1,0:T(8,128)(2,1)S(1)}, bf16[576,128]{1,0:T(8,128)(2,1)S(1)}, u32[]{:S(2)}, u32[]{:S(2)}) collective-permute-start(bf16[576,128]{1,0:T(8,128)(2,1)S(1)} %pad_maximum_fusion.refs_0_), channel_id=1, source_target_pairs={{0,2},{1,3},{2,0},{3,1},{4,6},{5,7},{6,4},{7,5},{8,10},{9,11},{10,... | collective-permute-start | bytes 442376 | tf_op jit(solution)/shard_map/ppermute | solution.py:251
  20.3 3.8 %collective-permute-start.5 = (bf16[576,128]{1,0:T(8,128)(2,1)S(1)}, bf16[576,128]{1,0:T(8,128)(2,1)S(1)}, u32[]{:S(2)}, u32[]{:S(2)}) collective-permute-start(bf16[576,128]{1,0:T(8,128)(2,1)S(1)} %pad_maximum_fusion.1), channel_id=1, source_target_pairs={{0,35},{1,34},{2,33},{3,32},{32,3},{33,2},{34,1},{35,0},{4,39},{5,... | collective-permute-start | bytes 442376 | tf_op jit(solution)/shard_map/ppermute | solution.py:248
  24.1 1.0 %collective-permute-start.4 = (bf16[576,128]{1,0:T(8,128)(2,1)S(1)}, bf16[576,128]{1,0:T(8,128)(2,1)S(1)}, u32[]{:S(2)}, u32[]{:S(2)}) collective-permute-start(bf16[576,128]{1,0:T(8,128)(2,1)S(1)} %pad_maximum_fusion.1), channel_id=1, source_target_pairs={{0,33},{1,32},{2,35},{3,34},{32,1},{33,0},{34,3},{35,2},{4,37},{5,... | collective-permute-start | bytes 442376 | tf_op jit(solution)/shard_map/ppermute | solution.py:248
  25.1 0.7 collective-permute-start.7
  25.9 1.3 %collective-permute-done.6.refs_3_ = bf16[576,128]{1,0:T(8,128)(2,1)S(1)} collective-permute-done((bf16[576,128]{1,0:T(8,128)(2,1)S(1)}, bf16[576,128]{1,0:T(8,128)(2,1)S(1)}, u32[]{:S(2)}, u32[]{:S(2)}) %collective-permute-start.6) | collective-permute-done | bytes 147488 | tf_op jit(solution)/shard_map/ppermute | solution.py:251
  27.2 1.1 %collective-permute-start.10 = (bf16[576,128]{1,0:T(8,128)(2,1)S(1)}, bf16[576,128]{1,0:T(8,128)(2,1)S(1)}, u32[]{:S(2)}, u32[]{:S(2)}) collective-permute-start(bf16[576,128]{1,0:T(8,128)(2,1)S(1)} %collective-permute-done.6.refs_3_), channel_id=1, source_target_pairs={{0,1},{1,0},{2,3},{3,2},{4,5},{5,4},{6,7},{7,6},{8,9},{9,8},{10,11... | collective-permute-start | bytes 442376 | tf_op jit(solution)/shard_map/ppermute | solution.py:254
  28.2 2.5 %collective-permute-done.5.refs_2_ = bf16[576,128]{1,0:T(8,128)(2,1)S(1)} collective-permute-done((bf16[576,128]{1,0:T(8,128)(2,1)S(1)}, bf16[576,128]{1,0:T(8,128)(2,1)S(1)}, u32[]{:S(2)}, u32[]{:S(2)}) %collective-permute-start.5) | collective-permute-done | bytes 147488 | tf_op jit(solution)/shard_map/ppermute | solution.py:248
  30.7 2.6 %collective-permute-start.9 = (bf16[576,128]{1,0:T(8,128)(2,1)S(1)}, bf16[576,128]{1,0:T(8,128)(2,1)S(1)}, u32[]{:S(2)}, u32[]{:S(2)}) collective-permute-start(bf16[576,128]{1,0:T(8,128)(2,1)S(1)} %collective-permute-done.5.refs_2_), channel_id=1, source_target_pairs={{0,1},{1,0},{2,3},{3,2},{4,5},{5,4},{6,7},{7,6},{8,9},{9,8},{10,11... | collective-permute-start | bytes 442376 | tf_op jit(solution)/shard_map/ppermute | solution.py:254
  33.3 2.8 %collective-permute-done.4.refs_1_ = bf16[576,128]{1,0:T(8,128)(2,1)S(1)} collective-permute-done((bf16[576,128]{1,0:T(8,128)(2,1)S(1)}, bf16[576,128]{1,0:T(8,128)(2,1)S(1)}, u32[]{:S(2)}, u32[]{:S(2)}) %collective-permute-start.4) | collective-permute-done | bytes 147488 | tf_op jit(solution)/shard_map/ppermute | solution.py:248
  36.2 3.0 %collective-permute-start.8 = (bf16[576,128]{1,0:T(8,128)(2,1)S(1)}, bf16[576,128]{1,0:T(8,128)(2,1)S(1)}, u32[]{:S(2)}, u32[]{:S(2)}) collective-permute-start(bf16[576,128]{1,0:T(8,128)(2,1)S(1)} %collective-permute-done.4.refs_1_), channel_id=1, source_target_pairs={{0,1},{1,0},{2,3},{3,2},{4,5},{5,4},{6,7},{7,6},{8,9},{9,8},{10,11... | collective-permute-start | bytes 442376 | tf_op jit(solution)/shard_map/ppermute | solution.py:254
  39.1 0.7 expand.2
  39.8 0.9 %add.2 = bf16[32,4,1152]{2,1,0:T(4,128)(2,1)} custom-call(bf16[4,128,1152]{2,1,0:T(8,128)(2,1)S(1)} %all-to-all-done.in_ref), custom_call_target="tpu_custom_call" | custom-call | flops 1000 | bytes 1000 | tf_op jit(solution)/shard_map/add/pallas_call | solution.py:214
  40.7 7.4 %all-to-all-start.1 = ((bf16[32,4,1152]{2,1,0:T(4,128)(2,1)}), bf16[32,4,1152]{2,1,0:T(4,128)(2,1)S(1)}, u32[]{:S(2)}, u32[]{:S(2)}) async-start(bf16[32,4,1152]{2,1,0:T(4,128)(2,1)} %add.2), calls=%async_computation.1 | async-start | bytes 589824 | tf_op jit(solution)/shard_map/all_to_all | solution.py:261
  48.1 0.5 expand.3
  48.6 0.7 scatter.6
  49.3 2.6 %collective-permute-start.11 = (bf16[1024,128]{1,0:T(8,128)(2,1)S(1)}, bf16[1024,128]{1,0:T(8,128)(2,1)S(1)}, u32[]{:S(2)}, u32[]{:S(2)}) collective-permute-start(bf16[1024,128]{1,0:T(8,128)(2,1)S(1)} %scatter.6), channel_id=1, source_target_pairs={{0,4},{4,0},{1,5},{5,1},{2,6},{6,2},{3,7},{7,3},{8,12},{12,8},{9,1... | collective-permute-start | bytes 786440 | tf_op jit(solution)/shard_map/ppermute | solution.py:280
  51.9 1.2 %scatter.7 = (bf16[1024,128]{1,0:T(8,128)(2,1)S(1)}, bf16[1024,128]{1,0:T(8,128)(2,1)S(1)}) custom-call(bf16[4,5,128,128]{3,2,1,0:T(8,128)(2,1)S(1)} %get-tuple-element.112.refs_0_, f32[4,5,8,128]{3,2,1,0:T(8,128)S(1)} %get-tuple-element.113.refs_1_, bf16[4,3,128,128]{3,2,1,0:T(8,128)(2,1)S(1)} %get-tuple-element.114.refs_2_, ...), custom_call_target="tpu_custom_call" | custom-call | flops 1000 | bytes 1000 | tf_op jit(solution)/shard_map/scatter/pallas_call | solution.py:214
  53.1 0.1 collective-permute-start.12
  53.2 0.5 collective-permute-start.13
  53.7 0.7 scatter.8
  54.4 0.3 collective-permute-done.12.refs_4_
  54.8 0.4 collective-permute-done.13.refs_5_
  55.1 1.9 %scatter.9 = (bf16[1024,128]{1,0:T(8,128)(2,1)}, bf16[1024,128]{1,0:T(8,128)(2,1)S(1)}) custom-call(bf16[4,5,128,128]{3,2,1,0:T(8,128)(2,1)S(1)} %get-tuple-element.104.refs_0_, f32[4,5,8,128]{3,2,1,0:T(8,128)S(1)} %get-tuple-element.105.refs_1_, bf16[4,3,128,128]{3,2,1,0:T(8,128)(2,1)S(1)} %get-tuple-element.106.refs_2_, ...), custom_call_target="tpu_custom_call" | custom-call | flops 1000 | bytes 1000 | tf_op jit(solution)/shard_map/scatter/pallas_call | solution.py:214
  57.0 0.7 scatter.10
  57.7 0.0 copy-start.3
  57.7 0.2 collective-permute-start.14
  57.9 3.0 %collective-permute-start.17 = (bf16[1024,128]{1,0:T(8,128)(2,1)S(1)}, bf16[1024,128]{1,0:T(8,128)(2,1)S(1)}, u32[]{:S(2)}, u32[]{:S(2)}) collective-permute-start(bf16[1024,128]{1,0:T(8,128)(2,1)S(1)} %scatter.8), channel_id=1, source_target_pairs={{0,16},{8,24},{16,0},{24,8},{1,17},{9,25},{17,1},{25,9},{2,18},{10... | collective-permute-start | bytes 786440 | tf_op jit(solution)/shard_map/ppermute | solution.py:298
  61.0 0.3 collective-permute-start.15
  61.2 2.4 %collective-permute-start.16 = (bf16[1024,128]{1,0:T(8,128)(2,1)S(1)}, bf16[1024,128]{1,0:T(8,128)(2,1)S(1)}, u32[]{:S(2)}, u32[]{:S(2)}) collective-permute-start(bf16[1024,128]{1,0:T(8,128)(2,1)S(1)} %get-tuple-element.118), channel_id=1, source_target_pairs={{0,24},{8,0},{16,8},{24,16},{1,25},{9,1},{17,9},{25,17},{2,26},{10... | collective-permute-start | bytes 786440 | tf_op jit(solution)/shard_map/ppermute | solution.py:302
  63.6 0.7 scatter.11.a_ref
  64.4 0.7 add.3
  65.0 2.2 %collective-permute-done.17.d_ref = bf16[1024,128]{1,0:T(8,128)(2,1)S(1)} collective-permute-done((bf16[1024,128]{1,0:T(8,128)(2,1)S(1)}, bf16[1024,128]{1,0:T(8,128)(2,1)S(1)}, u32[]{:S(2)}, u32[]{:S(2)}) %collective-permute-start.17) | collective-permute-done | bytes 262176 | tf_op jit(solution)/shard_map/ppermute | solution.py:298
  67.2 6.2 %collective-permute-done.15.b_ref = bf16[1024,128]{1,0:T(8,128)(2,1)S(1)} collective-permute-done((bf16[1024,128]{1,0:T(8,128)(2,1)}, bf16[1024,128]{1,0:T(8,128)(2,1)S(1)}, u32[]{:S(2)}, u32[]{:S(2)}) %collective-permute-start.15) | collective-permute-done | bytes 262176 | tf_op jit(solution)/shard_map/ppermute | solution.py:301
  73.5 1.3 %update.1 = (f32[1024,128]{1,0:T(8,128)}, f32[8,128]{1,0:T(8,128)}) custom-call(bf16[1024,128]{1,0:T(8,128)(2,1)S(1)} %scatter.11.a_ref, bf16[1024,128]{1,0:T(8,128)(2,1)S(1)} %collective-permute-done.15.b_ref, bf16[1024,128]{1,0:T(8,128)(2,1)S(1)} %collective-permute-done.16.c_ref, bf16[1024,128]{1,0:T(8,128)(2,1)S(1)} %collective-permute-done.17.d_ref, ...), custom_call_target="tpu_custom_call" | custom-call | flops 1000 | bytes 1000 | tf_op jit(solution)/shard_map/update/pallas_call | solution.py:214
  (28 shorter events, 0.1 us)
Async XLA Ops:
  0.6 0.8 %copy-start.7 = (s32[128,8,8]{0,2,1:T(8,128)S(1)}, s32[128,8,8]{0,2,1:T(8,128)}, u32[]{:S(2)}) copy-start(s32[128,8,8]{0,2,1:T(8,128)} %param.13) | copy-start | bytes 98308
  1.4 1.5 %copy-start = (bf16[1152,512]{1,0:T(8,128)(2,1)S(1)}, bf16[1152,512]{1,0:T(8,128)(2,1)}, u32[]{:S(2)}) copy-start(bf16[1152,512]{1,0:T(8,128)(2,1)} %down_ref.1) | copy-start | bytes 3538948
  1.4 1.6 %copy-start.1 = (bf16[512,1152]{1,0:T(8,128)(2,1)S(1)}, bf16[512,1152]{1,0:T(8,128)(2,1)}, u32[]{:S(2)}) copy-start(bf16[512,1152]{1,0:T(8,128)(2,1)} %up_ref.1) | copy-start | bytes 3538948
  1.4 1.7 %copy-start.2 = (bf16[128,1152]{1,0:T(8,128)(2,1)S(1)}, bf16[128,1152]{1,0:T(8,128)(2,1)}, u32[]{:S(2)}) copy-start(bf16[128,1152]{1,0:T(8,128)(2,1)} %cot_ref.1) | copy-start | bytes 884740
  1.4 1.8 %copy-start.4 = (bf16[128,1152]{1,0:T(8,128)(2,1)S(1)}, bf16[128,1152]{1,0:T(8,128)(2,1)}, u32[]{:S(2)}) copy-start(bf16[128,1152]{1,0:T(8,128)(2,1)} %in_ref) | copy-start | bytes 884740
  3.2 4.5 %copy-start.5 = (f32[1152]{0:T(1024)S(1)}, f32[1152]{0:T(1024)}, u32[]{:S(2)}) copy-start(f32[1152]{0:T(1024)} %param.12) | copy-start | bytes 13828
  4.3 6.6 %collective-permute-start.3 = (bf16[128,2816]{1,0:T(8,128)(2,1)S(1)}, bf16[128,2816]{1,0:T(8,128)(2,1)S(1)}, u32[]{:S(2)}, u32[]{:S(2)}) collective-permute-start(bf16[128,2816]{1,0:T(8,128)(2,1)S(1)} %get-tuple-element.71.pack_ref), channel_id=1, source_target_pairs={{0,4},{4,0},{1,5},{5,1},{2,6},{6,2},{3,7},{7,3},{8,12},{12,8},{9,1... | collective-permute-start | bytes 2162696 | tf_op jit(solution)/shard_map/ppermute | solution.py:238
  8.8 8.0 %collective-permute-start.2 = (bf16[2,144,128]{2,1,0:T(8,128)(2,1)S(1)}, bf16[2,144,128]{2,1,0:T(8,128)(2,1)S(1)}, u32[]{:S(2)}, u32[]{:S(2)}) collective-permute-start(bf16[2,144,128]{2,1,0:T(8,128)(2,1)S(1)} %get-tuple-element.124), channel_id=1, source_target_pairs={{0,192},{64,0},{128,64},{192,128},{1,193},{65,1},{129,65},{193,129... | collective-permute-start | bytes 221192 | tf_op jit(solution)/shard_map/ppermute | solution.py:239
  9.9 6.9 %collective-permute-start.1 = (bf16[2,144,128]{2,1,0:T(8,128)(2,1)S(1)}, bf16[2,144,128]{2,1,0:T(8,128)(2,1)S(1)}, u32[]{:S(2)}, u32[]{:S(2)}) collective-permute-start(bf16[2,144,128]{2,1,0:T(8,128)(2,1)S(1)} %get-tuple-element.125), channel_id=1, source_target_pairs={{0,128},{64,192},{128,0},{192,64},{1,129},{65,193},{129,1},{193,65... | collective-permute-start | bytes 221192 | tf_op jit(solution)/shard_map/ppermute | solution.py:239
  10.2 6.9 %collective-permute-start = (bf16[2,144,128]{2,1,0:T(8,128)(2,1)S(1)}, bf16[2,144,128]{2,1,0:T(8,128)(2,1)S(1)}, u32[]{:S(2)}, u32[]{:S(2)}) collective-permute-start(bf16[2,144,128]{2,1,0:T(8,128)(2,1)S(1)} %get-tuple-element.126), channel_id=1, source_target_pairs={{0,64},{64,128},{128,192},{192,0},{1,65},{65,129},{129,193},{193,1... | collective-permute-start | bytes 221192 | tf_op jit(solution)/shard_map/ppermute | solution.py:239
  12.5 27.3 %all-to-all-start = ((bf16[4,128,1152]{2,1,0:T(8,128)(2,1)}), bf16[4,128,1152]{2,1,0:T(8,128)(2,1)S(1)}, u32[]{:S(2)}, u32[]{:S(2)}) async-start(bf16[4,128,1152]{2,1,0:T(8,128)(2,1)} %weights.1), calls=%async_computation | async-start | bytes 2359296 | tf_op jit(solution)/shard_map/all_to_all | solution.py:261
  17.2 10.0 %collective-permute-start.6 = (bf16[576,128]{1,0:T(8,128)(2,1)S(1)}, bf16[576,128]{1,0:T(8,128)(2,1)S(1)}, u32[]{:S(2)}, u32[]{:S(2)}) collective-permute-start(bf16[576,128]{1,0:T(8,128)(2,1)S(1)} %pad_maximum_fusion.refs_0_), channel_id=1, source_target_pairs={{0,2},{1,3},{2,0},{3,1},{4,6},{5,7},{6,4},{7,5},{8,10},{9,11},{10,... | collective-permute-start | bytes 442376 | tf_op jit(solution)/shard_map/ppermute | solution.py:251
  20.3 10.4 %collective-permute-start.5 = (bf16[576,128]{1,0:T(8,128)(2,1)S(1)}, bf16[576,128]{1,0:T(8,128)(2,1)S(1)}, u32[]{:S(2)}, u32[]{:S(2)}) collective-permute-start(bf16[576,128]{1,0:T(8,128)(2,1)S(1)} %pad_maximum_fusion.1), channel_id=1, source_target_pairs={{0,35},{1,34},{2,33},{3,32},{32,3},{33,2},{34,1},{35,0},{4,39},{5,... | collective-permute-start | bytes 442376 | tf_op jit(solution)/shard_map/ppermute | solution.py:248
  24.1 12.0 %collective-permute-start.4 = (bf16[576,128]{1,0:T(8,128)(2,1)S(1)}, bf16[576,128]{1,0:T(8,128)(2,1)S(1)}, u32[]{:S(2)}, u32[]{:S(2)}) collective-permute-start(bf16[576,128]{1,0:T(8,128)(2,1)S(1)} %pad_maximum_fusion.1), channel_id=1, source_target_pairs={{0,33},{1,32},{2,35},{3,34},{32,1},{33,0},{34,3},{35,2},{4,37},{5,... | collective-permute-start | bytes 442376 | tf_op jit(solution)/shard_map/ppermute | solution.py:248
  25.1 14.0 %collective-permute-start.7 = (bf16[576,128]{1,0:T(8,128)(2,1)S(1)}, bf16[576,128]{1,0:T(8,128)(2,1)S(1)}, u32[]{:S(2)}, u32[]{:S(2)}) collective-permute-start(bf16[576,128]{1,0:T(8,128)(2,1)S(1)} %pad_maximum_fusion.refs_0_), channel_id=1, source_target_pairs={{0,1},{1,0},{2,3},{3,2},{4,5},{5,4},{6,7},{7,6},{8,9},{9,8},{10,11... | collective-permute-start | bytes 442376 | tf_op jit(solution)/shard_map/ppermute | solution.py:251
  27.2 20.9 %collective-permute-start.10 = (bf16[576,128]{1,0:T(8,128)(2,1)S(1)}, bf16[576,128]{1,0:T(8,128)(2,1)S(1)}, u32[]{:S(2)}, u32[]{:S(2)}) collective-permute-start(bf16[576,128]{1,0:T(8,128)(2,1)S(1)} %collective-permute-done.6.refs_3_), channel_id=1, source_target_pairs={{0,1},{1,0},{2,3},{3,2},{4,5},{5,4},{6,7},{7,6},{8,9},{9,8},{10,11... | collective-permute-start | bytes 442376 | tf_op jit(solution)/shard_map/ppermute | solution.py:254
  30.7 17.4 %collective-permute-start.9 = (bf16[576,128]{1,0:T(8,128)(2,1)S(1)}, bf16[576,128]{1,0:T(8,128)(2,1)S(1)}, u32[]{:S(2)}, u32[]{:S(2)}) collective-permute-start(bf16[576,128]{1,0:T(8,128)(2,1)S(1)} %collective-permute-done.5.refs_2_), channel_id=1, source_target_pairs={{0,1},{1,0},{2,3},{3,2},{4,5},{5,4},{6,7},{7,6},{8,9},{9,8},{10,11... | collective-permute-start | bytes 442376 | tf_op jit(solution)/shard_map/ppermute | solution.py:254
  36.2 12.0 %collective-permute-start.8 = (bf16[576,128]{1,0:T(8,128)(2,1)S(1)}, bf16[576,128]{1,0:T(8,128)(2,1)S(1)}, u32[]{:S(2)}, u32[]{:S(2)}) collective-permute-start(bf16[576,128]{1,0:T(8,128)(2,1)S(1)} %collective-permute-done.4.refs_1_), channel_id=1, source_target_pairs={{0,1},{1,0},{2,3},{3,2},{4,5},{5,4},{6,7},{7,6},{8,9},{9,8},{10,11... | collective-permute-start | bytes 442376 | tf_op jit(solution)/shard_map/ppermute | solution.py:254
  40.7 23.6 %all-to-all-start.1 = ((bf16[32,4,1152]{2,1,0:T(4,128)(2,1)}), bf16[32,4,1152]{2,1,0:T(4,128)(2,1)S(1)}, u32[]{:S(2)}, u32[]{:S(2)}) async-start(bf16[32,4,1152]{2,1,0:T(4,128)(2,1)} %add.2), calls=%async_computation.1 | async-start | bytes 589824 | tf_op jit(solution)/shard_map/all_to_all | solution.py:261
  49.3 4.4 %collective-permute-start.11 = (bf16[1024,128]{1,0:T(8,128)(2,1)S(1)}, bf16[1024,128]{1,0:T(8,128)(2,1)S(1)}, u32[]{:S(2)}, u32[]{:S(2)}) collective-permute-start(bf16[1024,128]{1,0:T(8,128)(2,1)S(1)} %scatter.6), channel_id=1, source_target_pairs={{0,4},{4,0},{1,5},{5,1},{2,6},{6,2},{3,7},{7,3},{8,12},{12,8},{9,1... | collective-permute-start | bytes 786440 | tf_op jit(solution)/shard_map/ppermute | solution.py:280
  53.1 1.6 %collective-permute-start.12 = (bf16[1024,128]{1,0:T(8,128)(2,1)S(1)}, bf16[1024,128]{1,0:T(8,128)(2,1)S(1)}, u32[]{:S(2)}, u32[]{:S(2)}) collective-permute-start(bf16[1024,128]{1,0:T(8,128)(2,1)S(1)} %get-tuple-element.108), channel_id=1, source_target_pairs={{0,4},{4,0},{1,5},{5,1},{2,6},{6,2},{3,7},{7,3},{8,12},{12,8},{9,1... | collective-permute-start | bytes 786440 | tf_op jit(solution)/shard_map/ppermute | solution.py:280
  53.2 1.9 %collective-permute-start.13 = (bf16[1024,128]{1,0:T(8,128)(2,1)S(1)}, bf16[1024,128]{1,0:T(8,128)(2,1)S(1)}, u32[]{:S(2)}, u32[]{:S(2)}) collective-permute-start(bf16[1024,128]{1,0:T(8,128)(2,1)S(1)} %get-tuple-element.109), channel_id=1, source_target_pairs={{0,4},{4,0},{1,5},{5,1},{2,6},{6,2},{3,7},{7,3},{8,12},{12,8},{9,1... | collective-permute-start | bytes 786440 | tf_op jit(solution)/shard_map/ppermute | solution.py:280
  57.7 15.7 %copy-start.3 = (f32[1024,128]{1,0:T(8,128)S(1)}, f32[1024,128]{1,0:T(8,128)}, u32[]{:S(2)}) copy-start(f32[1024,128]{1,0:T(8,128)} %table_ref.1) | copy-start | bytes 1572868
  57.7 15.7 %copy-start.6 = (f32[1024]{0:T(1024)S(1)}, f32[1024]{0:T(1024)}, u32[]{:S(2)}) copy-start(f32[1024]{0:T(1024)} %param.15) | copy-start | bytes 12292
  57.7 5.9 %collective-permute-start.14 = (bf16[1024,128]{1,0:T(8,128)(2,1)S(1)}, bf16[1024,128]{1,0:T(8,128)(2,1)S(1)}, u32[]{:S(2)}, u32[]{:S(2)}) collective-permute-start(bf16[1024,128]{1,0:T(8,128)(2,1)S(1)} %scatter.10), channel_id=1, source_target_pairs={{0,4},{4,0},{1,5},{5,1},{2,6},{6,2},{3,7},{7,3},{8,12},{12,8},{9,1... | collective-permute-start | bytes 786440 | tf_op jit(solution)/shard_map/ppermute | solution.py:280
  57.9 9.3 %collective-permute-start.17 = (bf16[1024,128]{1,0:T(8,128)(2,1)S(1)}, bf16[1024,128]{1,0:T(8,128)(2,1)S(1)}, u32[]{:S(2)}, u32[]{:S(2)}) collective-permute-start(bf16[1024,128]{1,0:T(8,128)(2,1)S(1)} %scatter.8), channel_id=1, source_target_pairs={{0,16},{8,24},{16,0},{24,8},{1,17},{9,25},{17,1},{25,9},{2,18},{10... | collective-permute-start | bytes 786440 | tf_op jit(solution)/shard_map/ppermute | solution.py:298
  61.0 12.5 %collective-permute-start.15 = (bf16[1024,128]{1,0:T(8,128)(2,1)}, bf16[1024,128]{1,0:T(8,128)(2,1)S(1)}, u32[]{:S(2)}, u32[]{:S(2)}) collective-permute-start(bf16[1024,128]{1,0:T(8,128)(2,1)} %get-tuple-element.117), channel_id=1, source_target_pairs={{0,8},{8,16},{16,24},{24,0},{1,9},{9,17},{17,25},{25,1},{2,10},{10... | collective-permute-start | bytes 786440 | tf_op jit(solution)/shard_map/ppermute | solution.py:301
  61.2 12.2 %collective-permute-start.16 = (bf16[1024,128]{1,0:T(8,128)(2,1)S(1)}, bf16[1024,128]{1,0:T(8,128)(2,1)S(1)}, u32[]{:S(2)}, u32[]{:S(2)}) collective-permute-start(bf16[1024,128]{1,0:T(8,128)(2,1)S(1)} %get-tuple-element.118), channel_id=1, source_target_pairs={{0,24},{8,0},{16,8},{24,16},{1,25},{9,1},{17,9},{25,17},{2,26},{10... | collective-permute-start | bytes 786440 | tf_op jit(solution)/shard_map/ppermute | solution.py:302

commit v6 on v5

--- a/solution.py
+++ b/solution.py
@@ -158,11 +158,11 @@
 
 
 def scatter(d, looks, rows, out_ref, firsts=()):
-    base = iota((256, 128), 0).astype(F32)
+    base = iota((512, 128), 0).astype(F32)
     look = jnp.concatenate([ref[d].reshape(-1, EMB) for ref in looks], axis=0)
-    for i in range(ROWS // 256):
-        here = base + float(i * 256)
-        s = slice(i * 256, (i + 1) * 256)
+    for i in range(ROWS // 512):
+        here = base + float(i * 512)
+        s = slice(i * 512, (i + 1) * 512)
         hot = jnp.concatenate([(here == ref[d, j, 0:1, :]).astype(BF16) for ref in rows for j in range(ref.shape[1])], axis=1)
         total = dot(hot, look, 1, 0)
         for first in firsts:

time: 75.1 us -> 74.6 us (level)
  no operation moved by 1% of the time
where the time goes in v6:
time: 74.6 us; the launch traced here: 74.3 us
  starting transfers between devices  41.4 us (55%)
  waiting for transfers between devices  16.1 us (22%)
  Pallas kernels  14.8 us (20%)
  local copies, waits for them, and re-layouts  1.04 us (1%)
  between operations  0.81 us (1%)
    pallas_call x15, Pallas kernels, call(): pl.pallas_call(kernel, out_shape=outs, in_specs=[VMEM] * len(operands), o...  14.8 us
    all_to_all x2, starting transfers between devices, exchanged(): return lax.all_to_all(v, axes, split_axis=0, concat_axis=0, tiled=True)  11.7 us
    ppermute x3, starting transfers between devices, pass_on(): return lax.ppermute(v, 'zl', [(i, i ^ 1) for i in range(NZL)])  6.61 us
    ppermute x1, waiting for transfers between devices, per_device(): right = lax.ppermute(right, 'x', ring(NX, 1))  6.24 us
    ppermute x2, waiting for transfers between devices, cross(): return lax.ppermute(far, ('zh', 'zl'), [(i, 7 - i ^ m) for i in range(8)])  5.33 us
    ppermute x2, starting transfers between devices, cross(): return lax.ppermute(far, ('zh', 'zl'), [(i, 7 - i ^ m) for i in range(8)])  4.85 us
    ppermute x2, starting transfers between devices, line(): return lax.ppermute(near, 'zl', [(i, i ^ m) for i in range(NZL)])  3.79 us
    ppermute x4, starting transfers between devices, swapped(): return [lax.ppermute(v, 'c', swap) for v in vs]  3.41 us
  transfers between devices with their start and end apart: 20, of which 8 were waited for; matrix products, arithmetic and copies ran while one was open for 0% of the time, Pallas kernels for 15%

profile of v6, /device:TPU:1, one launch (start us, length us, event | category | flops | bytes accessed | tf_op | source)
XLA Modules:
  0.0 74.3 jit_solution(1680089552262020027)
XLA Ops:
  0.6 0.7 %copy-done.7 = s32[128,8,8]{0,2,1:T(8,128)S(1)} copy-done((s32[128,8,8]{0,2,1:T(8,128)S(1)}, s32[128,8,8]{0,2,1:T(8,128)}, u32[]{:S(2)}) %copy-start.7) | copy-done | bytes 32792
  1.4 1.5 %rank.1.meta_ref = bf16[8,16,128]{2,1,0:T(8,128)(2,1)S(1)} custom-call(s32[64,128]{1,0:T(8,128)S(1)} %bitcast.32), custom_call_target="tpu_custom_call" | custom-call | flops 2000000000 | bytes 100000 | tf_op jit(solution)/shard_map/rank/pallas_call | solution.py:214
  2.9 0.1 copy-done.1
  3.0 0.0 copy-done.2
  3.1 0.1 copy-done.4
  3.2 1.1 %hidden.1 = (bf16[128,2816]{1,0:T(8,128)(2,1)S(1)}, bf16[128,512]{1,0:T(8,128)(2,1)S(1)}, bf16[128,1024]{1,0:T(8,128)(2,1)S(1)}) custom-call(bf16[128,1152]{1,0:T(8,128)(2,1)S(1)} %copy-done.4, bf16[128,1152]{1,0:T(8,128)(2,1)S(1)} %copy-done.2, bf16[1152,512]{1,0:T(8,128)(2,1)S(1)} %copy-done, bf16[512,1152]{1,0:T(8,128)(2,1)S(1)} %copy-done.1), custom_call_target="tpu_custom_call" | custom-call | flops 500000000 | bytes 4000000 | tf_op jit(solution)/shard_map/hidden/pallas_call | solution.py:214
  4.3 3.3 %collective-permute-start.3 = (bf16[128,2816]{1,0:T(8,128)(2,1)S(1)}, bf16[128,2816]{1,0:T(8,128)(2,1)S(1)}, u32[]{:S(2)}, u32[]{:S(2)}) collective-permute-start(bf16[128,2816]{1,0:T(8,128)(2,1)S(1)} %get-tuple-element.71.pack_ref), channel_id=1, source_target_pairs={{0,4},{4,0},{1,5},{5,1},{2,6},{6,2},{3,7},{7,3},{8,12},{12,8},{9,1... | collective-permute-start | bytes 2162696 | tf_op jit(solution)/shard_map/ppermute | solution.py:238
  7.6 1.2 %pooled.1 = (bf16[128,128]{1,0:T(8,128)(2,1)}, bf16[4,2,144,128]{3,2,1,0:T(8,128)(2,1)S(1)}) custom-call(bf16[128,1152]{1,0:T(8,128)(2,1)S(1)} %copy-done.2, bf16[128,1024]{1,0:T(8,128)(2,1)S(1)} %get-tuple-element.68.both_ref, bf16[1152,512]{1,0:T(8,128)(2,1)S(1)} %copy-done, bf16[512,1152]{1,0:T(8,128)(2,1)S(1)} %copy-done.1, f32[9,128]{1,0:T(8,128)S(1)} %bitcast.30, ...), custom_call_target="tpu_custom_call" | custom-call | flops 300000000 | bytes 4000000 | tf_op jit(solution)/shard_map/pooled/pallas_call | solution.py:214
  8.8 1.1 %collective-permute-start.2 = (bf16[2,144,128]{2,1,0:T(8,128)(2,1)S(1)}, bf16[2,144,128]{2,1,0:T(8,128)(2,1)S(1)}, u32[]{:S(2)}, u32[]{:S(2)}) collective-permute-start(bf16[2,144,128]{2,1,0:T(8,128)(2,1)S(1)} %get-tuple-element.124), channel_id=1, source_target_pairs={{0,192},{64,0},{128,64},{192,128},{1,193},{65,1},{129,65},{193,129... | collective-permute-start | bytes 221192 | tf_op jit(solution)/shard_map/ppermute | solution.py:239
  9.9 0.4 collective-permute-start.1
  10.2 0.7 collective-permute-start
  10.9 1.6 %weights.1 = bf16[4,128,1152]{2,1,0:T(8,128)(2,1)} custom-call(bf16[128,2816]{1,0:T(8,128)(2,1)S(1)} %get-tuple-element.71.pack_ref, bf16[128,512]{1,0:T(8,128)(2,1)S(1)} %get-tuple-element.72.cols_ref, bf16[128,2816]{1,0:T(8,128)(2,1)S(1)} %collective-permute-done.3.other_ref), custom_call_target="tpu_custom_call" | custom-call | flops 300000000 | bytes 3000000 | tf_op jit(solution)/shard_map/weights/pallas_call | solution.py:214
  12.5 4.3 %all-to-all-start = ((bf16[4,128,1152]{2,1,0:T(8,128)(2,1)}), bf16[4,128,1152]{2,1,0:T(8,128)(2,1)S(1)}, u32[]{:S(2)}, u32[]{:S(2)}) async-start(bf16[4,128,1152]{2,1,0:T(8,128)(2,1)} %weights.1), calls=%async_computation | async-start | bytes 2359296 | tf_op jit(solution)/shard_map/all_to_all | solution.py:261
  16.8 0.4 collective-permute-done
  17.2 3.0 %collective-permute-start.6 = (bf16[576,128]{1,0:T(8,128)(2,1)S(1)}, bf16[576,128]{1,0:T(8,128)(2,1)S(1)}, u32[]{:S(2)}, u32[]{:S(2)}) collective-permute-start(bf16[576,128]{1,0:T(8,128)(2,1)S(1)} %pad_maximum_fusion.refs_0_), channel_id=1, source_target_pairs={{0,2},{1,3},{2,0},{3,1},{4,6},{5,7},{6,4},{7,5},{8,10},{9,11},{10,... | collective-permute-start | bytes 442376 | tf_op jit(solution)/shard_map/ppermute | solution.py:251
  20.3 3.8 %collective-permute-start.5 = (bf16[576,128]{1,0:T(8,128)(2,1)S(1)}, bf16[576,128]{1,0:T(8,128)(2,1)S(1)}, u32[]{:S(2)}, u32[]{:S(2)}) collective-permute-start(bf16[576,128]{1,0:T(8,128)(2,1)S(1)} %pad_maximum_fusion.1), channel_id=1, source_target_pairs={{0,35},{1,34},{2,33},{3,32},{32,3},{33,2},{34,1},{35,0},{4,39},{5,... | collective-permute-start | bytes 442376 | tf_op jit(solution)/shard_map/ppermute | solution.py:248
  24.1 1.0 %collective-permute-start.4 = (bf16[576,128]{1,0:T(8,128)(2,1)S(1)}, bf16[576,128]{1,0:T(8,128)(2,1)S(1)}, u32[]{:S(2)}, u32[]{:S(2)}) collective-permute-start(bf16[576,128]{1,0:T(8,128)(2,1)S(1)} %pad_maximum_fusion.1), channel_id=1, source_target_pairs={{0,33},{1,32},{2,35},{3,34},{32,1},{33,0},{34,3},{35,2},{4,37},{5,... | collective-permute-start | bytes 442376 | tf_op jit(solution)/shard_map/ppermute | solution.py:248
  25.1 0.7 collective-permute-start.7
  25.9 1.3 %collective-permute-done.6.refs_3_ = bf16[576,128]{1,0:T(8,128)(2,1)S(1)} collective-permute-done((bf16[576,128]{1,0:T(8,128)(2,1)S(1)}, bf16[576,128]{1,0:T(8,128)(2,1)S(1)}, u32[]{:S(2)}, u32[]{:S(2)}) %collective-permute-start.6) | collective-permute-done | bytes 147488 | tf_op jit(solution)/shard_map/ppermute | solution.py:251
  27.2 1.1 %collective-permute-start.10 = (bf16[576,128]{1,0:T(8,128)(2,1)S(1)}, bf16[576,128]{1,0:T(8,128)(2,1)S(1)}, u32[]{:S(2)}, u32[]{:S(2)}) collective-permute-start(bf16[576,128]{1,0:T(8,128)(2,1)S(1)} %collective-permute-done.6.refs_3_), channel_id=1, source_target_pairs={{0,1},{1,0},{2,3},{3,2},{4,5},{5,4},{6,7},{7,6},{8,9},{9,8},{10,11... | collective-permute-start | bytes 442376 | tf_op jit(solution)/shard_map/ppermute | solution.py:254
  28.2 2.5 %collective-permute-done.5.refs_2_ = bf16[576,128]{1,0:T(8,128)(2,1)S(1)} collective-permute-done((bf16[576,128]{1,0:T(8,128)(2,1)S(1)}, bf16[576,128]{1,0:T(8,128)(2,1)S(1)}, u32[]{:S(2)}, u32[]{:S(2)}) %collective-permute-start.5) | collective-permute-done | bytes 147488 | tf_op jit(solution)/shard_map/ppermute | solution.py:248
  30.7 2.6 %collective-permute-start.9 = (bf16[576,128]{1,0:T(8,128)(2,1)S(1)}, bf16[576,128]{1,0:T(8,128)(2,1)S(1)}, u32[]{:S(2)}, u32[]{:S(2)}) collective-permute-start(bf16[576,128]{1,0:T(8,128)(2,1)S(1)} %collective-permute-done.5.refs_2_), channel_id=1, source_target_pairs={{0,1},{1,0},{2,3},{3,2},{4,5},{5,4},{6,7},{7,6},{8,9},{9,8},{10,11... | collective-permute-start | bytes 442376 | tf_op jit(solution)/shard_map/ppermute | solution.py:254
  33.3 2.8 %collective-permute-done.4.refs_1_ = bf16[576,128]{1,0:T(8,128)(2,1)S(1)} collective-permute-done((bf16[576,128]{1,0:T(8,128)(2,1)S(1)}, bf16[576,128]{1,0:T(8,128)(2,1)S(1)}, u32[]{:S(2)}, u32[]{:S(2)}) %collective-permute-start.4) | collective-permute-done | bytes 147488 | tf_op jit(solution)/shard_map/ppermute | solution.py:248
  36.2 3.0 %collective-permute-start.8 = (bf16[576,128]{1,0:T(8,128)(2,1)S(1)}, bf16[576,128]{1,0:T(8,128)(2,1)S(1)}, u32[]{:S(2)}, u32[]{:S(2)}) collective-permute-start(bf16[576,128]{1,0:T(8,128)(2,1)S(1)} %collective-permute-done.4.refs_1_), channel_id=1, source_target_pairs={{0,1},{1,0},{2,3},{3,2},{4,5},{5,4},{6,7},{7,6},{8,9},{9,8},{10,11... | collective-permute-start | bytes 442376 | tf_op jit(solution)/shard_map/ppermute | solution.py:254
  39.1 0.7 expand.2
  39.8 0.9 %add.2 = bf16[32,4,1152]{2,1,0:T(4,128)(2,1)} custom-call(bf16[4,128,1152]{2,1,0:T(8,128)(2,1)S(1)} %all-to-all-done.in_ref), custom_call_target="tpu_custom_call" | custom-call | flops 1000 | bytes 1000 | tf_op jit(solution)/shard_map/add/pallas_call | solution.py:214
  40.7 7.4 %all-to-all-start.1 = ((bf16[32,4,1152]{2,1,0:T(4,128)(2,1)}), bf16[32,4,1152]{2,1,0:T(4,128)(2,1)S(1)}, u32[]{:S(2)}, u32[]{:S(2)}) async-start(bf16[32,4,1152]{2,1,0:T(4,128)(2,1)} %add.2), calls=%async_computation.1 | async-start | bytes 589824 | tf_op jit(solution)/shard_map/all_to_all | solution.py:261
  48.1 0.5 expand.3
  48.6 0.7 scatter.6
  49.3 2.6 %collective-permute-start.11 = (bf16[1024,128]{1,0:T(8,128)(2,1)S(1)}, bf16[1024,128]{1,0:T(8,128)(2,1)S(1)}, u32[]{:S(2)}, u32[]{:S(2)}) collective-permute-start(bf16[1024,128]{1,0:T(8,128)(2,1)S(1)} %scatter.6), channel_id=1, source_target_pairs={{0,4},{4,0},{1,5},{5,1},{2,6},{6,2},{3,7},{7,3},{8,12},{12,8},{9,1... | collective-permute-start | bytes 786440 | tf_op jit(solution)/shard_map/ppermute | solution.py:280
  51.9 1.2 %scatter.7 = (bf16[1024,128]{1,0:T(8,128)(2,1)S(1)}, bf16[1024,128]{1,0:T(8,128)(2,1)S(1)}) custom-call(bf16[4,5,128,128]{3,2,1,0:T(8,128)(2,1)S(1)} %get-tuple-element.112.refs_0_, f32[4,5,8,128]{3,2,1,0:T(8,128)S(1)} %get-tuple-element.113.refs_1_, bf16[4,3,128,128]{3,2,1,0:T(8,128)(2,1)S(1)} %get-tuple-element.114.refs_2_, ...), custom_call_target="tpu_custom_call" | custom-call | flops 1000 | bytes 1000 | tf_op jit(solution)/shard_map/scatter/pallas_call | solution.py:214
  53.1 0.1 collective-permute-start.12
  53.2 0.5 collective-permute-start.13
  53.8 0.7 scatter.8
  54.5 0.3 collective-permute-done.12.refs_4_
  54.8 0.4 collective-permute-done.13.refs_5_
  55.1 1.4 %scatter.9 = (bf16[1024,128]{1,0:T(8,128)(2,1)}, bf16[1024,128]{1,0:T(8,128)(2,1)S(1)}) custom-call(bf16[4,5,128,128]{3,2,1,0:T(8,128)(2,1)S(1)} %get-tuple-element.104.refs_0_, f32[4,5,8,128]{3,2,1,0:T(8,128)S(1)} %get-tuple-element.105.refs_1_, bf16[4,3,128,128]{3,2,1,0:T(8,128)(2,1)S(1)} %get-tuple-element.106.refs_2_, ...), custom_call_target="tpu_custom_call" | custom-call | flops 1000 | bytes 1000 | tf_op jit(solution)/shard_map/scatter/pallas_call | solution.py:214
  56.5 0.7 scatter.10
  57.3 0.0 copy-start.3
  57.3 0.2 collective-permute-start.14
  57.5 3.0 %collective-permute-start.17 = (bf16[1024,128]{1,0:T(8,128)(2,1)S(1)}, bf16[1024,128]{1,0:T(8,128)(2,1)S(1)}, u32[]{:S(2)}, u32[]{:S(2)}) collective-permute-start(bf16[1024,128]{1,0:T(8,128)(2,1)S(1)} %scatter.8), channel_id=1, source_target_pairs={{0,16},{8,24},{16,0},{24,8},{1,17},{9,25},{17,1},{25,9},{2,18},{10... | collective-permute-start | bytes 786440 | tf_op jit(solution)/shard_map/ppermute | solution.py:298
  60.5 0.3 collective-permute-start.15
  60.8 2.4 %collective-permute-start.16 = (bf16[1024,128]{1,0:T(8,128)(2,1)S(1)}, bf16[1024,128]{1,0:T(8,128)(2,1)S(1)}, u32[]{:S(2)}, u32[]{:S(2)}) collective-permute-start(bf16[1024,128]{1,0:T(8,128)(2,1)S(1)} %get-tuple-element.118), channel_id=1, source_target_pairs={{0,24},{8,0},{16,8},{24,16},{1,25},{9,1},{17,9},{25,17},{2,26},{10... | collective-permute-start | bytes 786440 | tf_op jit(solution)/shard_map/ppermute | solution.py:302
  63.2 0.7 scatter.11.a_ref
  63.9 0.7 add.3
  64.6 2.2 %collective-permute-done.17.d_ref = bf16[1024,128]{1,0:T(8,128)(2,1)S(1)} collective-permute-done((bf16[1024,128]{1,0:T(8,128)(2,1)S(1)}, bf16[1024,128]{1,0:T(8,128)(2,1)S(1)}, u32[]{:S(2)}, u32[]{:S(2)}) %collective-permute-start.17) | collective-permute-done | bytes 262176 | tf_op jit(solution)/shard_map/ppermute | solution.py:298
  66.8 6.2 %collective-permute-done.15.b_ref = bf16[1024,128]{1,0:T(8,128)(2,1)S(1)} collective-permute-done((bf16[1024,128]{1,0:T(8,128)(2,1)}, bf16[1024,128]{1,0:T(8,128)(2,1)S(1)}, u32[]{:S(2)}, u32[]{:S(2)}) %collective-permute-start.15) | collective-permute-done | bytes 262176 | tf_op jit(solution)/shard_map/ppermute | solution.py:301
  73.0 1.3 %update.1 = (f32[1024,128]{1,0:T(8,128)}, f32[8,128]{1,0:T(8,128)}) custom-call(bf16[1024,128]{1,0:T(8,128)(2,1)S(1)} %scatter.11.a_ref, bf16[1024,128]{1,0:T(8,128)(2,1)S(1)} %collective-permute-done.15.b_ref, bf16[1024,128]{1,0:T(8,128)(2,1)S(1)} %collective-permute-done.16.c_ref, bf16[1024,128]{1,0:T(8,128)(2,1)S(1)} %collective-permute-done.17.d_ref, ...), custom_call_target="tpu_custom_call" | custom-call | flops 1000 | bytes 1000 | tf_op jit(solution)/shard_map/update/pallas_call | solution.py:214
  (28 shorter events, 0.1 us)
Async XLA Ops:
  0.6 0.8 %copy-start.7 = (s32[128,8,8]{0,2,1:T(8,128)S(1)}, s32[128,8,8]{0,2,1:T(8,128)}, u32[]{:S(2)}) copy-start(s32[128,8,8]{0,2,1:T(8,128)} %param.13) | copy-start | bytes 98308
  1.4 1.5 %copy-start = (bf16[1152,512]{1,0:T(8,128)(2,1)S(1)}, bf16[1152,512]{1,0:T(8,128)(2,1)}, u32[]{:S(2)}) copy-start(bf16[1152,512]{1,0:T(8,128)(2,1)} %down_ref.1) | copy-start | bytes 3538948
  1.4 1.6 %copy-start.1 = (bf16[512,1152]{1,0:T(8,128)(2,1)S(1)}, bf16[512,1152]{1,0:T(8,128)(2,1)}, u32[]{:S(2)}) copy-start(bf16[512,1152]{1,0:T(8,128)(2,1)} %up_ref.1) | copy-start | bytes 3538948
  1.4 1.7 %copy-start.2 = (bf16[128,1152]{1,0:T(8,128)(2,1)S(1)}, bf16[128,1152]{1,0:T(8,128)(2,1)}, u32[]{:S(2)}) copy-start(bf16[128,1152]{1,0:T(8,128)(2,1)} %cot_ref.1) | copy-start | bytes 884740
  1.4 1.8 %copy-start.4 = (bf16[128,1152]{1,0:T(8,128)(2,1)S(1)}, bf16[128,1152]{1,0:T(8,128)(2,1)}, u32[]{:S(2)}) copy-start(bf16[128,1152]{1,0:T(8,128)(2,1)} %in_ref) | copy-start | bytes 884740
  3.2 4.5 %copy-start.5 = (f32[1152]{0:T(1024)S(1)}, f32[1152]{0:T(1024)}, u32[]{:S(2)}) copy-start(f32[1152]{0:T(1024)} %param.12) | copy-start | bytes 13828
  4.3 6.6 %collective-permute-start.3 = (bf16[128,2816]{1,0:T(8,128)(2,1)S(1)}, bf16[128,2816]{1,0:T(8,128)(2,1)S(1)}, u32[]{:S(2)}, u32[]{:S(2)}) collective-permute-start(bf16[128,2816]{1,0:T(8,128)(2,1)S(1)} %get-tuple-element.71.pack_ref), channel_id=1, source_target_pairs={{0,4},{4,0},{1,5},{5,1},{2,6},{6,2},{3,7},{7,3},{8,12},{12,8},{9,1... | collective-permute-start | bytes 2162696 | tf_op jit(solution)/shard_map/ppermute | solution.py:238
  8.8 8.0 %collective-permute-start.2 = (bf16[2,144,128]{2,1,0:T(8,128)(2,1)S(1)}, bf16[2,144,128]{2,1,0:T(8,128)(2,1)S(1)}, u32[]{:S(2)}, u32[]{:S(2)}) collective-permute-start(bf16[2,144,128]{2,1,0:T(8,128)(2,1)S(1)} %get-tuple-element.124), channel_id=1, source_target_pairs={{0,192},{64,0},{128,64},{192,128},{1,193},{65,1},{129,65},{193,129... | collective-permute-start | bytes 221192 | tf_op jit(solution)/shard_map/ppermute | solution.py:239
  9.9 6.9 %collective-permute-start.1 = (bf16[2,144,128]{2,1,0:T(8,128)(2,1)S(1)}, bf16[2,144,128]{2,1,0:T(8,128)(2,1)S(1)}, u32[]{:S(2)}, u32[]{:S(2)}) collective-permute-start(bf16[2,144,128]{2,1,0:T(8,128)(2,1)S(1)} %get-tuple-element.125), channel_id=1, source_target_pairs={{0,128},{64,192},{128,0},{192,64},{1,129},{65,193},{129,1},{193,65... | collective-permute-start | bytes 221192 | tf_op jit(solution)/shard_map/ppermute | solution.py:239
  10.2 6.9 %collective-permute-start = (bf16[2,144,128]{2,1,0:T(8,128)(2,1)S(1)}, bf16[2,144,128]{2,1,0:T(8,128)(2,1)S(1)}, u32[]{:S(2)}, u32[]{:S(2)}) collective-permute-start(bf16[2,144,128]{2,1,0:T(8,128)(2,1)S(1)} %get-tuple-element.126), channel_id=1, source_target_pairs={{0,64},{64,128},{128,192},{192,0},{1,65},{65,129},{129,193},{193,1... | collective-permute-start | bytes 221192 | tf_op jit(solution)/shard_map/ppermute | solution.py:239
  12.5 27.3 %all-to-all-start = ((bf16[4,128,1152]{2,1,0:T(8,128)(2,1)}), bf16[4,128,1152]{2,1,0:T(8,128)(2,1)S(1)}, u32[]{:S(2)}, u32[]{:S(2)}) async-start(bf16[4,128,1152]{2,1,0:T(8,128)(2,1)} %weights.1), calls=%async_computation | async-start | bytes 2359296 | tf_op jit(solution)/shard_map/all_to_all | solution.py:261
  17.2 10.0 %collective-permute-start.6 = (bf16[576,128]{1,0:T(8,128)(2,1)S(1)}, bf16[576,128]{1,0:T(8,128)(2,1)S(1)}, u32[]{:S(2)}, u32[]{:S(2)}) collective-permute-start(bf16[576,128]{1,0:T(8,128)(2,1)S(1)} %pad_maximum_fusion.refs_0_), channel_id=1, source_target_pairs={{0,2},{1,3},{2,0},{3,1},{4,6},{5,7},{6,4},{7,5},{8,10},{9,11},{10,... | collective-permute-start | bytes 442376 | tf_op jit(solution)/shard_map/ppermute | solution.py:251
  20.3 10.4 %collective-permute-start.5 = (bf16[576,128]{1,0:T(8,128)(2,1)S(1)}, bf16[576,128]{1,0:T(8,128)(2,1)S(1)}, u32[]{:S(2)}, u32[]{:S(2)}) collective-permute-start(bf16[576,128]{1,0:T(8,128)(2,1)S(1)} %pad_maximum_fusion.1), channel_id=1, source_target_pairs={{0,35},{1,34},{2,33},{3,32},{32,3},{33,2},{34,1},{35,0},{4,39},{5,... | collective-permute-start | bytes 442376 | tf_op jit(solution)/shard_map/ppermute | solution.py:248
  24.1 12.0 %collective-permute-start.4 = (bf16[576,128]{1,0:T(8,128)(2,1)S(1)}, bf16[576,128]{1,0:T(8,128)(2,1)S(1)}, u32[]{:S(2)}, u32[]{:S(2)}) collective-permute-start(bf16[576,128]{1,0:T(8,128)(2,1)S(1)} %pad_maximum_fusion.1), channel_id=1, source_target_pairs={{0,33},{1,32},{2,35},{3,34},{32,1},{33,0},{34,3},{35,2},{4,37},{5,... | collective-permute-start | bytes 442376 | tf_op jit(solution)/shard_map/ppermute | solution.py:248
  25.1 14.0 %collective-permute-start.7 = (bf16[576,128]{1,0:T(8,128)(2,1)S(1)}, bf16[576,128]{1,0:T(8,128)(2,1)S(1)}, u32[]{:S(2)}, u32[]{:S(2)}) collective-permute-start(bf16[576,128]{1,0:T(8,128)(2,1)S(1)} %pad_maximum_fusion.refs_0_), channel_id=1, source_target_pairs={{0,1},{1,0},{2,3},{3,2},{4,5},{5,4},{6,7},{7,6},{8,9},{9,8},{10,11... | collective-permute-start | bytes 442376 | tf_op jit(solution)/shard_map/ppermute | solution.py:251
  27.2 20.9 %collective-permute-start.10 = (bf16[576,128]{1,0:T(8,128)(2,1)S(1)}, bf16[576,128]{1,0:T(8,128)(2,1)S(1)}, u32[]{:S(2)}, u32[]{:S(2)}) collective-permute-start(bf16[576,128]{1,0:T(8,128)(2,1)S(1)} %collective-permute-done.6.refs_3_), channel_id=1, source_target_pairs={{0,1},{1,0},{2,3},{3,2},{4,5},{5,4},{6,7},{7,6},{8,9},{9,8},{10,11... | collective-permute-start | bytes 442376 | tf_op jit(solution)/shard_map/ppermute | solution.py:254
  30.7 17.4 %collective-permute-start.9 = (bf16[576,128]{1,0:T(8,128)(2,1)S(1)}, bf16[576,128]{1,0:T(8,128)(2,1)S(1)}, u32[]{:S(2)}, u32[]{:S(2)}) collective-permute-start(bf16[576,128]{1,0:T(8,128)(2,1)S(1)} %collective-permute-done.5.refs_2_), channel_id=1, source_target_pairs={{0,1},{1,0},{2,3},{3,2},{4,5},{5,4},{6,7},{7,6},{8,9},{9,8},{10,11... | collective-permute-start | bytes 442376 | tf_op jit(solution)/shard_map/ppermute | solution.py:254
  36.2 12.0 %collective-permute-start.8 = (bf16[576,128]{1,0:T(8,128)(2,1)S(1)}, bf16[576,128]{1,0:T(8,128)(2,1)S(1)}, u32[]{:S(2)}, u32[]{:S(2)}) collective-permute-start(bf16[576,128]{1,0:T(8,128)(2,1)S(1)} %collective-permute-done.4.refs_1_), channel_id=1, source_target_pairs={{0,1},{1,0},{2,3},{3,2},{4,5},{5,4},{6,7},{7,6},{8,9},{9,8},{10,11... | collective-permute-start | bytes 442376 | tf_op jit(solution)/shard_map/ppermute | solution.py:254
  40.7 23.2 %all-to-all-start.1 = ((bf16[32,4,1152]{2,1,0:T(4,128)(2,1)}), bf16[32,4,1152]{2,1,0:T(4,128)(2,1)S(1)}, u32[]{:S(2)}, u32[]{:S(2)}) async-start(bf16[32,4,1152]{2,1,0:T(4,128)(2,1)} %add.2), calls=%async_computation.1 | async-start | bytes 589824 | tf_op jit(solution)/shard_map/all_to_all | solution.py:261
  49.3 4.4 %collective-permute-start.11 = (bf16[1024,128]{1,0:T(8,128)(2,1)S(1)}, bf16[1024,128]{1,0:T(8,128)(2,1)S(1)}, u32[]{:S(2)}, u32[]{:S(2)}) collective-permute-start(bf16[1024,128]{1,0:T(8,128)(2,1)S(1)} %scatter.6), channel_id=1, source_target_pairs={{0,4},{4,0},{1,5},{5,1},{2,6},{6,2},{3,7},{7,3},{8,12},{12,8},{9,1... | collective-permute-start | bytes 786440 | tf_op jit(solution)/shard_map/ppermute | solution.py:280
  53.1 1.6 %collective-permute-start.12 = (bf16[1024,128]{1,0:T(8,128)(2,1)S(1)}, bf16[1024,128]{1,0:T(8,128)(2,1)S(1)}, u32[]{:S(2)}, u32[]{:S(2)}) collective-permute-start(bf16[1024,128]{1,0:T(8,128)(2,1)S(1)} %get-tuple-element.108), channel_id=1, source_target_pairs={{0,4},{4,0},{1,5},{5,1},{2,6},{6,2},{3,7},{7,3},{8,12},{12,8},{9,1... | collective-permute-start | bytes 786440 | tf_op jit(solution)/shard_map/ppermute | solution.py:280
  53.2 1.9 %collective-permute-start.13 = (bf16[1024,128]{1,0:T(8,128)(2,1)S(1)}, bf16[1024,128]{1,0:T(8,128)(2,1)S(1)}, u32[]{:S(2)}, u32[]{:S(2)}) collective-permute-start(bf16[1024,128]{1,0:T(8,128)(2,1)S(1)} %get-tuple-element.109), channel_id=1, source_target_pairs={{0,4},{4,0},{1,5},{5,1},{2,6},{6,2},{3,7},{7,3},{8,12},{12,8},{9,1... | collective-permute-start | bytes 786440 | tf_op jit(solution)/shard_map/ppermute | solution.py:280
  57.3 15.7 %copy-start.3 = (f32[1024,128]{1,0:T(8,128)S(1)}, f32[1024,128]{1,0:T(8,128)}, u32[]{:S(2)}) copy-start(f32[1024,128]{1,0:T(8,128)} %table_ref.1) | copy-start | bytes 1572868
  57.3 15.7 %copy-start.6 = (f32[1024]{0:T(1024)S(1)}, f32[1024]{0:T(1024)}, u32[]{:S(2)}) copy-start(f32[1024]{0:T(1024)} %param.15) | copy-start | bytes 12292
  57.3 5.9 %collective-permute-start.14 = (bf16[1024,128]{1,0:T(8,128)(2,1)S(1)}, bf16[1024,128]{1,0:T(8,128)(2,1)S(1)}, u32[]{:S(2)}, u32[]{:S(2)}) collective-permute-start(bf16[1024,128]{1,0:T(8,128)(2,1)S(1)} %scatter.10), channel_id=1, source_target_pairs={{0,4},{4,0},{1,5},{5,1},{2,6},{6,2},{3,7},{7,3},{8,12},{12,8},{9,1... | collective-permute-start | bytes 786440 | tf_op jit(solution)/shard_map/ppermute | solution.py:280
  57.5 9.2 %collective-permute-start.17 = (bf16[1024,128]{1,0:T(8,128)(2,1)S(1)}, bf16[1024,128]{1,0:T(8,128)(2,1)S(1)}, u32[]{:S(2)}, u32[]{:S(2)}) collective-permute-start(bf16[1024,128]{1,0:T(8,128)(2,1)S(1)} %scatter.8), channel_id=1, source_target_pairs={{0,16},{8,24},{16,0},{24,8},{1,17},{9,25},{17,1},{25,9},{2,18},{10... | collective-permute-start | bytes 786440 | tf_op jit(solution)/shard_map/ppermute | solution.py:298
  60.5 12.5 %collective-permute-start.15 = (bf16[1024,128]{1,0:T(8,128)(2,1)}, bf16[1024,128]{1,0:T(8,128)(2,1)S(1)}, u32[]{:S(2)}, u32[]{:S(2)}) collective-permute-start(bf16[1024,128]{1,0:T(8,128)(2,1)} %get-tuple-element.117), channel_id=1, source_target_pairs={{0,8},{8,16},{16,24},{24,0},{1,9},{9,17},{17,25},{25,1},{2,10},{10... | collective-permute-start | bytes 786440 | tf_op jit(solution)/shard_map/ppermute | solution.py:301
  60.8 12.2 %collective-permute-start.16 = (bf16[1024,128]{1,0:T(8,128)(2,1)S(1)}, bf16[1024,128]{1,0:T(8,128)(2,1)S(1)}, u32[]{:S(2)}, u32[]{:S(2)}) collective-permute-start(bf16[1024,128]{1,0:T(8,128)(2,1)S(1)} %get-tuple-element.118), channel_id=1, source_target_pairs={{0,24},{8,0},{16,8},{24,16},{1,25},{9,1},{17,9},{25,17},{2,26},{10... | collective-permute-start | bytes 786440 | tf_op jit(solution)/shard_map/ppermute | solution.py:302

commit v7 on v6

--- a/solution.py
+++ b/solution.py
@@ -158,11 +158,11 @@
 
 
 def scatter(d, looks, rows, out_ref, firsts=()):
-    base = iota((512, 128), 0).astype(F32)
+    base = iota((1024, 128), 0).astype(F32)
     look = jnp.concatenate([ref[d].reshape(-1, EMB) for ref in looks], axis=0)
-    for i in range(ROWS // 512):
-        here = base + float(i * 512)
-        s = slice(i * 512, (i + 1) * 512)
+    for i in range(ROWS // 1024):
+        here = base + float(i * 1024)
+        s = slice(i * 1024, (i + 1) * 1024)
         hot = jnp.concatenate([(here == ref[d, j, 0:1, :]).astype(BF16) for ref in rows for j in range(ref.shape[1])], axis=1)
         total = dot(hot, look, 1, 0)
         for first in firsts:

time: 74.6 us -> 75.2 us (level)
  no operation moved by 1% of the time
where the time goes in v7:
time: 75.2 us; the launch traced here: 74.8 us
  starting transfers between devices  41.4 us (55%)
  waiting for transfers between devices  16.1 us (21%)
  Pallas kernels  15.4 us (20%)
  local copies, waits for them, and re-layouts  1.04 us (1%)
  between operations  0.81 us (1%)
    pallas_call x15, Pallas kernels, call(): pl.pallas_call(kernel, out_shape=outs, in_specs=[VMEM] * len(operands), o...  15.4 us
    all_to_all x2, starting transfers between devices, exchanged(): return lax.all_to_all(v, axes, split_axis=0, concat_axis=0, tiled=True)  11.7 us
    ppermute x3, starting transfers between devices, pass_on(): return lax.ppermute(v, 'zl', [(i, i ^ 1) for i in range(NZL)])  6.61 us
    ppermute x1, waiting for transfers between devices, per_device(): right = lax.ppermute(right, 'x', ring(NX, 1))  6.23 us
    ppermute x2, waiting for transfers between devices, cross(): return lax.ppermute(far, ('zh', 'zl'), [(i, 7 - i ^ m) for i in range(8)])  5.33 us
    ppermute x2, starting transfers between devices, cross(): return lax.ppermute(far, ('zh', 'zl'), [(i, 7 - i ^ m) for i in range(8)])  4.85 us
    ppermute x2, starting transfers between devices, line(): return lax.ppermute(near, 'zl', [(i, i ^ m) for i in range(NZL)])  3.79 us
    ppermute x4, starting transfers between devices, swapped(): return [lax.ppermute(v, 'c', swap) for v in vs]  3.42 us
  transfers between devices with their start and end apart: 20, of which 8 were waited for; matrix products, arithmetic and copies ran while one was open for 0% of the time, Pallas kernels for 15%

profile of v7, /device:TPU:1, one launch (start us, length us, event | category | flops | bytes accessed | tf_op | source)
XLA Modules:
  0.0 74.8 jit_solution(4695638288624549386)
XLA Ops:
  0.6 0.7 %copy-done.7 = s32[128,8,8]{0,2,1:T(8,128)S(1)} copy-done((s32[128,8,8]{0,2,1:T(8,128)S(1)}, s32[128,8,8]{0,2,1:T(8,128)}, u32[]{:S(2)}) %copy-start.7) | copy-done | bytes 32792
  1.4 1.5 %rank.1.meta_ref = bf16[8,16,128]{2,1,0:T(8,128)(2,1)S(1)} custom-call(s32[64,128]{1,0:T(8,128)S(1)} %bitcast.32), custom_call_target="tpu_custom_call" | custom-call | flops 2000000000 | bytes 100000 | tf_op jit(solution)/shard_map/rank/pallas_call | solution.py:214
  2.9 0.1 copy-done.1
  3.0 0.0 copy-done.2
  3.1 0.1 copy-done.4
  3.2 1.1 %hidden.1 = (bf16[128,2816]{1,0:T(8,128)(2,1)S(1)}, bf16[128,512]{1,0:T(8,128)(2,1)S(1)}, bf16[128,1024]{1,0:T(8,128)(2,1)S(1)}) custom-call(bf16[128,1152]{1,0:T(8,128)(2,1)S(1)} %copy-done.4, bf16[128,1152]{1,0:T(8,128)(2,1)S(1)} %copy-done.2, bf16[1152,512]{1,0:T(8,128)(2,1)S(1)} %copy-done, bf16[512,1152]{1,0:T(8,128)(2,1)S(1)} %copy-done.1), custom_call_target="tpu_custom_call" | custom-call | flops 500000000 | bytes 4000000 | tf_op jit(solution)/shard_map/hidden/pallas_call | solution.py:214
  4.3 3.3 %collective-permute-start.3 = (bf16[128,2816]{1,0:T(8,128)(2,1)S(1)}, bf16[128,2816]{1,0:T(8,128)(2,1)S(1)}, u32[]{:S(2)}, u32[]{:S(2)}) collective-permute-start(bf16[128,2816]{1,0:T(8,128)(2,1)S(1)} %get-tuple-element.71.pack_ref), channel_id=1, source_target_pairs={{0,4},{4,0},{1,5},{5,1},{2,6},{6,2},{3,7},{7,3},{8,12},{12,8},{9,1... | collective-permute-start | bytes 2162696 | tf_op jit(solution)/shard_map/ppermute | solution.py:238
  7.6 1.2 %pooled.1 = (bf16[128,128]{1,0:T(8,128)(2,1)}, bf16[4,2,144,128]{3,2,1,0:T(8,128)(2,1)S(1)}) custom-call(bf16[128,1152]{1,0:T(8,128)(2,1)S(1)} %copy-done.2, bf16[128,1024]{1,0:T(8,128)(2,1)S(1)} %get-tuple-element.68.both_ref, bf16[1152,512]{1,0:T(8,128)(2,1)S(1)} %copy-done, bf16[512,1152]{1,0:T(8,128)(2,1)S(1)} %copy-done.1, f32[9,128]{1,0:T(8,128)S(1)} %bitcast.30, ...), custom_call_target="tpu_custom_call" | custom-call | flops 300000000 | bytes 4000000 | tf_op jit(solution)/shard_map/pooled/pallas_call | solution.py:214
  8.8 1.1 %collective-permute-start.2 = (bf16[2,144,128]{2,1,0:T(8,128)(2,1)S(1)}, bf16[2,144,128]{2,1,0:T(8,128)(2,1)S(1)}, u32[]{:S(2)}, u32[]{:S(2)}) collective-permute-start(bf16[2,144,128]{2,1,0:T(8,128)(2,1)S(1)} %get-tuple-element.124), channel_id=1, source_target_pairs={{0,192},{64,0},{128,64},{192,128},{1,193},{65,1},{129,65},{193,129... | collective-permute-start | bytes 221192 | tf_op jit(solution)/shard_map/ppermute | solution.py:239
  9.9 0.4 collective-permute-start.1
  10.2 0.7 collective-permute-start
  10.9 1.6 %weights.1 = bf16[4,128,1152]{2,1,0:T(8,128)(2,1)} custom-call(bf16[128,2816]{1,0:T(8,128)(2,1)S(1)} %get-tuple-element.71.pack_ref, bf16[128,512]{1,0:T(8,128)(2,1)S(1)} %get-tuple-element.72.cols_ref, bf16[128,2816]{1,0:T(8,128)(2,1)S(1)} %collective-permute-done.3.other_ref), custom_call_target="tpu_custom_call" | custom-call | flops 300000000 | bytes 3000000 | tf_op jit(solution)/shard_map/weights/pallas_call | solution.py:214
  12.5 4.3 %all-to-all-start = ((bf16[4,128,1152]{2,1,0:T(8,128)(2,1)}), bf16[4,128,1152]{2,1,0:T(8,128)(2,1)S(1)}, u32[]{:S(2)}, u32[]{:S(2)}) async-start(bf16[4,128,1152]{2,1,0:T(8,128)(2,1)} %weights.1), calls=%async_computation | async-start | bytes 2359296 | tf_op jit(solution)/shard_map/all_to_all | solution.py:261
  16.8 0.4 collective-permute-done
  17.2 3.0 %collective-permute-start.6 = (bf16[576,128]{1,0:T(8,128)(2,1)S(1)}, bf16[576,128]{1,0:T(8,128)(2,1)S(1)}, u32[]{:S(2)}, u32[]{:S(2)}) collective-permute-start(bf16[576,128]{1,0:T(8,128)(2,1)S(1)} %pad_maximum_fusion.refs_0_), channel_id=1, source_target_pairs={{0,2},{1,3},{2,0},{3,1},{4,6},{5,7},{6,4},{7,5},{8,10},{9,11},{10,... | collective-permute-start | bytes 442376 | tf_op jit(solution)/shard_map/ppermute | solution.py:251
  20.3 3.8 %collective-permute-start.5 = (bf16[576,128]{1,0:T(8,128)(2,1)S(1)}, bf16[576,128]{1,0:T(8,128)(2,1)S(1)}, u32[]{:S(2)}, u32[]{:S(2)}) collective-permute-start(bf16[576,128]{1,0:T(8,128)(2,1)S(1)} %pad_maximum_fusion.1), channel_id=1, source_target_pairs={{0,35},{1,34},{2,33},{3,32},{32,3},{33,2},{34,1},{35,0},{4,39},{5,... | collective-permute-start | bytes 442376 | tf_op jit(solution)/shard_map/ppermute | solution.py:248
  24.1 1.0 %collective-permute-start.4 = (bf16[576,128]{1,0:T(8,128)(2,1)S(1)}, bf16[576,128]{1,0:T(8,128)(2,1)S(1)}, u32[]{:S(2)}, u32[]{:S(2)}) collective-permute-start(bf16[576,128]{1,0:T(8,128)(2,1)S(1)} %pad_maximum_fusion.1), channel_id=1, source_target_pairs={{0,33},{1,32},{2,35},{3,34},{32,1},{33,0},{34,3},{35,2},{4,37},{5,... | collective-permute-start | bytes 442376 | tf_op jit(solution)/shard_map/ppermute | solution.py:248
  25.1 0.7 collective-permute-start.7
  25.9 1.3 %collective-permute-done.6.refs_3_ = bf16[576,128]{1,0:T(8,128)(2,1)S(1)} collective-permute-done((bf16[576,128]{1,0:T(8,128)(2,1)S(1)}, bf16[576,128]{1,0:T(8,128)(2,1)S(1)}, u32[]{:S(2)}, u32[]{:S(2)}) %collective-permute-start.6) | collective-permute-done | bytes 147488 | tf_op jit(solution)/shard_map/ppermute | solution.py:251
  27.2 1.1 %collective-permute-start.10 = (bf16[576,128]{1,0:T(8,128)(2,1)S(1)}, bf16[576,128]{1,0:T(8,128)(2,1)S(1)}, u32[]{:S(2)}, u32[]{:S(2)}) collective-permute-start(bf16[576,128]{1,0:T(8,128)(2,1)S(1)} %collective-permute-done.6.refs_3_), channel_id=1, source_target_pairs={{0,1},{1,0},{2,3},{3,2},{4,5},{5,4},{6,7},{7,6},{8,9},{9,8},{10,11... | collective-permute-start | bytes 442376 | tf_op jit(solution)/shard_map/ppermute | solution.py:254
  28.2 2.5 %collective-permute-done.5.refs_2_ = bf16[576,128]{1,0:T(8,128)(2,1)S(1)} collective-permute-done((bf16[576,128]{1,0:T(8,128)(2,1)S(1)}, bf16[576,128]{1,0:T(8,128)(2,1)S(1)}, u32[]{:S(2)}, u32[]{:S(2)}) %collective-permute-start.5) | collective-permute-done | bytes 147488 | tf_op jit(solution)/shard_map/ppermute | solution.py:248
  30.7 2.6 %collective-permute-start.9 = (bf16[576,128]{1,0:T(8,128)(2,1)S(1)}, bf16[576,128]{1,0:T(8,128)(2,1)S(1)}, u32[]{:S(2)}, u32[]{:S(2)}) collective-permute-start(bf16[576,128]{1,0:T(8,128)(2,1)S(1)} %collective-permute-done.5.refs_2_), channel_id=1, source_target_pairs={{0,1},{1,0},{2,3},{3,2},{4,5},{5,4},{6,7},{7,6},{8,9},{9,8},{10,11... | collective-permute-start | bytes 442376 | tf_op jit(solution)/shard_map/ppermute | solution.py:254
  33.3 2.8 %collective-permute-done.4.refs_1_ = bf16[576,128]{1,0:T(8,128)(2,1)S(1)} collective-permute-done((bf16[576,128]{1,0:T(8,128)(2,1)S(1)}, bf16[576,128]{1,0:T(8,128)(2,1)S(1)}, u32[]{:S(2)}, u32[]{:S(2)}) %collective-permute-start.4) | collective-permute-done | bytes 147488 | tf_op jit(solution)/shard_map/ppermute | solution.py:248
  36.2 3.0 %collective-permute-start.8 = (bf16[576,128]{1,0:T(8,128)(2,1)S(1)}, bf16[576,128]{1,0:T(8,128)(2,1)S(1)}, u32[]{:S(2)}, u32[]{:S(2)}) collective-permute-start(bf16[576,128]{1,0:T(8,128)(2,1)S(1)} %collective-permute-done.4.refs_1_), channel_id=1, source_target_pairs={{0,1},{1,0},{2,3},{3,2},{4,5},{5,4},{6,7},{7,6},{8,9},{9,8},{10,11... | collective-permute-start | bytes 442376 | tf_op jit(solution)/shard_map/ppermute | solution.py:254
  39.1 0.7 expand.2
  39.8 0.9 %add.2 = bf16[32,4,1152]{2,1,0:T(4,128)(2,1)} custom-call(bf16[4,128,1152]{2,1,0:T(8,128)(2,1)S(1)} %all-to-all-done.in_ref), custom_call_target="tpu_custom_call" | custom-call | flops 1000 | bytes 1000 | tf_op jit(solution)/shard_map/add/pallas_call | solution.py:214
  40.7 7.4 %all-to-all-start.1 = ((bf16[32,4,1152]{2,1,0:T(4,128)(2,1)}), bf16[32,4,1152]{2,1,0:T(4,128)(2,1)S(1)}, u32[]{:S(2)}, u32[]{:S(2)}) async-start(bf16[32,4,1152]{2,1,0:T(4,128)(2,1)} %add.2), calls=%async_computation.1 | async-start | bytes 589824 | tf_op jit(solution)/shard_map/all_to_all | solution.py:261
  48.1 0.5 expand.3
  48.6 0.7 scatter.6
  49.3 2.6 %collective-permute-start.11 = (bf16[1024,128]{1,0:T(8,128)(2,1)S(1)}, bf16[1024,128]{1,0:T(8,128)(2,1)S(1)}, u32[]{:S(2)}, u32[]{:S(2)}) collective-permute-start(bf16[1024,128]{1,0:T(8,128)(2,1)S(1)} %scatter.6), channel_id=1, source_target_pairs={{0,4},{4,0},{1,5},{5,1},{2,6},{6,2},{3,7},{7,3},{8,12},{12,8},{9,1... | collective-permute-start | bytes 786440 | tf_op jit(solution)/shard_map/ppermute | solution.py:280
  51.9 1.2 %scatter.7 = (bf16[1024,128]{1,0:T(8,128)(2,1)S(1)}, bf16[1024,128]{1,0:T(8,128)(2,1)S(1)}) custom-call(bf16[4,5,128,128]{3,2,1,0:T(8,128)(2,1)S(1)} %get-tuple-element.112.refs_0_, f32[4,5,8,128]{3,2,1,0:T(8,128)S(1)} %get-tuple-element.113.refs_1_, bf16[4,3,128,128]{3,2,1,0:T(8,128)(2,1)S(1)} %get-tuple-element.114.refs_2_, ...), custom_call_target="tpu_custom_call" | custom-call | flops 1000 | bytes 1000 | tf_op jit(solution)/shard_map/scatter/pallas_call | solution.py:214
  53.2 0.1 collective-permute-start.12
  53.3 0.5 collective-permute-start.13
  53.8 0.7 scatter.8
  54.5 0.3 collective-permute-done.12.refs_4_
  54.8 0.4 collective-permute-done.13.refs_5_
  55.1 1.9 %scatter.9 = (bf16[1024,128]{1,0:T(8,128)(2,1)}, bf16[1024,128]{1,0:T(8,128)(2,1)S(1)}) custom-call(bf16[4,5,128,128]{3,2,1,0:T(8,128)(2,1)S(1)} %get-tuple-element.104.refs_0_, f32[4,5,8,128]{3,2,1,0:T(8,128)S(1)} %get-tuple-element.105.refs_1_, bf16[4,3,128,128]{3,2,1,0:T(8,128)(2,1)S(1)} %get-tuple-element.106.refs_2_, ...), custom_call_target="tpu_custom_call" | custom-call | flops 1000 | bytes 1000 | tf_op jit(solution)/shard_map/scatter/pallas_call | solution.py:214
  57.1 0.7 scatter.10
  57.8 0.0 copy-start.3
  57.8 0.2 collective-permute-start.14
  58.1 3.0 %collective-permute-start.17 = (bf16[1024,128]{1,0:T(8,128)(2,1)S(1)}, bf16[1024,128]{1,0:T(8,128)(2,1)S(1)}, u32[]{:S(2)}, u32[]{:S(2)}) collective-permute-start(bf16[1024,128]{1,0:T(8,128)(2,1)S(1)} %scatter.8), channel_id=1, source_target_pairs={{0,16},{8,24},{16,0},{24,8},{1,17},{9,25},{17,1},{25,9},{2,18},{10... | collective-permute-start | bytes 786440 | tf_op jit(solution)/shard_map/ppermute | solution.py:298
  61.1 0.3 collective-permute-start.15
  61.3 2.4 %collective-permute-start.16 = (bf16[1024,128]{1,0:T(8,128)(2,1)S(1)}, bf16[1024,128]{1,0:T(8,128)(2,1)S(1)}, u32[]{:S(2)}, u32[]{:S(2)}) collective-permute-start(bf16[1024,128]{1,0:T(8,128)(2,1)S(1)} %get-tuple-element.118), channel_id=1, source_target_pairs={{0,24},{8,0},{16,8},{24,16},{1,25},{9,1},{17,9},{25,17},{2,26},{10... | collective-permute-start | bytes 786440 | tf_op jit(solution)/shard_map/ppermute | solution.py:302
  63.7 0.7 scatter.11.a_ref
  64.5 0.7 add.3
  65.1 2.2 %collective-permute-done.17.d_ref = bf16[1024,128]{1,0:T(8,128)(2,1)S(1)} collective-permute-done((bf16[1024,128]{1,0:T(8,128)(2,1)S(1)}, bf16[1024,128]{1,0:T(8,128)(2,1)S(1)}, u32[]{:S(2)}, u32[]{:S(2)}) %collective-permute-start.17) | collective-permute-done | bytes 262176 | tf_op jit(solution)/shard_map/ppermute | solution.py:298
  67.3 6.2 %collective-permute-done.15.b_ref = bf16[1024,128]{1,0:T(8,128)(2,1)S(1)} collective-permute-done((bf16[1024,128]{1,0:T(8,128)(2,1)}, bf16[1024,128]{1,0:T(8,128)(2,1)S(1)}, u32[]{:S(2)}, u32[]{:S(2)}) %collective-permute-start.15) | collective-permute-done | bytes 262176 | tf_op jit(solution)/shard_map/ppermute | solution.py:301
  73.6 1.3 %update.1 = (f32[1024,128]{1,0:T(8,128)}, f32[8,128]{1,0:T(8,128)}) custom-call(bf16[1024,128]{1,0:T(8,128)(2,1)S(1)} %scatter.11.a_ref, bf16[1024,128]{1,0:T(8,128)(2,1)S(1)} %collective-permute-done.15.b_ref, bf16[1024,128]{1,0:T(8,128)(2,1)S(1)} %collective-permute-done.16.c_ref, bf16[1024,128]{1,0:T(8,128)(2,1)S(1)} %collective-permute-done.17.d_ref, ...), custom_call_target="tpu_custom_call" | custom-call | flops 1000 | bytes 1000 | tf_op jit(solution)/shard_map/update/pallas_call | solution.py:214
  (28 shorter events, 0.1 us)
Async XLA Ops:
  0.6 0.8 %copy-start.7 = (s32[128,8,8]{0,2,1:T(8,128)S(1)}, s32[128,8,8]{0,2,1:T(8,128)}, u32[]{:S(2)}) copy-start(s32[128,8,8]{0,2,1:T(8,128)} %param.13) | copy-start | bytes 98308
  1.4 1.5 %copy-start = (bf16[1152,512]{1,0:T(8,128)(2,1)S(1)}, bf16[1152,512]{1,0:T(8,128)(2,1)}, u32[]{:S(2)}) copy-start(bf16[1152,512]{1,0:T(8,128)(2,1)} %down_ref.1) | copy-start | bytes 3538948
  1.4 1.6 %copy-start.1 = (bf16[512,1152]{1,0:T(8,128)(2,1)S(1)}, bf16[512,1152]{1,0:T(8,128)(2,1)}, u32[]{:S(2)}) copy-start(bf16[512,1152]{1,0:T(8,128)(2,1)} %up_ref.1) | copy-start | bytes 3538948
  1.4 1.7 %copy-start.2 = (bf16[128,1152]{1,0:T(8,128)(2,1)S(1)}, bf16[128,1152]{1,0:T(8,128)(2,1)}, u32[]{:S(2)}) copy-start(bf16[128,1152]{1,0:T(8,128)(2,1)} %cot_ref.1) | copy-start | bytes 884740
  1.4 1.8 %copy-start.4 = (bf16[128,1152]{1,0:T(8,128)(2,1)S(1)}, bf16[128,1152]{1,0:T(8,128)(2,1)}, u32[]{:S(2)}) copy-start(bf16[128,1152]{1,0:T(8,128)(2,1)} %in_ref) | copy-start | bytes 884740
  3.2 4.5 %copy-start.5 = (f32[1152]{0:T(1024)S(1)}, f32[1152]{0:T(1024)}, u32[]{:S(2)}) copy-start(f32[1152]{0:T(1024)} %param.12) | copy-start | bytes 13828
  4.3 6.6 %collective-permute-start.3 = (bf16[128,2816]{1,0:T(8,128)(2,1)S(1)}, bf16[128,2816]{1,0:T(8,128)(2,1)S(1)}, u32[]{:S(2)}, u32[]{:S(2)}) collective-permute-start(bf16[128,2816]{1,0:T(8,128)(2,1)S(1)} %get-tuple-element.71.pack_ref), channel_id=1, source_target_pairs={{0,4},{4,0},{1,5},{5,1},{2,6},{6,2},{3,7},{7,3},{8,12},{12,8},{9,1... | collective-permute-start | bytes 2162696 | tf_op jit(solution)/shard_map/ppermute | solution.py:238
  8.8 8.0 %collective-permute-start.2 = (bf16[2,144,128]{2,1,0:T(8,128)(2,1)S(1)}, bf16[2,144,128]{2,1,0:T(8,128)(2,1)S(1)}, u32[]{:S(2)}, u32[]{:S(2)}) collective-permute-start(bf16[2,144,128]{2,1,0:T(8,128)(2,1)S(1)} %get-tuple-element.124), channel_id=1, source_target_pairs={{0,192},{64,0},{128,64},{192,128},{1,193},{65,1},{129,65},{193,129... | collective-permute-start | bytes 221192 | tf_op jit(solution)/shard_map/ppermute | solution.py:239
  9.9 6.9 %collective-permute-start.1 = (bf16[2,144,128]{2,1,0:T(8,128)(2,1)S(1)}, bf16[2,144,128]{2,1,0:T(8,128)(2,1)S(1)}, u32[]{:S(2)}, u32[]{:S(2)}) collective-permute-start(bf16[2,144,128]{2,1,0:T(8,128)(2,1)S(1)} %get-tuple-element.125), channel_id=1, source_target_pairs={{0,128},{64,192},{128,0},{192,64},{1,129},{65,193},{129,1},{193,65... | collective-permute-start | bytes 221192 | tf_op jit(solution)/shard_map/ppermute | solution.py:239
  10.2 6.9 %collective-permute-start = (bf16[2,144,128]{2,1,0:T(8,128)(2,1)S(1)}, bf16[2,144,128]{2,1,0:T(8,128)(2,1)S(1)}, u32[]{:S(2)}, u32[]{:S(2)}) collective-permute-start(bf16[2,144,128]{2,1,0:T(8,128)(2,1)S(1)} %get-tuple-element.126), channel_id=1, source_target_pairs={{0,64},{64,128},{128,192},{192,0},{1,65},{65,129},{129,193},{193,1... | collective-permute-start | bytes 221192 | tf_op jit(solution)/shard_map/ppermute | solution.py:239
  12.5 27.3 %all-to-all-start = ((bf16[4,128,1152]{2,1,0:T(8,128)(2,1)}), bf16[4,128,1152]{2,1,0:T(8,128)(2,1)S(1)}, u32[]{:S(2)}, u32[]{:S(2)}) async-start(bf16[4,128,1152]{2,1,0:T(8,128)(2,1)} %weights.1), calls=%async_computation | async-start | bytes 2359296 | tf_op jit(solution)/shard_map/all_to_all | solution.py:261
  17.2 10.0 %collective-permute-start.6 = (bf16[576,128]{1,0:T(8,128)(2,1)S(1)}, bf16[576,128]{1,0:T(8,128)(2,1)S(1)}, u32[]{:S(2)}, u32[]{:S(2)}) collective-permute-start(bf16[576,128]{1,0:T(8,128)(2,1)S(1)} %pad_maximum_fusion.refs_0_), channel_id=1, source_target_pairs={{0,2},{1,3},{2,0},{3,1},{4,6},{5,7},{6,4},{7,5},{8,10},{9,11},{10,... | collective-permute-start | bytes 442376 | tf_op jit(solution)/shard_map/ppermute | solution.py:251
  20.3 10.4 %collective-permute-start.5 = (bf16[576,128]{1,0:T(8,128)(2,1)S(1)}, bf16[576,128]{1,0:T(8,128)(2,1)S(1)}, u32[]{:S(2)}, u32[]{:S(2)}) collective-permute-start(bf16[576,128]{1,0:T(8,128)(2,1)S(1)} %pad_maximum_fusion.1), channel_id=1, source_target_pairs={{0,35},{1,34},{2,33},{3,32},{32,3},{33,2},{34,1},{35,0},{4,39},{5,... | collective-permute-start | bytes 442376 | tf_op jit(solution)/shard_map/ppermute | solution.py:248
  24.1 12.0 %collective-permute-start.4 = (bf16[576,128]{1,0:T(8,128)(2,1)S(1)}, bf16[576,128]{1,0:T(8,128)(2,1)S(1)}, u32[]{:S(2)}, u32[]{:S(2)}) collective-permute-start(bf16[576,128]{1,0:T(8,128)(2,1)S(1)} %pad_maximum_fusion.1), channel_id=1, source_target_pairs={{0,33},{1,32},{2,35},{3,34},{32,1},{33,0},{34,3},{35,2},{4,37},{5,... | collective-permute-start | bytes 442376 | tf_op jit(solution)/shard_map/ppermute | solution.py:248
  25.1 14.0 %collective-permute-start.7 = (bf16[576,128]{1,0:T(8,128)(2,1)S(1)}, bf16[576,128]{1,0:T(8,128)(2,1)S(1)}, u32[]{:S(2)}, u32[]{:S(2)}) collective-permute-start(bf16[576,128]{1,0:T(8,128)(2,1)S(1)} %pad_maximum_fusion.refs_0_), channel_id=1, source_target_pairs={{0,1},{1,0},{2,3},{3,2},{4,5},{5,4},{6,7},{7,6},{8,9},{9,8},{10,11... | collective-permute-start | bytes 442376 | tf_op jit(solution)/shard_map/ppermute | solution.py:251
  27.2 20.9 %collective-permute-start.10 = (bf16[576,128]{1,0:T(8,128)(2,1)S(1)}, bf16[576,128]{1,0:T(8,128)(2,1)S(1)}, u32[]{:S(2)}, u32[]{:S(2)}) collective-permute-start(bf16[576,128]{1,0:T(8,128)(2,1)S(1)} %collective-permute-done.6.refs_3_), channel_id=1, source_target_pairs={{0,1},{1,0},{2,3},{3,2},{4,5},{5,4},{6,7},{7,6},{8,9},{9,8},{10,11... | collective-permute-start | bytes 442376 | tf_op jit(solution)/shard_map/ppermute | solution.py:254
  30.7 17.4 %collective-permute-start.9 = (bf16[576,128]{1,0:T(8,128)(2,1)S(1)}, bf16[576,128]{1,0:T(8,128)(2,1)S(1)}, u32[]{:S(2)}, u32[]{:S(2)}) collective-permute-start(bf16[576,128]{1,0:T(8,128)(2,1)S(1)} %collective-permute-done.5.refs_2_), channel_id=1, source_target_pairs={{0,1},{1,0},{2,3},{3,2},{4,5},{5,4},{6,7},{7,6},{8,9},{9,8},{10,11... | collective-permute-start | bytes 442376 | tf_op jit(solution)/shard_map/ppermute | solution.py:254
  36.2 12.0 %collective-permute-start.8 = (bf16[576,128]{1,0:T(8,128)(2,1)S(1)}, bf16[576,128]{1,0:T(8,128)(2,1)S(1)}, u32[]{:S(2)}, u32[]{:S(2)}) collective-permute-start(bf16[576,128]{1,0:T(8,128)(2,1)S(1)} %collective-permute-done.4.refs_1_), channel_id=1, source_target_pairs={{0,1},{1,0},{2,3},{3,2},{4,5},{5,4},{6,7},{7,6},{8,9},{9,8},{10,11... | collective-permute-start | bytes 442376 | tf_op jit(solution)/shard_map/ppermute | solution.py:254
  40.7 23.7 %all-to-all-start.1 = ((bf16[32,4,1152]{2,1,0:T(4,128)(2,1)}), bf16[32,4,1152]{2,1,0:T(4,128)(2,1)S(1)}, u32[]{:S(2)}, u32[]{:S(2)}) async-start(bf16[32,4,1152]{2,1,0:T(4,128)(2,1)} %add.2), calls=%async_computation.1 | async-start | bytes 589824 | tf_op jit(solution)/shard_map/all_to_all | solution.py:261
  49.3 4.4 %collective-permute-start.11 = (bf16[1024,128]{1,0:T(8,128)(2,1)S(1)}, bf16[1024,128]{1,0:T(8,128)(2,1)S(1)}, u32[]{:S(2)}, u32[]{:S(2)}) collective-permute-start(bf16[1024,128]{1,0:T(8,128)(2,1)S(1)} %scatter.6), channel_id=1, source_target_pairs={{0,4},{4,0},{1,5},{5,1},{2,6},{6,2},{3,7},{7,3},{8,12},{12,8},{9,1... | collective-permute-start | bytes 786440 | tf_op jit(solution)/shard_map/ppermute | solution.py:280
  53.2 1.6 %collective-permute-start.12 = (bf16[1024,128]{1,0:T(8,128)(2,1)S(1)}, bf16[1024,128]{1,0:T(8,128)(2,1)S(1)}, u32[]{:S(2)}, u32[]{:S(2)}) collective-permute-start(bf16[1024,128]{1,0:T(8,128)(2,1)S(1)} %get-tuple-element.108), channel_id=1, source_target_pairs={{0,4},{4,0},{1,5},{5,1},{2,6},{6,2},{3,7},{7,3},{8,12},{12,8},{9,1... | collective-permute-start | bytes 786440 | tf_op jit(solution)/shard_map/ppermute | solution.py:280
  53.3 1.9 %collective-permute-start.13 = (bf16[1024,128]{1,0:T(8,128)(2,1)S(1)}, bf16[1024,128]{1,0:T(8,128)(2,1)S(1)}, u32[]{:S(2)}, u32[]{:S(2)}) collective-permute-start(bf16[1024,128]{1,0:T(8,128)(2,1)S(1)} %get-tuple-element.109), channel_id=1, source_target_pairs={{0,4},{4,0},{1,5},{5,1},{2,6},{6,2},{3,7},{7,3},{8,12},{12,8},{9,1... | collective-permute-start | bytes 786440 | tf_op jit(solution)/shard_map/ppermute | solution.py:280
  57.8 15.7 %copy-start.3 = (f32[1024,128]{1,0:T(8,128)S(1)}, f32[1024,128]{1,0:T(8,128)}, u32[]{:S(2)}) copy-start(f32[1024,128]{1,0:T(8,128)} %table_ref.1) | copy-start | bytes 1572868
  57.8 15.7 %copy-start.6 = (f32[1024]{0:T(1024)S(1)}, f32[1024]{0:T(1024)}, u32[]{:S(2)}) copy-start(f32[1024]{0:T(1024)} %param.15) | copy-start | bytes 12292
  57.8 5.9 %collective-permute-start.14 = (bf16[1024,128]{1,0:T(8,128)(2,1)S(1)}, bf16[1024,128]{1,0:T(8,128)(2,1)S(1)}, u32[]{:S(2)}, u32[]{:S(2)}) collective-permute-start(bf16[1024,128]{1,0:T(8,128)(2,1)S(1)} %scatter.10), channel_id=1, source_target_pairs={{0,4},{4,0},{1,5},{5,1},{2,6},{6,2},{3,7},{7,3},{8,12},{12,8},{9,1... | collective-permute-start | bytes 786440 | tf_op jit(solution)/shard_map/ppermute | solution.py:280
  58.1 9.3 %collective-permute-start.17 = (bf16[1024,128]{1,0:T(8,128)(2,1)S(1)}, bf16[1024,128]{1,0:T(8,128)(2,1)S(1)}, u32[]{:S(2)}, u32[]{:S(2)}) collective-permute-start(bf16[1024,128]{1,0:T(8,128)(2,1)S(1)} %scatter.8), channel_id=1, source_target_pairs={{0,16},{8,24},{16,0},{24,8},{1,17},{9,25},{17,1},{25,9},{2,18},{10... | collective-permute-start | bytes 786440 | tf_op jit(solution)/shard_map/ppermute | solution.py:298
  61.1 12.5 %collective-permute-start.15 = (bf16[1024,128]{1,0:T(8,128)(2,1)}, bf16[1024,128]{1,0:T(8,128)(2,1)S(1)}, u32[]{:S(2)}, u32[]{:S(2)}) collective-permute-start(bf16[1024,128]{1,0:T(8,128)(2,1)} %get-tuple-element.117), channel_id=1, source_target_pairs={{0,8},{8,16},{16,24},{24,0},{1,9},{9,17},{17,25},{25,1},{2,10},{10... | collective-permute-start | bytes 786440 | tf_op jit(solution)/shard_map/ppermute | solution.py:301
  61.3 12.2 %collective-permute-start.16 = (bf16[1024,128]{1,0:T(8,128)(2,1)S(1)}, bf16[1024,128]{1,0:T(8,128)(2,1)S(1)}, u32[]{:S(2)}, u32[]{:S(2)}) collective-permute-start(bf16[1024,128]{1,0:T(8,128)(2,1)S(1)} %get-tuple-element.118), channel_id=1, source_target_pairs={{0,24},{8,0},{16,8},{24,16},{1,25},{9,1},{17,9},{25,17},{2,26},{10... | collective-permute-start | bytes 786440 | tf_op jit(solution)/shard_map/ppermute | solution.py:302
